TPU v7x, 128 devices: a whole 4x4x4 slice. The times are simulated.
128 devices in a mesh: wide: 32 (over x, y_lo, z), narrow: 4 (over y_hi, core).
Axes of the slice: x: 4, y: 4 (y_hi: 2, y_lo: 2; y = y_hi * 2 + y_lo), z: 4, core: 2. Of those that a mesh axis runs over, the one named last changes fastest.
Arguments:
- sources: float32 [1, 2, 4096, 4096], P(None, None, 'wide', 'narrow'), may hold values from -4 to 4
- incident: float32 [1, 2, 4096, 4096], P(None, None, 'wide', 'narrow'), may hold values from -6 to 6
- contrast: float32 [2, 4096, 4096], P(None, 'wide', 'narrow'), may hold values from -5 to 5
- green: float32 [2, 8192, 8192], P(None, 'narrow', 'wide'), may hold values from -6 to 6
- angles: float32 [1024], replicated, may hold values from -3.140625 to 3.140625
- measured: float32 [1, 2, 1024], replicated, may hold values from -6 to 6
Outputs:
- residual: float32 [1, 2, 4096, 4096], P(None, None, 'wide', 'narrow')
- backprojection: float32 [1, 2, 4096, 4096], P(None, None, 'wide', 'narrow')
- data_residual: float32 [1, 2, 1024], replicated
All inputs are finite; a program needn't handle non-finite values.
Results may differ from a plain program's by a relative error of at most 0.0003.
Values sent between devices are 32-bit elements; how exact they have to be, the bound alone decides.
No kernel may reach another device: no remote copies, remote signals or barrier semaphores. Data moves between devices by JAX's collectives and lax.ppermute only.
A program may use at most 128 MiB of HBM per device.

v0:
```python
import math

import jax
import jax.numpy as jnp
from jax import lax
from jax.sharding import PartitionSpec as P

N = 4096
R = 1024
M = 8192


wave_step = 0.2 * math.pi
highest = lax.Precision.HIGHEST


def turn_table(count_in, count_out, length, direction):
    product = (
        jnp.arange(count_in, dtype=jnp.int32)[:, None]
        * jnp.arange(count_out, dtype=jnp.int32)[None, :]
        % length
    )
    phase_angle = product.astype(jnp.float32) * (direction * 2.0 * math.pi / length)
    cosine_part = jnp.cos(phase_angle)
    sine_part = jnp.sin(phase_angle)
    return jnp.stack(
        [jnp.stack([cosine_part, sine_part], 1), jnp.stack([-sine_part, cosine_part], 1)], 0
    )


def twiddle(values, length, direction):
    outer_count = values.shape[-2]
    inner_count = values.shape[-1]
    product = (
        jnp.arange(outer_count, dtype=jnp.int32)[:, None]
        * jnp.arange(inner_count, dtype=jnp.int32)[None, :]
        % length
    )
    phase_angle = product.astype(jnp.float32) * (direction * 2.0 * math.pi / length)
    cosine_part = jnp.cos(phase_angle)
    sine_part = jnp.sin(phase_angle)
    real_in = values[:, 0]
    imag_in = values[:, 1]
    return jnp.stack(
        [real_in * cosine_part - imag_in * sine_part, real_in * sine_part + imag_in * cosine_part],
        1,
    )


def forward_lines(values):
    batches, planes, line_count, inputs = values.shape
    length = 2 * inputs
    factor = length // 128
    blocks = values.reshape(batches, planes, line_count, factor // 2, 128)
    section_one = jnp.einsum(
        "balpq,apck->bclkq",
        blocks,
        turn_table(factor // 2, factor, factor, -1.0),
        precision=highest,
    )
    section_one = twiddle(section_one, length, -1.0)
    section_two = jnp.einsum(
        "balkq,aqcm->bclmk", section_one, turn_table(128, 128, 128, -1.0), precision=highest
    )
    return section_two.reshape(batches, planes, line_count, length)


def inverse_lines(values):
    batches, planes, line_count, length = values.shape
    factor = length // 128
    blocks = values.reshape(batches, planes, line_count, 128, factor)
    section_one = jnp.einsum(
        "balmk,amcq->bclkq", blocks, turn_table(128, 128, 128, 1.0), precision=highest
    )
    section_one = twiddle(section_one, length, 1.0)
    section_two = jnp.einsum(
        "balkq,akcp->bclpq",
        section_one,
        turn_table(factor, factor // 2, factor, 1.0),
        precision=highest,
    )
    return section_two.reshape(batches, planes, line_count, length // 2)


def complex_times(kernel, values):
    return jnp.stack(
        [
            kernel[0] * values[:, 0] - kernel[1] * values[:, 1],
            kernel[0] * values[:, 1] + kernel[1] * values[:, 0],
        ],
        1,
    )


def phase_table(index, direction_part):
    position = index.astype(jnp.float32) - N // 2 + 0.5
    stepped = wave_step * position
    return stepped[:, None] * direction_part[None, :]


def local(sources, incident, contrast, green, angles, measured):
    spread = lax.all_to_all(sources, "narrow", split_axis=2, concat_axis=3, tiled=True)
    spread = forward_lines(spread)
    spread = lax.all_to_all(spread, "narrow", split_axis=3, concat_axis=2, tiled=True)
    spread = jnp.swapaxes(spread, 2, 3)
    spread = lax.all_to_all(spread, "wide", split_axis=2, concat_axis=3, tiled=True)
    spread = forward_lines(spread)
    blocks = lax.all_to_all(spread, "wide", split_axis=3, concat_axis=2, tiled=True)
    blocks = complex_times(green, blocks)
    mixed = lax.all_to_all(blocks, "wide", split_axis=2, concat_axis=3, tiled=True)
    mixed = inverse_lines(mixed)
    mixed = lax.all_to_all(mixed, "wide", split_axis=3, concat_axis=2, tiled=True)
    mixed = jnp.swapaxes(mixed, 2, 3)
    mixed = lax.all_to_all(mixed, "narrow", split_axis=2, concat_axis=3, tiled=True)
    mixed = inverse_lines(mixed)
    scattered = lax.all_to_all(mixed, "narrow", split_axis=3, concat_axis=2, tiled=True) * (
        1.0 / (M * M)
    )
    field = incident + scattered
    residual = complex_times(contrast, field) - sources
    local_rows = sources.shape[2]
    local_cols = sources.shape[3]
    row_index = lax.axis_index("wide") * local_rows + jnp.arange(local_rows, dtype=jnp.int32)
    col_index = lax.axis_index("narrow") * local_cols + jnp.arange(local_cols, dtype=jnp.int32)
    row_phase = phase_table(row_index, jnp.cos(angles))
    col_phase = phase_table(col_index, jnp.sin(angles))
    row_cos = jnp.cos(row_phase)
    row_sin = -jnp.sin(row_phase)
    col_cos = jnp.cos(col_phase)
    col_sin = -jnp.sin(col_phase)
    by_real = jnp.einsum("taxy,yr->taxr", sources, col_cos, precision=highest)
    by_imag = jnp.einsum("taxy,yr->taxr", sources, col_sin, precision=highest)
    inner_real = by_real[:, 0] - by_imag[:, 1]
    inner_imag = by_imag[:, 0] + by_real[:, 1]
    part_real = jnp.sum(row_cos * inner_real - row_sin * inner_imag, axis=1)
    part_imag = jnp.sum(row_cos * inner_imag + row_sin * inner_real, axis=1)
    partial_value = jnp.stack([part_real, part_imag], 1)
    total = lax.psum(partial_value, ("wide", "narrow"))
    data_residual = measured - total * (1.0 / N)
    rho_real = data_residual[:, 0][:, None, :]
    rho_imag = data_residual[:, 1][:, None, :]
    weight_real = row_cos * rho_real + row_sin * rho_imag
    weight_imag = row_cos * rho_imag - row_sin * rho_real
    weights = jnp.stack([weight_real, weight_imag], 1)
    back_real = jnp.einsum("taxr,yr->taxy", weights, col_cos, precision=highest)
    back_imag = jnp.einsum("taxr,yr->taxy", weights, col_sin, precision=highest)
    scale = 1.0 / math.sqrt(R)
    backprojection = (
        jnp.stack([back_real[:, 0] + back_imag[:, 1], back_real[:, 1] - back_imag[:, 0]], 1) * scale
    )
    return (residual, backprojection, data_residual)


def solution(mesh):
    placed = (
        P(None, None, "wide", "narrow"),
        P(None, None, "wide", "narrow"),
        P(None, "wide", "narrow"),
        P(None, "narrow", "wide"),
        P(),
        P(),
    )
    return jax.shard_map(
        local,
        mesh=mesh,
        in_specs=placed,
        out_specs=(P(None, None, "wide", "narrow"), P(None, None, "wide", "narrow"), P()),
        check_vma=False,
    )
```

profile of v0, /device:TPU:0, one launch (start us, length us, event | category | flops | bytes accessed | tf_op | source)
XLA Modules:
  0.0 649.4 jit_solution(8153018307551116221)
XLA Ops:
  9.1 15.1 %all-to-all-done = f32[1,2,128,1024]{3,1,0,2:T(2,128)S(1)} async-done(((f32[1,2,128,1024]{3,1,0,2:T(2,128)}), f32[1,2,128,1024]{3,1,0,2:T(2,128)S(1)}, u32[]{:S(2)}, u32[]{:S(2)}) %all-to-all-start) | async-done | bytes 1048608 | tf_op jit(solution)/shard_map/all_to_all | solution.py:102
  35.8 9.8 %reshape.990 = f32[4,1,131072]{2,1,0:T(1,128)S(1)} reshape(f32[8192,1,2,32]{3,2,1,0:T(2,128)} %bitcast.282) | data formatting | bytes 4194304
  45.6 30.4 %all_to_all.123 = f32[4,1,131072]{2,1,0:T(1,128)} all-to-all(f32[4,1,131072]{2,1,0:T(1,128)S(1)} %reshape.990), channel_id=1, replica_groups=mesh['wide'=32,'narrow'=4] {'narrow'}, dimensions={0} | all-to-all | bytes 4194304 | tf_op jit(solution)/shard_map/all_to_all | solution.py:104
  76.6 7.6 %reduce.2 = f32[4,131072]{1,0:T(4,128)S(1)} reduce(f32[4,1,131072]{2,1,0:T(1,128)} %all_to_all.123, f32[]{:T(128)} %broadcast.951), dimensions={1}, to_apply=%all_to_all.93.reduce_sub_computation | reduce | bytes 4194308 | tf_op jit(solution)/shard_map/all_to_all | solution.py:104
  84.2 10.9 %reshape.991 = f32[8192,1,2,32]{3,2,1,0:T(2,128)} reshape(f32[4,131072]{1,0:T(4,128)S(1)} %reduce.2) | data formatting | bytes 4194304
  95.2 10.5 %copy.185 = f32[1,2,32,4,2048]{4,3,2,1,0:T(4,128)S(1)} copy(f32[1,2,32,4,2048]{2,1,4,3,0:T(2,128)} %bitcast.283) | data formatting | bytes 4194304 | tf_op jit(solution)/shard_map/all_to_all | solution.py:104
  111.0 35.6 %all_to_all.124 = f32[1,2,2048,128]{3,1,0,2:T(2,128)S(1)} all-to-all(f32[1,2,2048,128]{3,1,0,2:T(2,128)S(1)} %copy.141), channel_id=1, replica_groups=mesh['wide'=32,'narrow'=4] {'wide'}, dimensions={2} | all-to-all | bytes 4194304 | tf_op jit(solution)/shard_map/all_to_all | solution.py:106
  157.2 8.8 %copy.188 = f32[1,2,64,128,64]{2,1,4,3,0:T(2,128)} copy(f32[1,2,64,128,64]{3,4,2,1,0:T(8,128)} %fusion.21) | data formatting | bytes 8388608 | tf_op jit(solution)/shard_map/reshape | solution.py:65
  166.0 12.0 %reshape.992 = f32[32,1,32768]{2,1,0:T(1,128)} reshape(f32[8192,1,2,64]{3,2,1,0:T(2,128)} %bitcast.284) | data formatting | bytes 8388608
  178.0 55.3 %all_to_all.125 = f32[32,1,32768]{2,1,0:T(1,128)} all-to-all(f32[32,1,32768]{2,1,0:T(1,128)} %reshape.992), channel_id=1, replica_groups=mesh['wide'=32,'narrow'=4] {'wide'}, dimensions={0} | all-to-all | bytes 8388608 | tf_op jit(solution)/shard_map/all_to_all | solution.py:108
  233.3 13.7 %reduce.3 = f32[32,32768]{1,0:T(8,128)} reduce(f32[32,1,32768]{2,1,0:T(1,128)} %all_to_all.125, f32[]{:T(128)} %broadcast.951), dimensions={1}, to_apply=%all_to_all.100.reduce_sub_computation | reduce | bytes 8388612 | tf_op jit(solution)/shard_map/all_to_all | solution.py:108
  246.9 9.2 %reshape.993 = f32[8192,1,2,64]{3,2,1,0:T(2,128)} reshape(f32[32,32768]{1,0:T(8,128)} %reduce.3) | data formatting | bytes 8388608
  256.1 11.4 %copy.190 = f32[1,2,64,32,256]{4,2,3,1,0:T(8,128)} copy(f32[1,2,64,32,256]{2,1,4,3,0:T(2,128)} %bitcast.285) | data formatting | bytes 8388608 | tf_op jit(solution)/shard_map/all_to_all | solution.py:108
  271.9 12.3 %copy.149 = f32[1,2,2048,256]{3,1,0,2:T(2,128)} copy(f32[1,2,2048,256]{3,2,1,0:T(8,128)S(1)} %pad_maximum_fusion) | data formatting | bytes 8388608 | tf_op jit(solution)/shard_map/stack | solution.py:86
  290.2 54.1 %all-to-all-done.4 = f32[1,2,2048,256]{3,1,0,2:T(2,128)} async-done(((f32[1,2,2048,256]{3,1,0,2:T(2,128)}), f32[1,2,2048,256]{3,1,0,2:T(2,128)}, u32[]{:S(2)}, u32[]{:S(2)}) %all-to-all-start.4) | async-done | bytes 4194336 | tf_op jit(solution)/shard_map/all_to_all | solution.py:110
  357.9 16.3 %fusion.24 = f32[1,2,64,64,128]{4,3,2,1,0:T(8,128)S(1)} fusion(f32[2,64,128,64]{3,2,1,0:T(8,128)} %reshape.958, f32[1,128,2,128]{3,1,2,0:T(8,128)S(1)} %get-tuple-element.20, f32[1,128,2,128]{3,1,2,0:T(8,128)S(1)} %get-tuple-element.19), kind=kOutput, calls=%fused_computation.25 | convolution fusion | flops 3221291008 | bytes 8650752 | tf_op jit(solution)/shard_map/balmk,amcq->bclkq/dot_general | solution.py:72
  393.6 28.2 %all-to-all-done.5 = f32[32,1,16384]{2,1,0:T(1,128)} async-done(((f32[32,1,16384]{2,1,0:T(1,128)}), f32[32,1,16384]{2,1,0:T(1,128)}, u32[]{:S(2)}, u32[]{:S(2)}) %all-to-all-start.5) | async-done | bytes 2097184 | tf_op jit(solution)/shard_map/all_to_all | solution.py:112
  433.5 7.4 %copy.155 = f32[1,2,64,4096]{3,0,2,1:T(1,128)S(1)} copy(f32[1,2,64,4096]{2,1,0,3:T(2,128)} %bitcast.290) | data formatting | bytes 4194304 | tf_op jit(solution)/shard_map/all_to_all | solution.py:112
  451.6 17.5 %fusion.61 = f32[1,2,128,1024]{3,2,1,0:T(8,128)S(1)} fusion(f32[1024]{0:T(1024)S(1)} %get-tuple-element.32, f32[1024]{0:T(1024)S(1)} %get-tuple-element.45, f32[1,2,128,1024]{3,2,1,0:T(8,128)S(1)} %copy-done), kind=kOutput, calls=%fused_computation.60 | convolution fusion | flops 3222274048 | bytes 2105344 | tf_op jit(solution)/shard_map/taxy,yr->taxr/dot_general | solution.py:131
  469.2 18.1 %fusion.55 = f32[1,2,128,1024]{3,2,1,0:T(8,128)S(1)} fusion(f32[1024]{0:T(1024)S(1)} %get-tuple-element.32, f32[1024]{0:T(1024)S(1)} %get-tuple-element.45, f32[1,2,128,1024]{3,2,1,0:T(8,128)S(1)} %copy-done), kind=kOutput, calls=%fused_computation.58 | convolution fusion | flops 3223322624 | bytes 2105344 | tf_op jit(solution)/shard_map/taxy,yr->taxr/dot_general | solution.py:132
  489.8 65.5 %psum.7 = f32[1,2,1024]{2,1,0:T(2,128)} all-reduce(f32[1,2,1024]{2,1,0:T(2,128)S(1)} %pad_maximum_fusion.1), channel_id=1, replica_groups=mesh['wide'=32,'narrow'=4] {'wide','narrow'}, use_global_device_ids=true, to_apply=%region_2.3 | all-reduce | flops 2048 | bytes 16384 | tf_op jit(solution)/shard_map/psum | solution.py:138
  565.8 9.0 %fusion.49 = f32[1,2,32,64,128]{4,3,2,1,0:T(8,128)S(1)} fusion(f32[2,32,128,64]{3,2,1,0:T(8,128)} %reshape.961, f32[1,128,2,128]{3,1,2,0:T(8,128)S(1)} %get-tuple-element.20, f32[1,128,2,128]{3,1,2,0:T(8,128)S(1)} %get-tuple-element.19), kind=kOutput, calls=%fused_computation.56 | convolution fusion | flops 1610678272 | bytes 4456448 | tf_op jit(solution)/shard_map/balmk,amcq->bclkq/dot_general | solution.py:72
  590.3 17.2 %fusion.64 = f32[1,2,128,1024]{3,2,1,0:T(8,128)S(1)} fusion(f32[1024]{0:T(1024)S(1)} %get-tuple-element.32, f32[1024]{0:T(1024)S(1)} %copy-done.8, f32[1,1,128,1024]{3,2,1,0:T(8,128)S(1)} %copy-done.4, f32[1,1,128,1024]{3,2,1,0:T(8,128)S(1)} %copy-done.3), kind=kOutput, calls=%fused_computation.61 | convolution fusion | flops 3222536192 | bytes 2105344 | tf_op jit(solution)/shard_map/taxr,yr->taxy/dot_general | solution.py:145
  607.5 17.4 %fusion.58 = f32[1,2,128,1024]{3,2,1,0:T(8,128)S(1)} fusion(f32[1024]{0:T(1024)S(1)} %get-tuple-element.32, f32[1024]{0:T(1024)S(1)} %copy-done.8, f32[1,1,128,1024]{3,2,1,0:T(8,128)S(1)} %copy-done.4, f32[1,1,128,1024]{3,2,1,0:T(8,128)S(1)} %copy-done.3), kind=kOutput, calls=%fused_computation.59 | convolution fusion | flops 3223584768 | bytes 2105344 | tf_op jit(solution)/shard_map/taxr,yr->taxy/dot_general | solution.py:146
  (89 shorter events, 154.7 us)
Async XLA Ops:
  3.6 20.5 %all-to-all-start = ((f32[1,2,128,1024]{3,1,0,2:T(2,128)}), f32[1,2,128,1024]{3,1,0,2:T(2,128)S(1)}, u32[]{:S(2)}, u32[]{:S(2)}) async-start(f32[1,2,128,1024]{3,1,0,2:T(2,128)} %copy.134), calls=%async_computation | async-start | bytes 2097152 | tf_op jit(solution)/shard_map/all_to_all | solution.py:102
  284.1 60.1 %all-to-all-start.4 = ((f32[1,2,2048,256]{3,1,0,2:T(2,128)}), f32[1,2,2048,256]{3,1,0,2:T(2,128)}, u32[]{:S(2)}, u32[]{:S(2)}) async-start(f32[1,2,2048,256]{3,1,0,2:T(2,128)} %copy.149), calls=%async_computation.4 | async-start | bytes 8388608 | tf_op jit(solution)/shard_map/all_to_all | solution.py:110
  386.9 6.7 %copy-start.6 = (f32[1024]{0:T(1024)S(1)}, f32[1024]{0:T(1024)}, u32[]{:S(2)}) copy-start(f32[1024]{0:T(1024)} %param.10) | copy-start | bytes 12292
  386.9 34.9 %all-to-all-start.5 = ((f32[32,1,16384]{2,1,0:T(1,128)}), f32[32,1,16384]{2,1,0:T(1,128)}, u32[]{:S(2)}, u32[]{:S(2)}) async-start(f32[32,1,16384]{2,1,0:T(1,128)} %reshape.994), calls=%async_computation.5 | async-start | bytes 4194304 | tf_op jit(solution)/shard_map/all_to_all | solution.py:112
  393.6 75.5 %copy-start.7 = (f32[1024]{0:T(1024)}, f32[1024]{0:T(1024)S(1)}, u32[]{:S(2)}) copy-start(f32[1024]{0:T(1024)S(1)} %get-tuple-element.45) | copy-start | bytes 12292
  447.7 3.9 copy-start
  447.7 112.2 %all-to-all-start.6 = ((f32[1,2,128,2048]{3,1,0,2:T(2,128)}), f32[1,2,128,2048]{3,1,0,2:T(2,128)S(1)}, u32[]{:S(2)}, u32[]{:S(2)}) async-start(f32[1,2,128,2048]{3,1,0,2:T(2,128)} %copy.157), calls=%async_computation.6 | async-start | bytes 4194304 | tf_op jit(solution)/shard_map/all_to_all | solution.py:114
  451.6 35.7 %copy-start.9 = (f32[128]{0:T(128)}, f32[128]{0:T(128)S(1)}, u32[]{:S(2)}) copy-start(f32[128]{0:T(128)S(1)} %add_multiply_fusion.1) | copy-start | bytes 1540
  556.0 5.1 copy-start.5
  585.9 4.3 copy-start.3
  585.9 4.3 copy-start.4
  586.0 4.3 copy-start.8
  586.0 40.1 %all-to-all-start.7 = ((f32[4,1,65536]{2,1,0:T(1,128)}), f32[4,1,65536]{2,1,0:T(1,128)S(1)}, u32[]{:S(2)}, u32[]{:S(2)}) async-start(f32[4,1,65536]{2,1,0:T(1,128)} %reshape.996), calls=%async_computation.7 | async-start | bytes 2097152 | tf_op jit(solution)/shard_map/all_to_all | solution.py:116
  641.1 5.3 copy-start.1
  646.4 1.2 copy-start.2
where the time goes:
time: 660 us; the launch traced here: 649 us
  blocking collectives  187 us (28%)
  local copies, waits for them, and re-layouts  171 us (26%)
  matrix products  112 us (17%)
  waiting for transfers between devices  97.3 us (15%)
  other arithmetic  56.1 us (8%)
  starting transfers between devices  24.6 us (4%)
    unnamed x29, local copies, waits for them, and re-layouts  69.1 us
    psum x1, blocking collectives, local(): total = lax.psum(partial_value, ('wide', 'narrow'))  65.5 us
    all_to_all x1, blocking collectives, local(): lax.all_to_all(spread, 'wide', split_axis=3, concat_axis=2, tiled=True)  55.3 us
    all_to_all x1, waiting for transfers between devices, local(): lax.all_to_all(blocks, 'wide', split_axis=2, concat_axis=3, tiled=True)  54.1 us
    all_to_all x1, blocking collectives, local(): lax.all_to_all(spread, 'wide', split_axis=2, concat_axis=3, tiled=True)  35.6 us
    all_to_all x1, blocking collectives, local(): lax.all_to_all(spread, 'narrow', split_axis=3, concat_axis=2, tiled=True)  30.4 us
    all_to_all x1, waiting for transfers between devices, local(): lax.all_to_all(mixed, 'wide', split_axis=3, concat_axis=2, tiled=True)  28.2 us
    dot_general x2, matrix products, inverse_lines(): jnp.einsum('balmk,amcq->bclkq', blocks, turn_table(128, 128, 128, 1.0), p...  25.2 us
  transfers between devices with their start and end apart: 5, of which 3 were waited for; matrix products, arithmetic and copies ran while one was open for 12% of the time, Pallas kernels for 0%

commit v1 on v0

v1 whole, which is shorter than its diff:
```python
import functools
import math

import jax
import jax.numpy as jnp
import ml_dtypes
import numpy as np
from jax import lax
from jax.experimental import pallas as pl
from jax.experimental.pallas import tpu as pltpu
from jax.sharding import PartitionSpec as P

N = 4096
R = 1024
M = 8192
WIDE = 32
NARROW = 4

wave_step = 0.2 * math.pi
f32 = jnp.float32
bf16 = jnp.bfloat16
VMEM_LIMIT = 56 * 1024 * 1024


def complex_block(table):
    return np.block([[table.real, -table.imag], [table.imag, table.real]])


def halves(table):
    high = table.astype(np.float32).astype(ml_dtypes.bfloat16)
    low = (table - high.astype(np.float64)).astype(np.float32).astype(ml_dtypes.bfloat16)
    return high, low


def root(product, length, sign):
    return np.exp(sign * 2j * np.pi * (product % length) / length)


def pair(table):
    return np.stack([table.real, table.imag]).astype(np.float32)


@functools.lru_cache(None)
def tables():
    out = {}
    w = np.arange(32)
    k1 = np.arange(64)
    i = np.arange(128)
    m = np.arange(128)
    high, low = halves(complex_block(root(np.outer(k1, w), 64, -1)))
    out["t1"] = np.concatenate([high, high, low], 1)
    out["tw1"] = pair(root(np.outer(k1, i), M, -1))
    out["t2"] = np.stack(halves(complex_block(root(np.outer(m, i), 128, -1))))
    d = np.arange(128)
    s = 32 * (d % 4) + d // 4
    c1 = np.arange(256)
    out["t3"] = np.stack(halves(complex_block(root(np.outer(c1, s), 256, -1))))
    low_half = np.arange(128) < 64
    first = np.where(low_half[None, :], 1.0, root(c1, M, -1)[:, None])
    out["tw3"] = pair(first)
    out["step3"] = pair(root(2 * c1, M, -1)[:, None] * np.ones((1, 128)))
    lanes = []
    for flip in (0, 1):
        e = (np.arange(16) + 8 * flip) % 16
        lanes.append(pair(np.where(low_half[None, :], 1.0, root(e, 32, -1)[:, None])))
    out["lane3"] = np.stack(lanes)
    out["t4"] = np.stack(halves(complex_block(root(np.outer(s, c1), 256, 1))))
    out["t5"] = np.stack(halves(complex_block(root(np.outer(i, m), 128, 1))))
    lane_k1 = np.arange(128) % 64
    out["tw5"] = pair(root(np.outer(i, lane_k1), M, 1))
    inner = root(np.outer(w, k1), 64, 1) / (M * M)
    block = np.zeros((2, 2, 32, 2, 2, 64))
    for b0 in (0, 1):
        block[b0, 0, :, 0, b0, :] = inner.real
        block[b0, 0, :, 1, b0, :] = -inner.imag
        block[b0, 1, :, 0, b0, :] = inner.imag
        block[b0, 1, :, 1, b0, :] = inner.real
    out["t6"] = np.stack(halves(block.reshape(128, 256)))
    return out


def split(values):
    high = values.astype(bf16)
    low = (values - high.astype(f32)).astype(bf16)
    return high, low


def dot(a, b):
    return lax.dot_general(a, b, (((1,), (0,)), ((), ())), preferred_element_type=f32)


def dot_nt(a, b):
    return lax.dot_general(a, b, (((1,), (1,)), ((), ())), preferred_element_type=f32)


def dot3(table_high, table_low, values, product):
    high, low = split(values)
    return product(table_high, high) + (product(table_high, low) + product(table_low, high))


def times_root(value, numerator, length):
    re, im = value
    numerator %= length
    if numerator == 0:
        return value
    if 4 * numerator == length:
        return im, -re
    if 2 * numerator == length:
        return -re, -im
    if 4 * numerator == 3 * length:
        return -im, re
    if 8 * numerator == length:
        half = math.sqrt(0.5)
        return (re + im) * half, (im - re) * half
    if 8 * numerator == 3 * length:
        half = math.sqrt(0.5)
        return (im - re) * half, (-re - im) * half
    cosine = math.cos(2 * math.pi * numerator / length)
    sine = -math.sin(2 * math.pi * numerator / length)
    return re * cosine - im * sine, re * sine + im * cosine


def transform_list(values):
    count = len(values)
    if count == 1:
        return values
    if count == 2:
        (ar, ai), (br, bi) = values
        return [(ar + br, ai + bi), (ar - br, ai - bi)]
    if count == 4:
        (ar, ai), (br, bi), (cr, ci), (dr, di) = values
        pr, pi_, qr, qi = ar + cr, ai + ci, ar - cr, ai - ci
        sr, si, tr, ti = br + dr, bi + di, br - dr, bi - di
        return [(pr + sr, pi_ + si), (qr + ti, qi - tr), (pr - sr, pi_ - si), (qr - ti, qi + tr)]
    parts = [transform_list(values[start::4]) for start in range(4)]
    quarter = count // 4
    out = [None] * count
    for k in range(quarter):
        column = [times_root(parts[j][k], j * k, count) for j in range(4)]
        for q, value in enumerate(transform_list(column)):
            out[k + q * quarter] = value
    return out


def inverse_list(values):
    swapped = transform_list([(im, re) for re, im in values])
    return [(re, im) for im, re in swapped]


def spec_vmem():
    return pl.BlockSpec(memory_space=pltpu.VMEM)


def params():
    return pltpu.CompilerParams(vmem_limit_bytes=VMEM_LIMIT)


def cost(flops, bytes_accessed):
    return pl.CostEstimate(flops=flops, bytes_accessed=bytes_accessed, transcendentals=0)


def columns_kernel(source_ref, out_ref):
    for part in range(2):
        turned = source_ref[part].T
        for block in range(4):
            out_ref[pl.ds(block * 64 + part * 32, 32), :] = turned[block * 32 : block * 32 + 32]


def columns_major(source):
    return pl.pallas_call(
        columns_kernel,
        grid=(8,),
        in_specs=[pl.BlockSpec((2, 128, 128), lambda t: (0, 0, t))],
        out_specs=pl.BlockSpec((256, 128), lambda t: (t, 0)),
        out_shape=jax.ShapeDtypeStruct((2048, 128), f32),
        cost_estimate=cost(0, 2 << 20),
        name="columns_major",
    )(source)


def x_forward_kernel(a_ref, t1_ref, tw_ref, t2_ref, out_ref):
    @pl.loop(0, 16)
    def _(c):
        columns = []
        for b0 in range(2):
            re = a_ref[pl.ds(2 * c + b0, 32, stride=64), :]
            im = a_ref[pl.ds(2 * c + b0 + 32, 32, stride=64), :]
            columns.append(jnp.concatenate([re, im], 0))
        high, low = split(jnp.concatenate(columns, 1))
        u = dot(t1_ref[...], jnp.concatenate([high, low, high], 0))
        rows = []
        for b0 in range(2):
            ur = u[:64, 128 * b0 : 128 * b0 + 128]
            ui = u[64:, 128 * b0 : 128 * b0 + 128]
            rows.append(
                jnp.concatenate(
                    [ur * tw_ref[0] - ui * tw_ref[1], ur * tw_ref[1] + ui * tw_ref[0]], 1
                )
            )
        z = jnp.concatenate(rows, 0)
        out = dot3(t2_ref[0], t2_ref[1], z, dot_nt)
        out_ref[pl.ds(c, 128, stride=32), :] = out[:128]
        out_ref[pl.ds(c + 16, 128, stride=32), :] = out[128:]


def x_forward(a):
    t = tables()
    return pl.pallas_call(
        x_forward_kernel,
        in_specs=[spec_vmem()] * 4,
        out_specs=spec_vmem(),
        out_shape=jax.ShapeDtypeStruct((4096, 128), f32),
        compiler_params=params(),
        cost_estimate=cost(2 * 2048 * 65536 * 4, 4 << 20),
        name="x_forward",
    )(a, jnp.asarray(t["t1"]), jnp.asarray(t["tw1"]), jnp.asarray(t["t2"]))


def middle_kernel(
    place_ref, a_ref, r0_ref, r1_ref, r2_ref, r3_ref, t3_ref, tw_ref, step_ref, lane_ref, t4_ref,
    out_ref, u_ref, now_ref,
):
    flip = place_ref[0]
    upper = place_ref[1]
    sign = 1.0 - 2.0 * flip.astype(f32)

    def advance():
        sr = step_ref[0] * sign
        si = step_ref[1] * sign
        nr = now_ref[0]
        ni = now_ref[1]
        now_ref[0] = nr * sr - ni * si
        now_ref[1] = nr * si + ni * sr

    now_ref[...] = tw_ref[...]

    @pl.loop(0, 8)
    def _(cc):
        columns = []
        for half in range(2):
            re = a_ref[pl.ds(2 * cc + half, 128, stride=32), :]
            im = a_ref[pl.ds(2 * cc + half + 16, 128, stride=32), :]
            columns.append(jnp.concatenate([re, im], 0))
        u = dot3(t3_ref[0], t3_ref[1], jnp.concatenate(columns, 1), dot)
        for half in range(2):
            ur = u[:256, 128 * half : 128 * half + 128]
            ui = u[256:, 128 * half : 128 * half + 128]
            nr = now_ref[0]
            ni = now_ref[1]
            u_ref[2 * cc + half, 0] = ur * nr - ui * ni
            u_ref[2 * cc + half, 1] = ur * ni + ui * nr
            advance()

    lane = lax.broadcasted_iota(jnp.int32, (8, 128), 1)
    low = lane < 64
    sgn = jnp.where(low, 1.0, -1.0).astype(f32)
    mine = low == (upper == 0)

    @pl.loop(0, 32)
    def _(tile):
        rows = pl.ds(pl.multiple_of(tile * 8, 8), 8)
        values = [(u_ref[c, 0, rows, :], u_ref[c, 1, rows, :]) for c in range(16)]
        spectrum = transform_list(values)
        back = []
        for e in range(16):
            g, q, row_block = e // 8, (e // 4) % 2, e % 4
            own_ref, other_ref = ((r0_ref, r2_ref), (r1_ref, r3_ref))[g]
            grows = pl.ds(pl.multiple_of(tile * 8 + row_block * 256, 8), 8)
            green = []
            for part in range(2):
                own = own_ref[part, grows, :]
                other = other_ref[part, grows, :]
                green.append(jnp.where(mine, own, other) if q == 0 else jnp.where(mine, other, own))
            lr = lane_ref[0, e]
            li = lane_ref[1, e]
            sr, si = spectrum[e]
            vr = sr * lr - si * li
            vi = sr * li + si * lr
            rr = pltpu.roll(vr, 64, 1)
            ri = pltpu.roll(vi, 64, 1)
            if q == 0:
                fr, fi = sgn * vr + rr, sgn * vi + ri
            else:
                fr, fi = vr - sgn * rr, vi - sgn * ri
            pr = green[0] * fr - green[1] * fi
            pi_ = green[0] * fi + green[1] * fr
            rr = pltpu.roll(pr, 64, 1)
            ri = pltpu.roll(pi_, 64, 1)
            if q == 0:
                vr, vi = sgn * pr + rr, sgn * pi_ + ri
            else:
                vr, vi = pr + sgn * rr, pi_ + sgn * ri
            back.append((vr * lr + vi * li, vi * lr - vr * li))
        for c, (re, im) in enumerate(inverse_list(back)):
            u_ref[c, 0, rows, :] = re
            u_ref[c, 1, rows, :] = im

    now_ref[...] = tw_ref[...]

    @pl.loop(0, 8)
    def _(cc):
        columns = []
        for half in range(2):
            ur = u_ref[2 * cc + half, 0]
            ui = u_ref[2 * cc + half, 1]
            nr = now_ref[0]
            ni = now_ref[1]
            columns.append(jnp.concatenate([ur * nr + ui * ni, ui * nr - ur * ni], 0))
            advance()
        out = dot3(t4_ref[0], t4_ref[1], jnp.concatenate(columns, 1), dot)
        for half in range(2):
            lanes = slice(128 * half, 128 * half + 128)
            out_ref[pl.ds(2 * cc + half, 128, stride=32), :] = out[:128, lanes]
            out_ref[pl.ds(2 * cc + half + 16, 128, stride=32), :] = out[128:, lanes]


def middle(a, greens, place):
    t = tables()
    lane = lax.dynamic_index_in_dim(jnp.asarray(t["lane3"]), place[0], 0, keepdims=False)
    lane = jnp.broadcast_to(lane[:, :, None, :], (2, 16, 8, 128))
    return pl.pallas_call(
        middle_kernel,
        in_specs=[pl.BlockSpec(memory_space=pltpu.SMEM)] + [spec_vmem()] * 10,
        out_specs=spec_vmem(),
        out_shape=jax.ShapeDtypeStruct((4096, 128), f32),
        scratch_shapes=[pltpu.VMEM((16, 2, 256, 128), f32), pltpu.VMEM((2, 256, 128), f32)],
        compiler_params=params(),
        cost_estimate=cost(2 * 8 * 2 * 512 * 65536 * 3, 10 << 20),
        name="middle",
    )(
        place, a, *greens, jnp.asarray(t["t3"]), jnp.asarray(t["tw3"]), jnp.asarray(t["step3"]),
        lane, jnp.asarray(t["t4"]),
    )


def x_inverse_kernel(a_ref, t5_ref, tw_ref, t6_ref, out_ref):
    @pl.loop(0, 8)
    def _(cc):
        columns = []
        for half in range(2):
            re = a_ref[pl.ds(2 * cc + half, 128, stride=32), :]
            im = a_ref[pl.ds(2 * cc + half + 16, 128, stride=32), :]
            columns.append(jnp.concatenate([re, im], 0))
        u = dot3(t5_ref[0], t5_ref[1], jnp.concatenate(columns, 1), dot)
        rows = []
        for half in range(2):
            ur = u[:128, 128 * half : 128 * half + 128]
            ui = u[128:, 128 * half : 128 * half + 128]
            rows.append(
                jnp.concatenate(
                    [ur * tw_ref[0] - ui * tw_ref[1], ur * tw_ref[1] + ui * tw_ref[0]], 1
                )
            )
        out = dot3(t6_ref[0], t6_ref[1], jnp.concatenate(rows, 0), dot_nt)
        for half in range(2):
            lanes = slice(128 * half, 128 * half + 128)
            for b0 in range(2):
                b = 2 * (2 * cc + half) + b0
                out_ref[pl.ds(b, 32, stride=64), :] = out[64 * b0 : 64 * b0 + 32, lanes]
                out_ref[pl.ds(b + 32, 32, stride=64), :] = out[64 * b0 + 32 : 64 * b0 + 64, lanes]


def x_inverse(a):
    t = tables()
    return pl.pallas_call(
        x_inverse_kernel,
        in_specs=[spec_vmem()] * 4,
        out_specs=spec_vmem(),
        out_shape=jax.ShapeDtypeStruct((2048, 128), f32),
        compiler_params=params(),
        cost_estimate=cost(2 * 2048 * 65536 * 4, 4 << 20),
        name="x_inverse",
    )(a, jnp.asarray(t["t5"]), jnp.asarray(t["tw5"]), jnp.asarray(t["t6"]))


def residual_kernel(a_ref, incident_ref, contrast_ref, source_ref, out_ref):
    field = []
    for part in range(2):
        rows = [a_ref[pl.ds(block * 64 + part * 32, 32), :] for block in range(4)]
        field.append(incident_ref[part] + jnp.concatenate(rows, 0).T)
    out_ref[0] = contrast_ref[0] * field[0] - contrast_ref[1] * field[1] - source_ref[0]
    out_ref[1] = contrast_ref[0] * field[1] + contrast_ref[1] * field[0] - source_ref[1]


def residual_of(a, incident, contrast, source):
    tile = pl.BlockSpec((2, 128, 128), lambda t: (0, 0, t))
    return pl.pallas_call(
        residual_kernel,
        grid=(8,),
        in_specs=[pl.BlockSpec((256, 128), lambda t: (t, 0)), tile, tile, tile],
        out_specs=tile,
        out_shape=jax.ShapeDtypeStruct((2, 128, 1024), f32),
        cost_estimate=cost(0, 5 << 20),
        name="residual",
    )(a, incident, contrast, source)


def pack_kernel(place_ref, green_ref, out0_ref, out1_ref, out2_ref, out3_ref):
    flip = place_ref[0]
    upper = place_ref[1]
    lane = lax.broadcasted_iota(jnp.int32, (256, 128), 1)
    low = lane < 64
    pick = low == (flip == 0)
    swap = upper == 1
    outs = ((out0_ref, out1_ref), (out2_ref, out3_ref))
    for part in range(2):
        for across in range(2):
            column = jnp.where(swap, 1 - across, across)
            lanes = pl.ds(pl.multiple_of(column * 128, 128), 128)
            first = green_ref[part, 0, :, lanes]
            second = green_ref[part, 1, :, lanes]
            chooses_first = low != swap
            straight = jnp.where(chooses_first, first, second)
            crossed = pltpu.roll(jnp.where(chooses_first, second, first), 64, 1)
            outs[across][0][part] = jnp.where(pick, straight, crossed)
            outs[across][1][part] = jnp.where(pick, crossed, straight)


def pack_green(green, place):
    out = pl.BlockSpec((2, 256, 128), lambda t: (0, t, 0))
    shape = jax.ShapeDtypeStruct((2, 1024, 128), f32)
    return pl.pallas_call(
        pack_kernel,
        grid=(4,),
        in_specs=[
            pl.BlockSpec(memory_space=pltpu.SMEM),
            pl.BlockSpec((2, 2, 256, 256), lambda t: (0, 0, t, 0)),
        ],
        out_specs=[out] * 4,
        out_shape=[shape] * 4,
        compiler_params=params(),
        cost_estimate=cost(0, 8 << 20),
        name="pack_green",
    )(place, green.reshape(2, 2, 1024, 256))


def project_kernel(source_ref, ea_ref, eb_ref, row_ref, out_ref, lhs_ref, rhs_ref):
    @pl.when(pl.program_id(0) == 0)
    def _():
        re = source_ref[0]
        im = source_ref[1]
        for rows, cols, value in (
            (0, 0, re), (0, 1024, -im), (128, 0, im), (128, 1024, re),
        ):
            high, low = split(value)
            lhs_ref[0, rows : rows + 128, cols : cols + 1024] = high
            lhs_ref[1, rows : rows + 128, cols : cols + 1024] = low

    br = eb_ref[0]
    bi = eb_ref[1]
    for a in range(32):
        ar = ea_ref[0, a : a + 1, :]
        ai = ea_ref[1, a : a + 1, :]
        for part, value in ((0, ar * br - ai * bi), (1, ar * bi + ai * br)):
            high, low = split(value)
            rhs_ref[0, part * 1024 + a * 32 : part * 1024 + a * 32 + 32, :] = high
            rhs_ref[1, part * 1024 + a * 32 : part * 1024 + a * 32 + 32, :] = low
    inner = dot(lhs_ref[0], rhs_ref[0]) + (dot(lhs_ref[0], rhs_ref[1]) + dot(lhs_ref[1], rhs_ref[0]))
    ir = inner[:128]
    ii = inner[128:]
    fr = row_ref[0]
    fi = row_ref[1]
    pr = jnp.sum(fr * ir - fi * ii, axis=0, keepdims=True)
    pi_ = jnp.sum(fr * ii + fi * ir, axis=0, keepdims=True)
    out_ref[...] = jnp.concatenate([pr, pi_, jnp.zeros((6, pr.shape[1]), f32)], 0)


def project(source, ea, eb, rows):
    tile = 256
    whole = pl.BlockSpec((2, 128, 1024), lambda t: (0, 0, 0))
    return pl.pallas_call(
        project_kernel,
        grid=(R // tile,),
        in_specs=[
            whole,
            pl.BlockSpec((2, 32, tile), lambda t: (0, 0, t)),
            pl.BlockSpec((2, 32, tile), lambda t: (0, 0, t)),
            pl.BlockSpec((2, 128, tile), lambda t: (0, 0, t)),
        ],
        out_specs=pl.BlockSpec((8, tile), lambda t: (0, t)),
        out_shape=jax.ShapeDtypeStruct((8, R), f32),
        scratch_shapes=[pltpu.VMEM((2, 256, 2048), bf16), pltpu.VMEM((2, 2048, tile), bf16)],
        compiler_params=params(),
        cost_estimate=cost(2 * 256 * 2048 * 1024 * 3, 4 << 20),
        name="project",
    )(source, ea, eb, rows)


def backproject_kernel(weight_ref, ea_ref, eb_ref, out_ref, lhs_ref, rhs_ref):
    @pl.when(pl.program_id(0) == 0)
    def _():
        wr = weight_ref[0]
        wi = weight_ref[1]
        for rows, cols, value in (
            (0, 0, wr), (0, 1024, wi), (128, 0, wi), (128, 1024, -wr),
        ):
            high, low = split(value)
            lhs_ref[0, rows : rows + 128, cols : cols + 1024] = high
            lhs_ref[1, rows : rows + 128, cols : cols + 1024] = low

    br = eb_ref[0]
    bi = eb_ref[1]
    for a in range(8):
        ar = ea_ref[0, a : a + 1, :]
        ai = ea_ref[1, a : a + 1, :]
        for part, value in ((0, ar * br - ai * bi), (1, ar * bi + ai * br)):
            high, low = split(value)
            rhs_ref[0, a * 32 : a * 32 + 32, part * 1024 : part * 1024 + 1024] = high
            rhs_ref[1, a * 32 : a * 32 + 32, part * 1024 : part * 1024 + 1024] = low
    out = dot_nt(lhs_ref[0], rhs_ref[0]) + (
        dot_nt(lhs_ref[0], rhs_ref[1]) + dot_nt(lhs_ref[1], rhs_ref[0])
    )
    out_ref[0] = out[:128]
    out_ref[1] = out[128:]


def backproject(weights, ea, eb):
    whole = pl.BlockSpec((2, 128, 1024), lambda t: (0, 0, 0))
    return pl.pallas_call(
        backproject_kernel,
        grid=(4,),
        in_specs=[
            whole,
            pl.BlockSpec((2, 8, 1024), lambda t: (0, t, 0)),
            pl.BlockSpec((2, 32, 1024), lambda t: (0, 0, 0)),
        ],
        out_specs=pl.BlockSpec((2, 128, 256), lambda t: (0, 0, t)),
        out_shape=jax.ShapeDtypeStruct((2, 128, 1024), f32),
        scratch_shapes=[pltpu.VMEM((2, 256, 2048), bf16), pltpu.VMEM((2, 256, 2048), bf16)],
        compiler_params=params(),
        cost_estimate=cost(2 * 256 * 2048 * 1024 * 3, 4 << 20),
        name="backproject",
    )(weights, ea, eb)


def phase_pair(position, direction):
    phase = (wave_step * position)[:, None] * direction[None, :]
    return jnp.stack([jnp.cos(phase), -jnp.sin(phase)])


def sum_everywhere(value):
    def exchange(value, axis, size, strides):
        parts = [value] + [
            lax.ppermute(value, axis, [(j, j ^ stride) for j in range(size)]) for stride in strides
        ]
        while len(parts) > 1:
            parts = [parts[j] + parts[j + 1] for j in range(0, len(parts), 2)]
        return parts[0]

    value = exchange(value, "narrow", NARROW, (1,))
    value = exchange(value, "narrow", NARROW, (2,))
    value = exchange(value, "wide", WIDE, (4,))
    value = exchange(value, "wide", WIDE, (1, 2, 3))
    return exchange(value, "wide", WIDE, (8, 16, 24))


def local(sources, incident, contrast, green, angles, measured):
    wide = lax.axis_index("wide")
    narrow = lax.axis_index("narrow")
    place = jnp.stack([narrow % 2, narrow // 2]).astype(jnp.int32)
    source = sources[0]

    lines = columns_major(source)
    lines = lax.all_to_all(lines.reshape(WIDE, 64, 128), "wide", 0, 0, tiled=True)

    packed = pack_green(green, place)
    greens = [packed[0]] + [
        lax.ppermute(packed[k], "narrow", [(j, j ^ k) for j in range(NARROW)]) for k in (1, 2, 3)
    ]

    lines = x_forward(lines.reshape(2048, 128))
    lines = lax.all_to_all(lines.reshape(128, 32, 128), ("wide", "narrow"), 0, 0, tiled=True)
    lines = middle(lines.reshape(4096, 128), greens, place)
    lines = lax.all_to_all(lines.reshape(128, 32, 128), ("wide", "narrow"), 0, 0, tiled=True)
    lines = x_inverse(lines.reshape(4096, 128))
    lines = lax.all_to_all(lines.reshape(WIDE, 64, 128), "wide", 0, 0, tiled=True)
    residual = residual_of(lines.reshape(2048, 128), incident[0], contrast, source)

    row_position = (wide * 128 + jnp.arange(128, dtype=jnp.int32)).astype(f32) - N // 2 + 0.5
    block_position = (narrow * 1024 + 32 * jnp.arange(32, dtype=jnp.int32)).astype(f32) - N // 2 + 0.5
    cell_position = jnp.arange(32, dtype=jnp.int32).astype(f32)
    rows = phase_pair(row_position, jnp.cos(angles))
    sine = jnp.sin(angles)
    ea = phase_pair(block_position, sine)
    eb = phase_pair(cell_position, sine)
    partial_value = project(source, ea, eb, rows)
    total = sum_everywhere(partial_value)[:2]
    data_residual = measured - total[None] * (1.0 / N)
    rho_real = data_residual[0, 0][None, :]
    rho_imag = data_residual[0, 1][None, :]
    scale = 1.0 / math.sqrt(R)
    weights = jnp.stack(
        [
            (rows[0] * rho_real + rows[1] * rho_imag) * scale,
            (rows[0] * rho_imag - rows[1] * rho_real) * scale,
        ]
    )
    back = backproject(weights, ea, eb)
    return (residual[None], back[None], data_residual)


def solution(mesh):
    placed = (
        P(None, None, "wide", "narrow"),
        P(None, None, "wide", "narrow"),
        P(None, "wide", "narrow"),
        P(None, "narrow", "wide"),
        P(),
        P(),
    )
    return jax.shard_map(
        local,
        mesh=mesh,
        in_specs=placed,
        out_specs=(P(None, None, "wide", "narrow"), P(None, None, "wide", "narrow"), P()),
        check_vma=False,
    )
```

time: 660 us -> 234 us (0.35); the launches traced: 649 us -> 233 us
  local copies, waits for them, and re-layouts: 171 us -> 3.77 us
  blocking collectives: 187 us -> 25.9 us
  matrix products: 112 us -> 0 us
  Pallas kernels: 0 us -> 74 us
  other arithmetic: 56.1 us -> 9.41 us
  waiting for transfers between devices: 97.3 us -> 80.3 us
  starting transfers between devices: 24.6 us -> 38.6 us
    dot_general x12 -> x0, matrix products: 112 us -> none  [the longest x2 25.2 us: inverse_lines(): jnp.einsum('balmk,amcq->bclkq', blocks, turn_table(128, 128, 128, 1.0), p...]
    all_to_all x3 -> x1, blocking collectives: 121 us -> 25.9 us  [local(): lax.all_to_all(lines.reshape(WIDE, 64, 128), 'wide', 0, 0, tiled=True)]
    all_to_all x5 -> x3, waiting for transfers between devices: 97.3 us -> 3.05 us  [the longest x1 3.04 us: local(): lax.all_to_all(lines.reshape(WIDE, 64, 128), 'wide', 0, 0, tiled=True)]
    ppermute x0 -> x12, waiting for transfers between devices: none -> 77.2 us  [the longest x3 61.1 us: local(): lax.ppermute(packed[k], 'narrow', [(j, j ^ k) for j in range(NARROW)])]
    pallas_call x0 -> x8, Pallas kernels: none -> 74 us  [the longest x1 22.1 us: middle(): pl.pallas_call(middle_kernel, in_specs=[pl.BlockSpec(memory_space=pltpu.S...]
    unnamed x29 -> x16, local copies, waits for them, and re-layouts: 69.1 us -> 3.03 us
    psum x1 -> x0, blocking collectives: 65.5 us -> none  [local(): total = lax.psum(partial_value, ('wide', 'narrow'))]
    all_to_all x10 -> x0, local copies, waits for them, and re-layouts: 44.7 us -> none  [the longest x3 13.5 us: local(): lax.all_to_all(spread, 'narrow', split_axis=3, concat_axis=2, tiled=True)]
  transfers between devices with their start and end apart: 5 -> 15, of which waited for: 3 -> 8; matrix products, arithmetic and copies ran while one was open for 12% -> 4% of each run, Pallas kernels for 0% -> 12%
where the time goes in v1:
time: 234 us; the launch traced here: 233 us
  waiting for transfers between devices  80.3 us (34%)
  Pallas kernels  74 us (32%)
  starting transfers between devices  38.6 us (16%)
  blocking collectives  25.9 us (11%)
  other arithmetic  9.41 us (4%)
  local copies, waits for them, and re-layouts  3.77 us (2%)
    ppermute x3, waiting for transfers between devices, local(): lax.ppermute(packed[k], 'narrow', [(j, j ^ k) for j in range(NARROW)])  61.1 us
    all_to_all x1, blocking collectives, local(): lax.all_to_all(lines.reshape(WIDE, 64, 128), 'wide', 0, 0, tiled=True)  25.9 us
    pallas_call x1, Pallas kernels, middle(): pl.pallas_call(middle_kernel, in_specs=[pl.BlockSpec(memory_space=pltpu.S...  22.1 us
    ppermute x9, waiting for transfers between devices, exchange(): lax.ppermute(value, axis, [(j, j ^ stride) for j in range(size)])  16.1 us
    all_to_all x2, starting transfers between devices, local(): lax.all_to_all(lines.reshape(128, 32, 128), ('wide', 'narrow'), 0, 0, til...  15.1 us
    ppermute x9, starting transfers between devices, exchange(): lax.ppermute(value, axis, [(j, j ^ stride) for j in range(size)])  13 us
    pallas_call x1, Pallas kernels, x_forward(): pl.pallas_call(x_forward_kernel, in_specs=[spec_vmem()] * 4, out_specs=sp...  11.8 us
    pallas_call x1, Pallas kernels, x_inverse(): pl.pallas_call(x_inverse_kernel, in_specs=[spec_vmem()] * 4, out_specs=sp...  9.56 us
  transfers between devices with their start and end apart: 15, of which 8 were waited for; matrix products, arithmetic and copies ran while one was open for 4% of the time, Pallas kernels for 12%

profile of v1, /device:TPU:0, one launch (start us, length us, event | category | flops | bytes accessed | tf_op | source)
XLA Modules:
  0.0 232.7 jit_solution(4736536131498027527)
XLA Ops:
  0.6 5.5 %columns_major.1 = f32[2048,128]{1,0:T(8,128)} custom-call(f32[2,128,1024]{2,1,0:T(8,128)} %bitcast.23), custom_call_target="tpu_custom_call" | custom-call | bytes 2097152 | tf_op jit(solution)/shard_map/columns_major/pallas_call | solution.py:170
  6.1 25.9 %all_to_all.20 = f32[32,64,128]{2,1,0:T(8,128)} all-to-all(f32[32,64,128]{2,1,0:T(8,128)} %bitcast.28), channel_id=1, replica_groups=mesh['wide'=32,'narrow'=4] {'wide'}, dimensions={0} | all-to-all | bytes 2097152 | tf_op jit(solution)/shard_map/all_to_all | solution.py:564
  32.0 11.8 %x_forward.1 = f32[4096,128]{1,0:T(8,128)} custom-call(f32[2048,128]{1,0:T(8,128)} %bitcast.36, bf16[128,192]{1,0:T(8,128)(2,1)} %constant.81.clone.t1_ref, f32[2,64,128]{2,1,0:T(8,128)} %constant.82.clone.tw_ref, bf16[2,256,256]{2,1,0:T(8,128)(2,1)} %constant.83.clone.t2_ref), custom_call_target="tpu_custom_call" | custom-call | flops 1073741824 | bytes 4194304 | tf_op jit(solution)/shard_map/x_forward/pallas_call | solution.py:208
  43.8 6.9 %all-to-all-start.1 = ((f32[128,32,128]{2,1,0:T(8,128)}), f32[128,32,128]{2,1,0:T(8,128)S(1)}, u32[]{:S(2)}, u32[]{:S(2)}) async-start(f32[128,32,128]{2,1,0:T(8,128)} %bitcast.32), calls=%async_computation.1 | async-start | bytes 4194304 | tf_op jit(solution)/shard_map/all_to_all | solution.py:572
  51.4 5.0 %pack_green.1 = (f32[2,1024,128]{2,1,0:T(8,128)}, f32[2,1024,128]{2,1,0:T(8,128)}, f32[2,1024,128]{2,1,0:T(8,128)}, f32[2,1024,128]{2,1,0:T(8,128)}) custom-call(s32[2]{0:T(128)} %pad_add_fusion.place_ref, f32[2,2,1024,256]{3,2,1,0:T(8,128)} %bitcast.27), custom_call_target="tpu_custom_call" | custom-call | bytes 8388608 | tf_op jit(solution)/shard_map/pack_green/pallas_call | solution.py:422
  56.4 2.6 %collective-permute-start.1 = (f32[2,1024,128]{2,1,0:T(8,128)}, f32[2,1024,128]{2,1,0:T(8,128)}, u32[]{:S(2)}, u32[]{:S(2)}) collective-permute-start(f32[2,1024,128]{2,1,0:T(8,128)} %get-tuple-element.9), channel_id=1, source_target_pairs={{0,2},{1,3},{2,0},{3,1},{4,6},{5,7},{6,4},{7,5},{8,10},{9,11},{10,... | collective-permute-start | bytes 3145736 | tf_op jit(solution)/shard_map/ppermute | solution.py:568
  59.8 39.6 %collective-permute-done.1.r2_ref = f32[2,1024,128]{2,1,0:T(8,128)} collective-permute-done((f32[2,1024,128]{2,1,0:T(8,128)}, f32[2,1024,128]{2,1,0:T(8,128)}, u32[]{:S(2)}, u32[]{:S(2)}) %collective-permute-start.1) | collective-permute-done | bytes 1048608 | tf_op jit(solution)/shard_map/ppermute | solution.py:568
  99.3 21.5 %collective-permute-done.2.r3_ref = f32[2,1024,128]{2,1,0:T(8,128)} collective-permute-done((f32[2,1024,128]{2,1,0:T(8,128)}, f32[2,1024,128]{2,1,0:T(8,128)}, u32[]{:S(2)}, u32[]{:S(2)}) %collective-permute-start.2) | collective-permute-done | bytes 1048608 | tf_op jit(solution)/shard_map/ppermute | solution.py:568
  122.2 22.1 %middle.1 = f32[4096,128]{1,0:T(8,128)} custom-call(s32[2]{0:T(128)} %pad_add_fusion.place_ref, f32[4096,128]{1,0:T(8,128)} %bitcast.31, f32[2,1024,128]{2,1,0:T(8,128)} %get-tuple-element.7.r0_ref, f32[2,1024,128]{2,1,0:T(8,128)} %copy-done.7, f32[2,1024,128]{2,1,0:T(8,128)} %collective-permute-done.1.r2_ref, ...), custom_call_target="tpu_custom_call" | custom-call | flops 3221225472 | bytes 10485760 | tf_op jit(solution)/shard_map/middle/pallas_call | solution.py:321
  144.3 8.2 %all-to-all-start.2 = ((f32[128,32,128]{2,1,0:T(8,128)}), f32[128,32,128]{2,1,0:T(8,128)S(1)}, u32[]{:S(2)}, u32[]{:S(2)}) async-start(f32[128,32,128]{2,1,0:T(8,128)} %bitcast.29), calls=%async_computation.2 | async-start | bytes 4194304 | tf_op jit(solution)/shard_map/all_to_all | solution.py:574
  157.5 6.9 %project.1 = f32[8,1024]{1,0:T(8,128)} custom-call(f32[2,128,1024]{2,1,0:T(8,128)} %bitcast.24, f32[2,32,1024]{2,1,0:T(8,128)} %get-tuple-element.25.ea_ref, f32[2,32,1024]{2,1,0:T(8,128)} %get-tuple-element.26.eb_ref, f32[2,128,1024]{2,1,0:T(8,128)} %pad_maximum_fusion.row_ref), custom_call_target="tpu_custom_call" | custom-call | flops 3221225472 | bytes 4194304 | tf_op jit(solution)/shard_map/project/pallas_call | solution.py:471
  166.6 2.5 %collective-permute-start.4 = (f32[8,1024]{1,0:T(8,128)S(1)}, f32[8,1024]{1,0:T(8,128)S(1)}, u32[]{:S(2)}, u32[]{:S(2)}) collective-permute-start(f32[8,1024]{1,0:T(8,128)S(1)} %add.104), channel_id=1, source_target_pairs={{0,2},{1,3},{2,0},{3,1},{4,6},{5,7},{6,4},{7,5},{8,10},{9,11},{10,... | collective-permute-start | bytes 98312 | tf_op jit(solution)/shard_map/ppermute | solution.py:544
  169.1 6.9 %collective-permute-done.4 = f32[8,1024]{1,0:T(8,128)S(1)} collective-permute-done((f32[8,1024]{1,0:T(8,128)S(1)}, f32[8,1024]{1,0:T(8,128)S(1)}, u32[]{:S(2)}, u32[]{:S(2)}) %collective-permute-start.4) | collective-permute-done | bytes 32800 | tf_op jit(solution)/shard_map/ppermute | solution.py:544
  175.9 3.9 %collective-permute-done.5 = f32[8,1024]{1,0:T(8,128)S(1)} collective-permute-done((f32[8,1024]{1,0:T(8,128)S(1)}, f32[8,1024]{1,0:T(8,128)S(1)}, u32[]{:S(2)}, u32[]{:S(2)}) %collective-permute-start.5) | collective-permute-done | bytes 32800 | tf_op jit(solution)/shard_map/ppermute | solution.py:544
  179.8 3.0 %collective-permute-start.7 = (f32[8,1024]{1,0:T(8,128)S(1)}, f32[8,1024]{1,0:T(8,128)S(1)}, u32[]{:S(2)}, u32[]{:S(2)}) collective-permute-start(f32[8,1024]{1,0:T(8,128)S(1)} %add.106), channel_id=1, source_target_pairs={{0,8},{4,12},{8,0},{12,4},{16,24},{20,28},{24,16},{28,20},{32,40},... | collective-permute-start | bytes 98312 | tf_op jit(solution)/shard_map/ppermute | solution.py:544
  182.9 3.2 %collective-permute-start.8 = (f32[8,1024]{1,0:T(8,128)S(1)}, f32[8,1024]{1,0:T(8,128)S(1)}, u32[]{:S(2)}, u32[]{:S(2)}) collective-permute-start(f32[8,1024]{1,0:T(8,128)S(1)} %add.106), channel_id=1, source_target_pairs={{0,12},{4,8},{8,4},{12,0},{16,28},{20,24},{24,20},{28,16},{32,44},... | collective-permute-start | bytes 98312 | tf_op jit(solution)/shard_map/ppermute | solution.py:544
  186.0 2.0 collective-permute-done.8
  189.9 3.3 %collective-permute-start.11 = (f32[8,1024]{1,0:T(8,128)S(1)}, f32[8,1024]{1,0:T(8,128)S(1)}, u32[]{:S(2)}, u32[]{:S(2)}) collective-permute-start(f32[8,1024]{1,0:T(8,128)S(1)} %add_add_fusion), channel_id=1, source_target_pairs={{0,96},{4,100},{8,104},{12,108},{16,112},{20,116},{24,120},{28,124... | collective-permute-start | bytes 98312 | tf_op jit(solution)/shard_map/ppermute | solution.py:544
  195.6 9.6 %x_inverse.1 = f32[2048,128]{1,0:T(8,128)} custom-call(f32[4096,128]{1,0:T(8,128)} %bitcast.30, bf16[2,256,256]{2,1,0:T(8,128)(2,1)} %constant.89.clone.t5_ref, f32[2,128,128]{2,1,0:T(8,128)} %constant.90.clone.tw_ref, bf16[2,128,256]{2,1,0:T(8,128)(2,1)} %constant.91.clone.t6_ref), custom_call_target="tpu_custom_call" | custom-call | flops 1073741824 | bytes 4194304 | tf_op jit(solution)/shard_map/x_inverse/pallas_call | solution.py:365
  205.2 7.1 %all-to-all-start.3 = ((f32[32,64,128]{2,1,0:T(8,128)}), f32[32,64,128]{2,1,0:T(8,128)S(1)}, u32[]{:S(2)}, u32[]{:S(2)}) async-start(f32[32,64,128]{2,1,0:T(8,128)} %bitcast.35), calls=%async_computation.3 | async-start | bytes 2097152 | tf_op jit(solution)/shard_map/all_to_all | solution.py:576
  212.4 2.0 add_multiply_fusion
  215.6 6.9 %backproject.1 = f32[2,128,1024]{2,1,0:T(8,128)} custom-call(f32[2,128,1024]{2,1,0:T(8,128)} %pad_maximum_fusion.1.weight_ref, f32[2,32,1024]{2,1,0:T(8,128)} %get-tuple-element.25.ea_ref, f32[2,32,1024]{2,1,0:T(8,128)} %get-tuple-element.26.eb_ref), custom_call_target="tpu_custom_call" | custom-call | flops 3221225472 | bytes 4194304 | tf_op jit(solution)/shard_map/backproject/pallas_call | solution.py:519
  222.5 3.0 %all-to-all-done.3 = f32[32,64,128]{2,1,0:T(8,128)S(1)} async-done(((f32[32,64,128]{2,1,0:T(8,128)}), f32[32,64,128]{2,1,0:T(8,128)S(1)}, u32[]{:S(2)}, u32[]{:S(2)}) %all-to-all-start.3) | async-done | bytes 1048608 | tf_op jit(solution)/shard_map/all_to_all | solution.py:576
  226.5 6.2 %residual.1 = f32[2,128,1024]{2,1,0:T(8,128)} custom-call(f32[2048,128]{1,0:T(8,128)} %bitcast.26, f32[2,128,1024]{2,1,0:T(8,128)} %bitcast.33, f32[2,128,1024]{2,1,0:T(8,128)} %contrast_ref.1, f32[2,128,1024]{2,1,0:T(8,128)} %bitcast.25), custom_call_target="tpu_custom_call" | custom-call | bytes 5242880 | tf_op jit(solution)/shard_map/residual/pallas_call | solution.py:387
  (50 shorter events, 16.3 us)
Async XLA Ops:
  43.8 77.1 %all-to-all-start.1 = ((f32[128,32,128]{2,1,0:T(8,128)}), f32[128,32,128]{2,1,0:T(8,128)S(1)}, u32[]{:S(2)}, u32[]{:S(2)}) async-start(f32[128,32,128]{2,1,0:T(8,128)} %bitcast.32), calls=%async_computation.1 | async-start | bytes 4194304 | tf_op jit(solution)/shard_map/all_to_all | solution.py:572
  51.4 8.4 %copy-start.4 = (f32[2,2,16,128]{3,2,1,0:T(8,128)S(1)}, f32[2,2,16,128]{3,2,1,0:T(8,128)}, u32[]{:S(2)}) copy-start(f32[2,2,16,128]{3,2,1,0:T(8,128)} %constant.84.clone) | copy-start | bytes 98308
  56.4 3.4 %collective-permute-start = (f32[2,1024,128]{2,1,0:T(8,128)}, f32[2,1024,128]{2,1,0:T(8,128)S(1)}, u32[]{:S(2)}, u32[]{:S(2)}) collective-permute-start(f32[2,1024,128]{2,1,0:T(8,128)} %get-tuple-element.8), channel_id=1, source_target_pairs={{0,1},{1,0},{2,3},{3,2},{4,5},{5,4},{6,7},{7,6},{8,9},{9,8},{10,11... | collective-permute-start | bytes 3145736 | tf_op jit(solution)/shard_map/ppermute | solution.py:568
  56.4 43.0 %collective-permute-start.1 = (f32[2,1024,128]{2,1,0:T(8,128)}, f32[2,1024,128]{2,1,0:T(8,128)}, u32[]{:S(2)}, u32[]{:S(2)}) collective-permute-start(f32[2,1024,128]{2,1,0:T(8,128)} %get-tuple-element.9), channel_id=1, source_target_pairs={{0,2},{1,3},{2,0},{3,1},{4,6},{5,7},{6,4},{7,5},{8,10},{9,11},{10,... | collective-permute-start | bytes 3145736 | tf_op jit(solution)/shard_map/ppermute | solution.py:568
  59.0 61.9 %collective-permute-start.2 = (f32[2,1024,128]{2,1,0:T(8,128)}, f32[2,1024,128]{2,1,0:T(8,128)}, u32[]{:S(2)}, u32[]{:S(2)}) collective-permute-start(f32[2,1024,128]{2,1,0:T(8,128)} %get-tuple-element.10), channel_id=1, source_target_pairs={{0,3},{1,2},{2,1},{3,0},{4,7},{5,6},{6,5},{7,4},{8,11},{9,10},{10,... | collective-permute-start | bytes 3145736 | tf_op jit(solution)/shard_map/ppermute | solution.py:568
  59.7 61.8 %copy-start.7 = (f32[2,1024,128]{2,1,0:T(8,128)}, f32[2,1024,128]{2,1,0:T(8,128)S(1)}, u32[]{:S(2)}) copy-start(f32[2,1024,128]{2,1,0:T(8,128)S(1)} %collective-permute-done.r1_ref) | copy-start | bytes 3145732
  120.9 1.4 copy-start.2
  144.3 8.2 %copy-start.6 = (f32[1024]{0:T(1024)S(1)}, f32[1024]{0:T(1024)}, u32[]{:S(2)}) copy-start(f32[1024]{0:T(1024)} %param.21) | copy-start | bytes 12292
  144.3 50.0 %all-to-all-start.2 = ((f32[128,32,128]{2,1,0:T(8,128)}), f32[128,32,128]{2,1,0:T(8,128)S(1)}, u32[]{:S(2)}, u32[]{:S(2)}) async-start(f32[128,32,128]{2,1,0:T(8,128)} %bitcast.29), calls=%async_computation.2 | async-start | bytes 4194304 | tf_op jit(solution)/shard_map/all_to_all | solution.py:574
  164.4 1.4 collective-permute-start.3
  166.6 9.3 %collective-permute-start.4 = (f32[8,1024]{1,0:T(8,128)S(1)}, f32[8,1024]{1,0:T(8,128)S(1)}, u32[]{:S(2)}, u32[]{:S(2)}) collective-permute-start(f32[8,1024]{1,0:T(8,128)S(1)} %add.104), channel_id=1, source_target_pairs={{0,2},{1,3},{2,0},{3,1},{4,6},{5,7},{6,4},{7,5},{8,10},{9,11},{10,... | collective-permute-start | bytes 98312 | tf_op jit(solution)/shard_map/ppermute | solution.py:544
  175.9 3.9 %collective-permute-start.5 = (f32[8,1024]{1,0:T(8,128)S(1)}, f32[8,1024]{1,0:T(8,128)S(1)}, u32[]{:S(2)}, u32[]{:S(2)}) collective-permute-start(f32[8,1024]{1,0:T(8,128)S(1)} %add.105), channel_id=1, source_target_pairs={{0,16},{4,20},{8,24},{12,28},{16,0},{20,4},{24,8},{28,12},{32,48},... | collective-permute-start | bytes 98312 | tf_op jit(solution)/shard_map/ppermute | solution.py:544
  179.8 6.2 %collective-permute-start.7 = (f32[8,1024]{1,0:T(8,128)S(1)}, f32[8,1024]{1,0:T(8,128)S(1)}, u32[]{:S(2)}, u32[]{:S(2)}) collective-permute-start(f32[8,1024]{1,0:T(8,128)S(1)} %add.106), channel_id=1, source_target_pairs={{0,8},{4,12},{8,0},{12,4},{16,24},{20,28},{24,16},{28,20},{32,40},... | collective-permute-start | bytes 98312 | tf_op jit(solution)/shard_map/ppermute | solution.py:544
  182.9 5.1 %collective-permute-start.8 = (f32[8,1024]{1,0:T(8,128)S(1)}, f32[8,1024]{1,0:T(8,128)S(1)}, u32[]{:S(2)}, u32[]{:S(2)}) collective-permute-start(f32[8,1024]{1,0:T(8,128)S(1)} %add.106), channel_id=1, source_target_pairs={{0,12},{4,8},{8,4},{12,0},{16,28},{20,24},{24,20},{28,16},{32,44},... | collective-permute-start | bytes 98312 | tf_op jit(solution)/shard_map/ppermute | solution.py:544
  186.0 3.9 %collective-permute-start.6 = (f32[8,1024]{1,0:T(8,128)S(1)}, f32[8,1024]{1,0:T(8,128)S(1)}, u32[]{:S(2)}, u32[]{:S(2)}) collective-permute-start(f32[8,1024]{1,0:T(8,128)S(1)} %add.106), channel_id=1, source_target_pairs={{0,4},{4,0},{8,12},{12,8},{16,20},{20,16},{24,28},{28,24},{32,36},... | collective-permute-start | bytes 98312 | tf_op jit(solution)/shard_map/ppermute | solution.py:544
  189.9 22.4 %collective-permute-start.11 = (f32[8,1024]{1,0:T(8,128)S(1)}, f32[8,1024]{1,0:T(8,128)S(1)}, u32[]{:S(2)}, u32[]{:S(2)}) collective-permute-start(f32[8,1024]{1,0:T(8,128)S(1)} %add_add_fusion), channel_id=1, source_target_pairs={{0,96},{4,100},{8,104},{12,108},{16,112},{20,116},{24,120},{28,124... | collective-permute-start | bytes 98312 | tf_op jit(solution)/shard_map/ppermute | solution.py:544
  193.2 19.2 %collective-permute-start.10 = (f32[8,1024]{1,0:T(8,128)S(1)}, f32[8,1024]{1,0:T(8,128)S(1)}, u32[]{:S(2)}, u32[]{:S(2)}) collective-permute-start(f32[8,1024]{1,0:T(8,128)S(1)} %add_add_fusion), channel_id=1, source_target_pairs={{0,64},{4,68},{8,72},{12,76},{16,80},{20,84},{24,88},{28,92},{32,9... | collective-permute-start | bytes 98312 | tf_op jit(solution)/shard_map/ppermute | solution.py:544
  194.3 18.1 %collective-permute-start.9 = (f32[8,1024]{1,0:T(8,128)S(1)}, f32[8,1024]{1,0:T(8,128)S(1)}, u32[]{:S(2)}, u32[]{:S(2)}) collective-permute-start(f32[8,1024]{1,0:T(8,128)S(1)} %add_add_fusion), channel_id=1, source_target_pairs={{0,32},{4,36},{8,40},{12,44},{16,48},{20,52},{24,56},{28,60},{32,0... | collective-permute-start | bytes 98312 | tf_op jit(solution)/shard_map/ppermute | solution.py:544
  194.3 1.4 copy-start.1
  195.6 16.8 %copy-start.5 = (f32[1,2,1024]{2,1,0:T(2,128)S(1)}, f32[1,2,1024]{2,1,0:T(2,128)}, u32[]{:S(2)}) copy-start(f32[1,2,1024]{2,1,0:T(2,128)} %param.22) | copy-start | bytes 24580
  205.2 20.4 %all-to-all-start.3 = ((f32[32,64,128]{2,1,0:T(8,128)}), f32[32,64,128]{2,1,0:T(8,128)S(1)}, u32[]{:S(2)}, u32[]{:S(2)}) async-start(f32[32,64,128]{2,1,0:T(8,128)} %bitcast.35), calls=%async_computation.3 | async-start | bytes 2097152 | tf_op jit(solution)/shard_map/all_to_all | solution.py:576
  212.4 10.1 %copy-start.3 = (f32[1,2,1024]{2,1,0:T(2,128)}, f32[1,2,1024]{2,1,0:T(2,128)S(1)}, u32[]{:S(2)}) copy-start(f32[1,2,1024]{2,1,0:T(2,128)S(1)} %fusion.6) | copy-start | bytes 24580
  225.5 1.0 copy-start

commit v2 on v1

--- a/solution.py
+++ b/solution.py
@@ -160,18 +160,20 @@
 
 
 def columns_kernel(source_ref, out_ref):
-    for part in range(2):
-        turned = source_ref[part].T
-        for block in range(4):
-            out_ref[pl.ds(block * 64 + part * 32, 32), :] = turned[block * 32 : block * 32 + 32]
+    for tile in range(4):
+        for part in range(2):
+            turned = source_ref[part, :, 128 * tile : 128 * tile + 128].T
+            for block in range(4):
+                first = 256 * tile + block * 64 + part * 32
+                out_ref[first : first + 32, :] = turned[block * 32 : block * 32 + 32]
 
 
 def columns_major(source):
     return pl.pallas_call(
         columns_kernel,
-        grid=(8,),
-        in_specs=[pl.BlockSpec((2, 128, 128), lambda t: (0, 0, t))],
-        out_specs=pl.BlockSpec((256, 128), lambda t: (t, 0)),
+        grid=(2,),
+        in_specs=[pl.BlockSpec((2, 128, 512), lambda t: (0, 0, t))],
+        out_specs=pl.BlockSpec((1024, 128), lambda t: (t, 0)),
         out_shape=jax.ShapeDtypeStruct((2048, 128), f32),
         cost_estimate=cost(0, 2 << 20),
         name="columns_major",
@@ -179,7 +181,7 @@
 
 
 def x_forward_kernel(a_ref, t1_ref, tw_ref, t2_ref, out_ref):
-    @pl.loop(0, 16)
+    @pl.loop(0, 16, unroll=8)
     def _(c):
         columns = []
         for b0 in range(2):
@@ -218,8 +220,15 @@
 
 def middle_kernel(
     place_ref, a_ref, r0_ref, r1_ref, r2_ref, r3_ref, t3_ref, tw_ref, step_ref, lane_ref, t4_ref,
-    out_ref, u_ref, now_ref,
+    out_ref, u_ref, now_ref, green_ref, late_ref, arrived,
 ):
+    copies = [
+        pltpu.make_async_copy(ref, green_ref.at[k], arrived.at[k])
+        for k, ref in enumerate((r0_ref, r1_ref, r2_ref.at[0], r3_ref))
+    ]
+    copies.append(pltpu.make_async_copy(t4_ref, late_ref, arrived.at[4]))
+    for copy in copies:
+        copy.start()
     flip = place_ref[0]
     upper = place_ref[1]
     sign = 1.0 - 2.0 * flip.astype(f32)
@@ -234,7 +243,7 @@
 
     now_ref[...] = tw_ref[...]
 
-    @pl.loop(0, 8)
+    @pl.loop(0, 8, unroll=2)
     def _(cc):
         columns = []
         for half in range(2):
@@ -251,12 +260,15 @@
             u_ref[2 * cc + half, 1] = ur * ni + ui * nr
             advance()
 
+    for copy in copies:
+        copy.wait()
+
     lane = lax.broadcasted_iota(jnp.int32, (8, 128), 1)
     low = lane < 64
     sgn = jnp.where(low, 1.0, -1.0).astype(f32)
     mine = low == (upper == 0)
 
-    @pl.loop(0, 32)
+    @pl.loop(0, 32, unroll=2)
     def _(tile):
         rows = pl.ds(pl.multiple_of(tile * 8, 8), 8)
         values = [(u_ref[c, 0, rows, :], u_ref[c, 1, rows, :]) for c in range(16)]
@@ -264,15 +276,14 @@
         back = []
         for e in range(16):
             g, q, row_block = e // 8, (e // 4) % 2, e % 4
-            own_ref, other_ref = ((r0_ref, r2_ref), (r1_ref, r3_ref))[g]
             grows = pl.ds(pl.multiple_of(tile * 8 + row_block * 256, 8), 8)
             green = []
             for part in range(2):
-                own = own_ref[part, grows, :]
-                other = other_ref[part, grows, :]
+                own = green_ref[g, part, grows, :]
+                other = green_ref[g + 2, part, grows, :]
                 green.append(jnp.where(mine, own, other) if q == 0 else jnp.where(mine, other, own))
-            lr = lane_ref[0, e]
-            li = lane_ref[1, e]
+            lr = lane_ref[flip, 0, e : e + 1, :]
+            li = lane_ref[flip, 1, e : e + 1, :]
             sr, si = spectrum[e]
             vr = sr * lr - si * li
             vi = sr * li + si * lr
@@ -297,7 +308,7 @@
 
     now_ref[...] = tw_ref[...]
 
-    @pl.loop(0, 8)
+    @pl.loop(0, 8, unroll=2)
     def _(cc):
         columns = []
         for half in range(2):
@@ -307,7 +318,7 @@
             ni = now_ref[1]
             columns.append(jnp.concatenate([ur * nr + ui * ni, ui * nr - ur * ni], 0))
             advance()
-        out = dot3(t4_ref[0], t4_ref[1], jnp.concatenate(columns, 1), dot)
+        out = dot3(late_ref[0], late_ref[1], jnp.concatenate(columns, 1), dot)
         for half in range(2):
             lanes = slice(128 * half, 128 * half + 128)
             out_ref[pl.ds(2 * cc + half, 128, stride=32), :] = out[:128, lanes]
@@ -316,25 +327,32 @@
 
 def middle(a, greens, place):
     t = tables()
-    lane = lax.dynamic_index_in_dim(jnp.asarray(t["lane3"]), place[0], 0, keepdims=False)
-    lane = jnp.broadcast_to(lane[:, :, None, :], (2, 16, 8, 128))
     return pl.pallas_call(
         middle_kernel,
-        in_specs=[pl.BlockSpec(memory_space=pltpu.SMEM)] + [spec_vmem()] * 10,
+        in_specs=[pl.BlockSpec(memory_space=pltpu.SMEM), spec_vmem()]
+        + [pl.BlockSpec(memory_space=pl.ANY)] * 4
+        + [spec_vmem()] * 4
+        + [pl.BlockSpec(memory_space=pl.ANY)],
         out_specs=spec_vmem(),
         out_shape=jax.ShapeDtypeStruct((4096, 128), f32),
-        scratch_shapes=[pltpu.VMEM((16, 2, 256, 128), f32), pltpu.VMEM((2, 256, 128), f32)],
+        scratch_shapes=[
+            pltpu.VMEM((16, 2, 256, 128), f32),
+            pltpu.VMEM((2, 256, 128), f32),
+            pltpu.VMEM((4, 2, 1024, 128), f32),
+            pltpu.VMEM((2, 256, 512), bf16),
+            pltpu.SemaphoreType.DMA((5,)),
+        ],
         compiler_params=params(),
         cost_estimate=cost(2 * 8 * 2 * 512 * 65536 * 3, 10 << 20),
         name="middle",
     )(
         place, a, *greens, jnp.asarray(t["t3"]), jnp.asarray(t["tw3"]), jnp.asarray(t["step3"]),
-        lane, jnp.asarray(t["t4"]),
+        jnp.asarray(t["lane3"]), jnp.asarray(t["t4"]),
     )
 
 
 def x_inverse_kernel(a_ref, t5_ref, tw_ref, t6_ref, out_ref):
-    @pl.loop(0, 8)
+    @pl.loop(0, 8, unroll=8)
     def _(cc):
         columns = []
         for half in range(2):
@@ -374,63 +392,67 @@
 
 
 def residual_kernel(a_ref, incident_ref, contrast_ref, source_ref, out_ref):
-    field = []
-    for part in range(2):
-        rows = [a_ref[pl.ds(block * 64 + part * 32, 32), :] for block in range(4)]
-        field.append(incident_ref[part] + jnp.concatenate(rows, 0).T)
-    out_ref[0] = contrast_ref[0] * field[0] - contrast_ref[1] * field[1] - source_ref[0]
-    out_ref[1] = contrast_ref[0] * field[1] + contrast_ref[1] * field[0] - source_ref[1]
+    for tile in range(4):
+        lanes = slice(128 * tile, 128 * tile + 128)
+        field = []
+        for part in range(2):
+            rows = []
+            for block in range(4):
+                first = 256 * tile + block * 64 + part * 32
+                rows.append(a_ref[first : first + 32, :])
+            field.append(incident_ref[part, :, lanes] + jnp.concatenate(rows, 0).T)
+        cr = contrast_ref[0, :, lanes]
+        ci = contrast_ref[1, :, lanes]
+        out_ref[0, :, lanes] = cr * field[0] - ci * field[1] - source_ref[0, :, lanes]
+        out_ref[1, :, lanes] = cr * field[1] + ci * field[0] - source_ref[1, :, lanes]
 
 
 def residual_of(a, incident, contrast, source):
-    tile = pl.BlockSpec((2, 128, 128), lambda t: (0, 0, t))
+    tile = pl.BlockSpec((2, 128, 512), lambda t: (0, 0, t))
     return pl.pallas_call(
         residual_kernel,
-        grid=(8,),
-        in_specs=[pl.BlockSpec((256, 128), lambda t: (t, 0)), tile, tile, tile],
+        grid=(2,),
+        in_specs=[pl.BlockSpec((1024, 128), lambda t: (t, 0)), tile, tile, tile],
         out_specs=tile,
         out_shape=jax.ShapeDtypeStruct((2, 128, 1024), f32),
+        compiler_params=params(),
         cost_estimate=cost(0, 5 << 20),
         name="residual",
     )(a, incident, contrast, source)
 
 
-def pack_kernel(place_ref, green_ref, out0_ref, out1_ref, out2_ref, out3_ref):
+def pack_kernel(across, place_ref, green_ref, out_ref):
     flip = place_ref[0]
     upper = place_ref[1]
-    lane = lax.broadcasted_iota(jnp.int32, (256, 128), 1)
+    lane = lax.broadcasted_iota(jnp.int32, (512, 128), 1)
     low = lane < 64
     pick = low == (flip == 0)
     swap = upper == 1
-    outs = ((out0_ref, out1_ref), (out2_ref, out3_ref))
+    column = jnp.where(swap, 1 - across, across)
+    lanes = pl.ds(pl.multiple_of(column * 128, 128), 128)
+    chooses_first = low != swap
     for part in range(2):
-        for across in range(2):
-            column = jnp.where(swap, 1 - across, across)
-            lanes = pl.ds(pl.multiple_of(column * 128, 128), 128)
-            first = green_ref[part, 0, :, lanes]
-            second = green_ref[part, 1, :, lanes]
-            chooses_first = low != swap
-            straight = jnp.where(chooses_first, first, second)
-            crossed = pltpu.roll(jnp.where(chooses_first, second, first), 64, 1)
-            outs[across][0][part] = jnp.where(pick, straight, crossed)
-            outs[across][1][part] = jnp.where(pick, crossed, straight)
-
-
-def pack_green(green, place):
-    out = pl.BlockSpec((2, 256, 128), lambda t: (0, t, 0))
-    shape = jax.ShapeDtypeStruct((2, 1024, 128), f32)
-    return pl.pallas_call(
-        pack_kernel,
-        grid=(4,),
+        first = green_ref[part, 0, :, lanes]
+        second = green_ref[part, 1, :, lanes]
+        straight = jnp.where(chooses_first, first, second)
+        crossed = pltpu.roll(jnp.where(chooses_first, second, first), 64, 1)
+        out_ref[0, part] = jnp.where(pick, straight, crossed)
+        out_ref[1, part] = jnp.where(pick, crossed, straight)
+
+
+def pack_green(green, place, across):
+    return pl.pallas_call(
+        functools.partial(pack_kernel, across),
+        grid=(2,),
         in_specs=[
             pl.BlockSpec(memory_space=pltpu.SMEM),
-            pl.BlockSpec((2, 2, 256, 256), lambda t: (0, 0, t, 0)),
+            pl.BlockSpec((2, 2, 512, 256), lambda t: (0, 0, t, 0)),
         ],
-        out_specs=[out] * 4,
-        out_shape=[shape] * 4,
+        out_specs=pl.BlockSpec((2, 2, 512, 128), lambda t: (0, 0, t, 0)),
+        out_shape=jax.ShapeDtypeStruct((2, 2, 1024, 128), f32),
         compiler_params=params(),
-        cost_estimate=cost(0, 8 << 20),
-        name="pack_green",
+        cost_estimate=cost(0, 6 << 20),
+        name="pack_far" if across else "pack_near",
     )(place, green.reshape(2, 2, 1024, 256))
 
 
@@ -538,7 +560,7 @@
     return jnp.stack([jnp.cos(phase), -jnp.sin(phase)])
 
 
-def sum_everywhere(value):
+def sum_over(value, steps):
     def exchange(value, axis, size, strides):
         parts = [value] + [
             lax.ppermute(value, axis, [(j, j ^ stride) for j in range(size)]) for stride in strides
@@ -547,11 +569,9 @@
             parts = [parts[j] + parts[j + 1] for j in range(0, len(parts), 2)]
         return parts[0]
 
-    value = exchange(value, "narrow", NARROW, (1,))
-    value = exchange(value, "narrow", NARROW, (2,))
-    value = exchange(value, "wide", WIDE, (4,))
-    value = exchange(value, "wide", WIDE, (1, 2, 3))
-    return exchange(value, "wide", WIDE, (8, 16, 24))
+    for axis, size, strides in steps:
+        value = exchange(value, axis, size, strides)
+    return value
 
 
 def local(sources, incident, contrast, green, angles, measured):
@@ -560,21 +580,16 @@
     place = jnp.stack([narrow % 2, narrow // 2]).astype(jnp.int32)
     source = sources[0]
 
-    lines = columns_major(source)
+    def partner(value, k):
+        return lax.ppermute(value, "narrow", [(j, j ^ k) for j in range(NARROW)])
+
+    far = pack_green(green, place, 1)
+    far, source_after, green_after = lax.optimization_barrier((far, source, green))
+    far = partner(far, 2)
+    lines = columns_major(source_after)
+    near = pack_green(green_after, place, 0)
+    near_partner = partner(near[1], 1)
     lines = lax.all_to_all(lines.reshape(WIDE, 64, 128), "wide", 0, 0, tiled=True)
-
-    packed = pack_green(green, place)
-    greens = [packed[0]] + [
-        lax.ppermute(packed[k], "narrow", [(j, j ^ k) for j in range(NARROW)]) for k in (1, 2, 3)
-    ]
-
-    lines = x_forward(lines.reshape(2048, 128))
-    lines = lax.all_to_all(lines.reshape(128, 32, 128), ("wide", "narrow"), 0, 0, tiled=True)
-    lines = middle(lines.reshape(4096, 128), greens, place)
-    lines = lax.all_to_all(lines.reshape(128, 32, 128), ("wide", "narrow"), 0, 0, tiled=True)
-    lines = x_inverse(lines.reshape(4096, 128))
-    lines = lax.all_to_all(lines.reshape(WIDE, 64, 128), "wide", 0, 0, tiled=True)
-    residual = residual_of(lines.reshape(2048, 128), incident[0], contrast, source)
 
     row_position = (wide * 128 + jnp.arange(128, dtype=jnp.int32)).astype(f32) - N // 2 + 0.5
     block_position = (narrow * 1024 + 32 * jnp.arange(32, dtype=jnp.int32)).astype(f32) - N // 2 + 0.5
@@ -584,7 +599,23 @@
     ea = phase_pair(block_position, sine)
     eb = phase_pair(cell_position, sine)
     partial_value = project(source, ea, eb, rows)
-    total = sum_everywhere(partial_value)[:2]
+    lines, partial_value = lax.optimization_barrier((lines, partial_value))
+    lines = x_forward(lines.reshape(2048, 128))
+    lines = lax.all_to_all(lines.reshape(128, 32, 128), ("wide", "narrow"), 0, 0, tiled=True)
+
+    total = sum_over(partial_value, [("wide", WIDE, (1, 2, 3)), ("wide", WIDE, (8, 16, 24))])
+    total, far, near_partner = lax.optimization_barrier((total, far, near_partner))
+    total = sum_over(total, [("narrow", NARROW, (1,))])
+    greens = [near[0], near_partner, far, partner(far[1], 1)]
+    total, lines = lax.optimization_barrier((total, lines))
+    lines = middle(lines.reshape(4096, 128), greens, place)
+    total, lines = lax.optimization_barrier((total, lines))
+    lines = lax.all_to_all(lines.reshape(128, 32, 128), ("wide", "narrow"), 0, 0, tiled=True)
+    total = sum_over(total, [("wide", WIDE, (4,)), ("narrow", NARROW, (2,))])[:2]
+    lines = x_inverse(lines.reshape(4096, 128))
+    lines = lax.all_to_all(lines.reshape(WIDE, 64, 128), "wide", 0, 0, tiled=True)
+    residual = residual_of(lines.reshape(2048, 128), incident[0], contrast, source)
+
     data_residual = measured - total[None] * (1.0 / N)
     rho_real = data_residual[0, 0][None, :]
     rho_imag = data_residual[0, 1][None, :]

time: 234 us -> 189 us (0.81)
  blocking collectives: 25.9 us -> 0 us
  waiting for transfers between devices: 80.3 us -> 61.6 us
  Pallas kernels: 74 us -> 56.4 us
  starting transfers between devices: 38.6 us -> 51.8 us
  local copies, waits for them, and re-layouts: 3.77 us -> 8.87 us
    ppermute x3, waiting for transfers between devices: 61.1 us -> 12.3 us  [partner(): return lax.ppermute(value, 'narrow', [(j, j ^ k) for j in range(NARROW)])]
    all_to_all x1 -> x0, blocking collectives: 25.9 us -> none  [local(): lax.all_to_all(lines.reshape(WIDE, 64, 128), 'wide', 0, 0, tiled=True)]
    ppermute x9, waiting for transfers between devices: 16.1 us -> 31.6 us  [exchange(): lax.ppermute(value, axis, [(j, j ^ stride) for j in range(size)])]
    all_to_all x2, waiting for transfers between devices: 0.01 us -> 11.6 us  [local(): lax.all_to_all(lines.reshape(128, 32, 128), ('wide', 'narrow'), 0, 0, til...]
    ppermute x9, starting transfers between devices: 13 us -> 20.9 us  [exchange(): lax.ppermute(value, axis, [(j, j ^ stride) for j in range(size)])]
    all_to_all x1 -> x2, starting transfers between devices: 7.15 us -> 14.4 us  [local(): lax.all_to_all(lines.reshape(WIDE, 64, 128), 'wide', 0, 0, tiled=True)]
    pallas_call x1, Pallas kernels: 22.1 us -> 16.9 us  [middle(): pl.pallas_call(middle_kernel, in_specs=[pl.BlockSpec(memory_space=pltpu.S...]
    squeeze x0 -> x2, local copies, waits for them, and re-layouts: none -> 4.53 us  [local(): greens = [near[0], near_partner, far, partner(far[1], 1)]]
  transfers between devices with their start and end apart: 15 -> 16, of which waited for: 8 -> 10; matrix products, arithmetic and copies ran while one was open for 4% -> 7% of each run, Pallas kernels for 12% -> 16%
where the time goes in v2:
time: 189 us; the launch traced here: 188 us
  waiting for transfers between devices  61.6 us (33%)
  Pallas kernels  56.4 us (30%)
  starting transfers between devices  51.8 us (27%)
  local copies, waits for them, and re-layouts  8.87 us (5%)
  other arithmetic  8.67 us (5%)
    ppermute x9, waiting for transfers between devices, exchange(): lax.ppermute(value, axis, [(j, j ^ stride) for j in range(size)])  31.6 us
    ppermute x9, starting transfers between devices, exchange(): lax.ppermute(value, axis, [(j, j ^ stride) for j in range(size)])  20.9 us
    pallas_call x1, Pallas kernels, middle(): pl.pallas_call(middle_kernel, in_specs=[pl.BlockSpec(memory_space=pltpu.S...  16.9 us
    all_to_all x2, starting transfers between devices, local(): lax.all_to_all(lines.reshape(WIDE, 64, 128), 'wide', 0, 0, tiled=True)  14.4 us
    all_to_all x2, starting transfers between devices, local(): lax.all_to_all(lines.reshape(128, 32, 128), ('wide', 'narrow'), 0, 0, til...  13.5 us
    ppermute x3, waiting for transfers between devices, partner(): return lax.ppermute(value, 'narrow', [(j, j ^ k) for j in range(NARROW)])  12.3 us
    all_to_all x2, waiting for transfers between devices, local(): lax.all_to_all(lines.reshape(128, 32, 128), ('wide', 'narrow'), 0, 0, til...  11.6 us
    pallas_call x1, Pallas kernels, x_forward(): pl.pallas_call(x_forward_kernel, in_specs=[spec_vmem()] * 4, out_specs=sp...  7.36 us
  transfers between devices with their start and end apart: 16, of which 10 were waited for; matrix products, arithmetic and copies ran while one was open for 7% of the time, Pallas kernels for 16%

profile of v2, /device:TPU:0, one launch (start us, length us, event | category | flops | bytes accessed | tf_op | source)
XLA Modules:
  0.0 188.2 jit_solution(1292382951378016632)
XLA Ops:
  1.2 3.4 %pack_far.1 = f32[2,2,1024,128]{3,2,1,0:T(8,128)} custom-call(s32[2]{0:T(128)} %pad_add_fusion.place_ref, f32[2,2,1024,256]{3,2,1,0:T(8,128)} %bitcast.28), custom_call_target="tpu_custom_call" | custom-call | bytes 6291456 | tf_op jit(solution)/shard_map/pack_far/pallas_call | solution.py:444
  6.9 9.3 %all-to-all-start = ((f32[32,64,128]{2,1,0:T(8,128)}), f32[32,64,128]{2,1,0:T(8,128)S(1)}, u32[]{:S(2)}, u32[]{:S(2)}) async-start(f32[32,64,128]{2,1,0:T(8,128)} %bitcast.34), calls=%async_computation | async-start | bytes 2097152 | tf_op jit(solution)/shard_map/all_to_all | solution.py:592
  16.2 3.5 %pack_near.1 = f32[2,2,1024,128]{3,2,1,0:T(8,128)} custom-call(s32[2]{0:T(128)} %pad_add_fusion.place_ref, f32[2,2,1024,256]{3,2,1,0:T(8,128)} %bitcast.29), custom_call_target="tpu_custom_call" | custom-call | bytes 6291456 | tf_op jit(solution)/shard_map/pack_near/pallas_call | solution.py:444
  19.7 3.2 %slice_bitcast_fusion = (f32[2,1024,128]{2,1,0:T(8,128)}, f32[2,1024,128]{2,1,0:T(8,128)}) fusion(f32[2,2,1024,128]{3,2,1,0:T(8,128)} %pack_near.1), kind=kLoop, calls=%fused_computation | loop fusion | bytes 4194304 | tf_op jit(solution)/shard_map/squeeze | solution.py:609
  22.9 2.9 %collective-permute-start.6 = (f32[2,2,1024,128]{3,2,1,0:T(8,128)S(1)}, f32[2,2,1024,128]{3,2,1,0:T(8,128)}, u32[]{:S(2)}, u32[]{:S(2)}) collective-permute-start(f32[2,2,1024,128]{3,2,1,0:T(8,128)S(1)} %copy-done.1), channel_id=1, source_target_pairs={{0,2},{1,3},{2,0},{3,1},{4,6},{5,7},{6,4},{7,5},{8,10},{9,11},{10,... | collective-permute-start | bytes 6291464 | tf_op jit(solution)/shard_map/ppermute | solution.py:584
  30.8 6.9 %project.1 = f32[8,1024]{1,0:T(8,128)} custom-call(f32[2,128,1024]{2,1,0:T(8,128)} %bitcast.31, f32[2,32,1024]{2,1,0:T(8,128)} %get-tuple-element.43.ea_ref, f32[2,32,1024]{2,1,0:T(8,128)} %get-tuple-element.44.eb_ref, f32[2,128,1024]{2,1,0:T(8,128)} %pad_maximum_fusion.row_ref), custom_call_target="tpu_custom_call" | custom-call | flops 3221225472 | bytes 4194304 | tf_op jit(solution)/shard_map/project/pallas_call | solution.py:493
  38.7 7.4 %x_forward.1 = f32[4096,128]{1,0:T(8,128)} custom-call(f32[2048,128]{1,0:T(8,128)} %bitcast.40, bf16[128,192]{1,0:T(8,128)(2,1)} %constant.77.clone.t1_ref, f32[2,64,128]{2,1,0:T(8,128)} %constant.78.clone.tw_ref, bf16[2,256,256]{2,1,0:T(8,128)(2,1)} %constant.79.clone.t2_ref), custom_call_target="tpu_custom_call" | custom-call | flops 1073741824 | bytes 4194304 | tf_op jit(solution)/shard_map/x_forward/pallas_call | solution.py:210
  46.1 8.9 %all-to-all-start.1 = ((f32[128,32,128]{2,1,0:T(8,128)}), f32[128,32,128]{2,1,0:T(8,128)}, u32[]{:S(2)}, u32[]{:S(2)}) async-start(f32[128,32,128]{2,1,0:T(8,128)} %bitcast.35), calls=%async_computation.1 | async-start | bytes 4194304 | tf_op jit(solution)/shard_map/all_to_all | solution.py:604
  55.0 2.8 %collective-permute-start.2 = (f32[8,1024]{1,0:T(8,128)S(1)}, f32[8,1024]{1,0:T(8,128)S(1)}, u32[]{:S(2)}, u32[]{:S(2)}) collective-permute-start(f32[8,1024]{1,0:T(8,128)S(1)} %copy-done.4), channel_id=1, source_target_pairs={{0,12},{4,8},{8,4},{12,0},{16,28},{20,24},{24,20},{28,16},{32,44},... | collective-permute-start | bytes 98312 | tf_op jit(solution)/shard_map/ppermute | solution.py:566
  59.1 2.8 %collective-permute-done.2 = f32[8,1024]{1,0:T(8,128)S(1)} collective-permute-done((f32[8,1024]{1,0:T(8,128)S(1)}, f32[8,1024]{1,0:T(8,128)S(1)}, u32[]{:S(2)}, u32[]{:S(2)}) %collective-permute-start.2) | collective-permute-done | bytes 32800 | tf_op jit(solution)/shard_map/ppermute | solution.py:566
  62.0 4.6 %collective-permute-done.1 = f32[8,1024]{1,0:T(8,128)S(1)} collective-permute-done((f32[8,1024]{1,0:T(8,128)S(1)}, f32[8,1024]{1,0:T(8,128)S(1)}, u32[]{:S(2)}, u32[]{:S(2)}) %collective-permute-start.1) | collective-permute-done | bytes 32800 | tf_op jit(solution)/shard_map/ppermute | solution.py:566
  66.6 10.1 %collective-permute-start.5 = (f32[8,1024]{1,0:T(8,128)S(1)}, f32[8,1024]{1,0:T(8,128)S(1)}, u32[]{:S(2)}, u32[]{:S(2)}) collective-permute-start(f32[8,1024]{1,0:T(8,128)S(1)} %add_add_fusion.1), channel_id=1, source_target_pairs={{0,96},{4,100},{8,104},{12,108},{16,112},{20,116},{24,120},{28,124... | collective-permute-start | bytes 98312 | tf_op jit(solution)/shard_map/ppermute | solution.py:566
  82.2 12.3 %collective-permute-done.6.r2_ref = f32[2,2,1024,128]{3,2,1,0:T(8,128)} collective-permute-done((f32[2,2,1024,128]{3,2,1,0:T(8,128)S(1)}, f32[2,2,1024,128]{3,2,1,0:T(8,128)}, u32[]{:S(2)}, u32[]{:S(2)}) %collective-permute-start.6) | collective-permute-done | bytes 2097184 | tf_op jit(solution)/shard_map/ppermute | solution.py:584
  98.5 4.5 %all-to-all-done.1 = f32[128,32,128]{2,1,0:T(8,128)} async-done(((f32[128,32,128]{2,1,0:T(8,128)}), f32[128,32,128]{2,1,0:T(8,128)}, u32[]{:S(2)}, u32[]{:S(2)}) %all-to-all-start.1) | async-done | bytes 2097184 | tf_op jit(solution)/shard_map/all_to_all | solution.py:604
  104.0 16.9 %middle.1 = f32[4096,128]{1,0:T(8,128)} custom-call(s32[2]{0:T(128)} %pad_add_fusion.place_ref, f32[4096,128]{1,0:T(8,128)} %bitcast.9.a_ref, f32[2,1024,128]{2,1,0:T(8,128)} %get-tuple-element.27.r0_ref, f32[2,1024,128]{2,1,0:T(8,128)} %collective-permute-done.7.r1_ref, f32[2,2,1024,128]{3,2,1,0:T(8,128)} %collective-permute-done.6.r2_ref, ...), custom_call_target="tpu_custom_call" | custom-call | flops 3221225472 | bytes 10485760 | tf_op jit(solution)/shard_map/middle/pallas_call | solution.py:330
  121.0 4.7 %all-to-all-start.2 = ((f32[128,32,128]{2,1,0:T(8,128)}), f32[128,32,128]{2,1,0:T(8,128)S(1)}, u32[]{:S(2)}, u32[]{:S(2)}) async-start(f32[128,32,128]{2,1,0:T(8,128)} %bitcast.36), calls=%async_computation.2 | async-start | bytes 4194304 | tf_op jit(solution)/shard_map/all_to_all | solution.py:613
  126.6 17.5 %collective-permute-done.10 = f32[8,1024]{1,0:T(8,128)S(1)} collective-permute-done((f32[8,1024]{1,0:T(8,128)S(1)}, f32[8,1024]{1,0:T(8,128)S(1)}, u32[]{:S(2)}, u32[]{:S(2)}) %collective-permute-start.10) | collective-permute-done | bytes 32800 | tf_op jit(solution)/shard_map/ppermute | solution.py:566
  144.1 4.2 %collective-permute-start.11 = (f32[8,1024]{1,0:T(8,128)S(1)}, f32[8,1024]{1,0:T(8,128)S(1)}, u32[]{:S(2)}, u32[]{:S(2)}) collective-permute-start(f32[8,1024]{1,0:T(8,128)S(1)} %add.106), channel_id=1, source_target_pairs={{0,2},{1,3},{2,0},{3,1},{4,6},{5,7},{6,4},{7,5},{8,10},{9,11},{10,... | collective-permute-start | bytes 98312 | tf_op jit(solution)/shard_map/ppermute | solution.py:566
  148.3 7.0 %all-to-all-done.2 = f32[128,32,128]{2,1,0:T(8,128)S(1)} async-done(((f32[128,32,128]{2,1,0:T(8,128)}), f32[128,32,128]{2,1,0:T(8,128)S(1)}, u32[]{:S(2)}, u32[]{:S(2)}) %all-to-all-start.2) | async-done | bytes 2097184 | tf_op jit(solution)/shard_map/all_to_all | solution.py:613
  156.7 5.9 %x_inverse.1 = f32[2048,128]{1,0:T(8,128)} custom-call(f32[4096,128]{1,0:T(8,128)} %bitcast.37, bf16[2,256,256]{2,1,0:T(8,128)(2,1)} %constant.85.clone.t5_ref, f32[2,128,128]{2,1,0:T(8,128)} %constant.86.clone.tw_ref, bf16[2,128,256]{2,1,0:T(8,128)(2,1)} %constant.87.clone.t6_ref), custom_call_target="tpu_custom_call" | custom-call | flops 1073741824 | bytes 4194304 | tf_op jit(solution)/shard_map/x_inverse/pallas_call | solution.py:383
  162.6 5.1 %all-to-all-start.3 = ((f32[32,64,128]{2,1,0:T(8,128)}), f32[32,64,128]{2,1,0:T(8,128)S(1)}, u32[]{:S(2)}, u32[]{:S(2)}) async-start(f32[32,64,128]{2,1,0:T(8,128)} %bitcast.41), calls=%async_computation.3 | async-start | bytes 2097152 | tf_op jit(solution)/shard_map/all_to_all | solution.py:616
  171.0 6.9 %backproject.1 = f32[2,128,1024]{2,1,0:T(8,128)} custom-call(f32[2,128,1024]{2,1,0:T(8,128)} %pad_maximum_fusion.1.weight_ref, f32[2,32,1024]{2,1,0:T(8,128)} %get-tuple-element.43.ea_ref, f32[2,32,1024]{2,1,0:T(8,128)} %get-tuple-element.44.eb_ref), custom_call_target="tpu_custom_call" | custom-call | flops 3221225472 | bytes 4194304 | tf_op jit(solution)/shard_map/backproject/pallas_call | solution.py:541
  177.9 6.2 %all-to-all-done.3 = f32[32,64,128]{2,1,0:T(8,128)S(1)} async-done(((f32[32,64,128]{2,1,0:T(8,128)}), f32[32,64,128]{2,1,0:T(8,128)S(1)}, u32[]{:S(2)}, u32[]{:S(2)}) %all-to-all-start.3) | async-done | bytes 1048608 | tf_op jit(solution)/shard_map/all_to_all | solution.py:616
  185.1 3.2 %residual.1 = f32[2,128,1024]{2,1,0:T(8,128)} custom-call(f32[2048,128]{1,0:T(8,128)} %bitcast.33, f32[2,128,1024]{2,1,0:T(8,128)} %bitcast.38, f32[2,128,1024]{2,1,0:T(8,128)} %contrast_ref.1, f32[2,128,1024]{2,1,0:T(8,128)} %bitcast.32), custom_call_target="tpu_custom_call" | custom-call | bytes 5242880 | tf_op jit(solution)/shard_map/residual/pallas_call | solution.py:412
  (54 shorter events, 27.1 us)
Async XLA Ops:
  6.9 30.8 %all-to-all-start = ((f32[32,64,128]{2,1,0:T(8,128)}), f32[32,64,128]{2,1,0:T(8,128)S(1)}, u32[]{:S(2)}, u32[]{:S(2)}) async-start(f32[32,64,128]{2,1,0:T(8,128)} %bitcast.34), calls=%async_computation | async-start | bytes 2097152 | tf_op jit(solution)/shard_map/all_to_all | solution.py:592
  19.7 3.3 %copy-start.1 = (f32[2,2,1024,128]{3,2,1,0:T(8,128)S(1)}, f32[2,2,1024,128]{3,2,1,0:T(8,128)}, u32[]{:S(2)}) copy-start(f32[2,2,1024,128]{3,2,1,0:T(8,128)} %pack_far.1) | copy-start | bytes 6291460
  19.7 6.2 %copy-start.7 = (f32[1024]{0:T(1024)S(1)}, f32[1024]{0:T(1024)}, u32[]{:S(2)}) copy-start(f32[1024]{0:T(1024)} %param.21) | copy-start | bytes 12292
  22.9 59.2 %collective-permute-start.7 = (f32[2,1024,128]{2,1,0:T(8,128)}, f32[2,1024,128]{2,1,0:T(8,128)}, u32[]{:S(2)}, u32[]{:S(2)}) collective-permute-start(f32[2,1024,128]{2,1,0:T(8,128)} %get-tuple-element.28), channel_id=1, source_target_pairs={{0,1},{1,0},{2,3},{3,2},{4,5},{5,4},{6,7},{7,6},{8,9},{9,8},{10,11... | collective-permute-start | bytes 3145736 | tf_op jit(solution)/shard_map/ppermute | solution.py:584
  22.9 71.5 %collective-permute-start.6 = (f32[2,2,1024,128]{3,2,1,0:T(8,128)S(1)}, f32[2,2,1024,128]{3,2,1,0:T(8,128)}, u32[]{:S(2)}, u32[]{:S(2)}) collective-permute-start(f32[2,2,1024,128]{3,2,1,0:T(8,128)S(1)} %copy-done.1), channel_id=1, source_target_pairs={{0,2},{1,3},{2,0},{3,1},{4,6},{5,7},{6,4},{7,5},{8,10},{9,11},{10,... | collective-permute-start | bytes 6291464 | tf_op jit(solution)/shard_map/ppermute | solution.py:584
  46.1 8.9 %copy-start.4 = (f32[8,1024]{1,0:T(8,128)S(1)}, f32[8,1024]{1,0:T(8,128)}, u32[]{:S(2)}) copy-start(f32[8,1024]{1,0:T(8,128)} %project.1) | copy-start | bytes 98308
  46.1 57.0 %all-to-all-start.1 = ((f32[128,32,128]{2,1,0:T(8,128)}), f32[128,32,128]{2,1,0:T(8,128)}, u32[]{:S(2)}, u32[]{:S(2)}) async-start(f32[128,32,128]{2,1,0:T(8,128)} %bitcast.35), calls=%async_computation.1 | async-start | bytes 4194304 | tf_op jit(solution)/shard_map/all_to_all | solution.py:604
  55.0 7.0 %collective-permute-start.2 = (f32[8,1024]{1,0:T(8,128)S(1)}, f32[8,1024]{1,0:T(8,128)S(1)}, u32[]{:S(2)}, u32[]{:S(2)}) collective-permute-start(f32[8,1024]{1,0:T(8,128)S(1)} %copy-done.4), channel_id=1, source_target_pairs={{0,12},{4,8},{8,4},{12,0},{16,28},{20,24},{24,20},{28,16},{32,44},... | collective-permute-start | bytes 98312 | tf_op jit(solution)/shard_map/ppermute | solution.py:566
  57.8 8.8 %collective-permute-start.1 = (f32[8,1024]{1,0:T(8,128)S(1)}, f32[8,1024]{1,0:T(8,128)S(1)}, u32[]{:S(2)}, u32[]{:S(2)}) collective-permute-start(f32[8,1024]{1,0:T(8,128)S(1)} %copy-done.4), channel_id=1, source_target_pairs={{0,8},{4,12},{8,0},{12,4},{16,24},{20,28},{24,16},{28,20},{32,40},... | collective-permute-start | bytes 98312 | tf_op jit(solution)/shard_map/ppermute | solution.py:566
  58.1 8.5 %collective-permute-start = (f32[8,1024]{1,0:T(8,128)S(1)}, f32[8,1024]{1,0:T(8,128)S(1)}, u32[]{:S(2)}, u32[]{:S(2)}) collective-permute-start(f32[8,1024]{1,0:T(8,128)S(1)} %copy-done.4), channel_id=1, source_target_pairs={{0,4},{4,0},{8,12},{12,8},{16,20},{20,16},{24,28},{28,24},{32,36},... | collective-permute-start | bytes 98312 | tf_op jit(solution)/shard_map/ppermute | solution.py:566
  66.6 13.5 %collective-permute-start.5 = (f32[8,1024]{1,0:T(8,128)S(1)}, f32[8,1024]{1,0:T(8,128)S(1)}, u32[]{:S(2)}, u32[]{:S(2)}) collective-permute-start(f32[8,1024]{1,0:T(8,128)S(1)} %add_add_fusion.1), channel_id=1, source_target_pairs={{0,96},{4,100},{8,104},{12,108},{16,112},{20,116},{24,120},{28,124... | collective-permute-start | bytes 98312 | tf_op jit(solution)/shard_map/ppermute | solution.py:566
  76.7 5.4 %collective-permute-start.4 = (f32[8,1024]{1,0:T(8,128)S(1)}, f32[8,1024]{1,0:T(8,128)S(1)}, u32[]{:S(2)}, u32[]{:S(2)}) collective-permute-start(f32[8,1024]{1,0:T(8,128)S(1)} %add_add_fusion.1), channel_id=1, source_target_pairs={{0,64},{4,68},{8,72},{12,76},{16,80},{20,84},{24,88},{28,92},{32,9... | collective-permute-start | bytes 98312 | tf_op jit(solution)/shard_map/ppermute | solution.py:566
  77.7 4.4 %collective-permute-start.3 = (f32[8,1024]{1,0:T(8,128)S(1)}, f32[8,1024]{1,0:T(8,128)S(1)}, u32[]{:S(2)}, u32[]{:S(2)}) collective-permute-start(f32[8,1024]{1,0:T(8,128)S(1)} %add_add_fusion.1), channel_id=1, source_target_pairs={{0,32},{4,36},{8,40},{12,44},{16,48},{20,52},{24,56},{28,60},{32,0... | collective-permute-start | bytes 98312 | tf_op jit(solution)/shard_map/ppermute | solution.py:566
  95.8 7.3 %collective-permute-start.9 = (f32[2,1024,128]{2,1,0:T(8,128)S(1)}, f32[2,1024,128]{2,1,0:T(8,128)S(1)}, u32[]{:S(2)}, u32[]{:S(2)}) collective-permute-start(f32[2,1024,128]{2,1,0:T(8,128)S(1)} %slice_bitcast_fusion.2), channel_id=1, source_target_pairs={{0,1},{1,0},{2,3},{3,2},{4,5},{5,4},{6,7},{7,6},{8,9},{9,8},{10,11... | collective-permute-start | bytes 3145736 | tf_op jit(solution)/shard_map/ppermute | solution.py:584
  95.9 2.7 %collective-permute-start.8 = (f32[8,1024]{1,0:T(8,128)S(1)}, f32[8,1024]{1,0:T(8,128)S(1)}, u32[]{:S(2)}, u32[]{:S(2)}) collective-permute-start(f32[8,1024]{1,0:T(8,128)S(1)} %add_add_fusion), channel_id=1, source_target_pairs={{0,1},{1,0},{2,3},{3,2},{4,5},{5,4},{6,7},{7,6},{8,9},{9,8},{10,11... | collective-permute-start | bytes 98312 | tf_op jit(solution)/shard_map/ppermute | solution.py:566
  103.1 1.0 copy-start.8
  121.0 34.4 %all-to-all-start.2 = ((f32[128,32,128]{2,1,0:T(8,128)}), f32[128,32,128]{2,1,0:T(8,128)S(1)}, u32[]{:S(2)}, u32[]{:S(2)}) async-start(f32[128,32,128]{2,1,0:T(8,128)} %bitcast.36), calls=%async_computation.2 | async-start | bytes 4194304 | tf_op jit(solution)/shard_map/all_to_all | solution.py:613
  125.6 18.4 %collective-permute-start.10 = (f32[8,1024]{1,0:T(8,128)S(1)}, f32[8,1024]{1,0:T(8,128)S(1)}, u32[]{:S(2)}, u32[]{:S(2)}) collective-permute-start(f32[8,1024]{1,0:T(8,128)S(1)} %add.105), channel_id=1, source_target_pairs={{0,16},{4,20},{8,24},{12,28},{16,0},{20,4},{24,8},{28,12},{32,48},... | collective-permute-start | bytes 98312 | tf_op jit(solution)/shard_map/ppermute | solution.py:566
  144.1 23.7 %collective-permute-start.11 = (f32[8,1024]{1,0:T(8,128)S(1)}, f32[8,1024]{1,0:T(8,128)S(1)}, u32[]{:S(2)}, u32[]{:S(2)}) collective-permute-start(f32[8,1024]{1,0:T(8,128)S(1)} %add.106), channel_id=1, source_target_pairs={{0,2},{1,3},{2,0},{3,1},{4,6},{5,7},{6,4},{7,5},{8,10},{9,11},{10,... | collective-permute-start | bytes 98312 | tf_op jit(solution)/shard_map/ppermute | solution.py:566
  155.4 1.3 copy-start.2
  156.7 11.1 %copy-start.6 = (f32[1,2,1024]{2,1,0:T(2,128)S(1)}, f32[1,2,1024]{2,1,0:T(2,128)}, u32[]{:S(2)}) copy-start(f32[1,2,1024]{2,1,0:T(2,128)} %param.22) | copy-start | bytes 24580
  162.6 21.4 %all-to-all-start.3 = ((f32[32,64,128]{2,1,0:T(8,128)}), f32[32,64,128]{2,1,0:T(8,128)S(1)}, u32[]{:S(2)}, u32[]{:S(2)}) async-start(f32[32,64,128]{2,1,0:T(8,128)} %bitcast.41), calls=%async_computation.3 | async-start | bytes 2097152 | tf_op jit(solution)/shard_map/all_to_all | solution.py:616
  167.8 10.1 %copy-start.5 = (f32[1,2,1024]{2,1,0:T(2,128)}, f32[1,2,1024]{2,1,0:T(2,128)S(1)}, u32[]{:S(2)}) copy-start(f32[1,2,1024]{2,1,0:T(2,128)S(1)} %fusion.5) | copy-start | bytes 24580
  184.1 1.0 copy-start
  (1 other events, 1.0 us)

commit v3 on v2

--- a/solution.py
+++ b/solution.py
@@ -19,17 +19,16 @@
 wave_step = 0.2 * math.pi
 f32 = jnp.float32
 bf16 = jnp.bfloat16
-VMEM_LIMIT = 56 * 1024 * 1024
 
 
 def complex_block(table):
     return np.block([[table.real, -table.imag], [table.imag, table.real]])
 
 
-def halves(table):
+def terms(table):
     high = table.astype(np.float32).astype(ml_dtypes.bfloat16)
     low = (table - high.astype(np.float64)).astype(np.float32).astype(ml_dtypes.bfloat16)
-    return high, low
+    return np.concatenate([high, high, low], 1)
 
 
 def root(product, length, sign):
@@ -47,25 +46,25 @@
     k1 = np.arange(64)
     i = np.arange(128)
     m = np.arange(128)
-    high, low = halves(complex_block(root(np.outer(k1, w), 64, -1)))
-    out["t1"] = np.concatenate([high, high, low], 1)
+    out["t1"] = terms(complex_block(root(np.outer(k1, w), 64, -1)))
     out["tw1"] = pair(root(np.outer(k1, i), M, -1))
-    out["t2"] = np.stack(halves(complex_block(root(np.outer(m, i), 128, -1))))
+    out["t2"] = terms(complex_block(root(np.outer(m, i), 128, -1)))
     d = np.arange(128)
     s = 32 * (d % 4) + d // 4
     c1 = np.arange(256)
-    out["t3"] = np.stack(halves(complex_block(root(np.outer(c1, s), 256, -1))))
+    out["t3"] = terms(complex_block(root(np.outer(c1, s), 256, -1)))
     low_half = np.arange(128) < 64
     first = np.where(low_half[None, :], 1.0, root(c1, M, -1)[:, None])
     out["tw3"] = pair(first)
     out["step3"] = pair(root(2 * c1, M, -1)[:, None] * np.ones((1, 128)))
     lanes = []
     for flip in (0, 1):
-        e = (np.arange(16) + 8 * flip) % 16
-        lanes.append(pair(np.where(low_half[None, :], 1.0, root(e, 32, -1)[:, None])))
+        first_e = (np.array([0, 1, 2, 3, 8, 9, 10, 11]) + 8 * flip) % 16
+        e = np.where(low_half[None, :], first_e[:, None], first_e[:, None] + 4)
+        lanes.append(pair(root(e, 32, -1)))
     out["lane3"] = np.stack(lanes)
-    out["t4"] = np.stack(halves(complex_block(root(np.outer(s, c1), 256, 1))))
-    out["t5"] = np.stack(halves(complex_block(root(np.outer(i, m), 128, 1))))
+    out["t4"] = terms(complex_block(root(np.outer(s, c1), 256, 1)))
+    out["t5"] = terms(complex_block(root(np.outer(i, m), 128, 1)))
     lane_k1 = np.arange(128) % 64
     out["tw5"] = pair(root(np.outer(i, lane_k1), M, 1))
     inner = root(np.outer(w, k1), 64, 1) / (M * M)
@@ -75,7 +74,7 @@
         block[b0, 0, :, 1, b0, :] = -inner.imag
         block[b0, 1, :, 0, b0, :] = inner.imag
         block[b0, 1, :, 1, b0, :] = inner.real
-    out["t6"] = np.stack(halves(block.reshape(128, 256)))
+    out["t6"] = terms(block.reshape(128, 256))
     return out
 
 
@@ -93,9 +92,14 @@
     return lax.dot_general(a, b, (((1,), (1,)), ((), ())), preferred_element_type=f32)
 
 
-def dot3(table_high, table_low, values, product):
+def dot3(table, values):
     high, low = split(values)
-    return product(table_high, high) + (product(table_high, low) + product(table_low, high))
+    return dot(table, jnp.concatenate([high, low, high], 0))
+
+
+def dot3_nt(table, values):
+    high, low = split(values)
+    return dot_nt(table, jnp.concatenate([high, low, high], 1))
 
 
 def times_root(value, numerator, length):
@@ -151,8 +155,26 @@
     return pl.BlockSpec(memory_space=pltpu.VMEM)
 
 
-def params():
-    return pltpu.CompilerParams(vmem_limit_bytes=VMEM_LIMIT)
+def spec_hbm():
+    return pl.BlockSpec(memory_space=pltpu.HBM)
+
+
+def in_hbm(*values):
+    return [pltpu.with_memory_space_constraint(jnp.asarray(value), pltpu.HBM) for value in values]
+
+
+def fetch(sources, targets, arrived):
+    copies = [
+        pltpu.make_async_copy(source, target, arrived.at[k])
+        for k, (source, target) in enumerate(zip(sources, targets))
+    ]
+    for copy in copies:
+        copy.start()
+    return copies
+
+
+def params(mebibytes=16):
+    return pltpu.CompilerParams(vmem_limit_bytes=mebibytes << 20)
 
 
 def cost(flops, bytes_accessed):
@@ -174,13 +196,18 @@
         grid=(2,),
         in_specs=[pl.BlockSpec((2, 128, 512), lambda t: (0, 0, t))],
         out_specs=pl.BlockSpec((1024, 128), lambda t: (t, 0)),
-        out_shape=jax.ShapeDtypeStruct((2048, 128), f32),
+        out_shape=pltpu.HBM((2048, 128), f32),
         cost_estimate=cost(0, 2 << 20),
         name="columns_major",
     )(source)
 
 
-def x_forward_kernel(a_ref, t1_ref, tw_ref, t2_ref, out_ref):
+def x_forward_kernel(
+    a_ref, t1_hbm, tw_hbm, t2_hbm, out_hbm, t1_ref, tw_ref, t2_ref, out_ref, arrived, sent
+):
+    for copy in fetch((t1_hbm, tw_hbm, t2_hbm), (t1_ref, tw_ref, t2_ref), arrived):
+        copy.wait()
+
     @pl.loop(0, 16, unroll=8)
     def _(c):
         columns = []
@@ -188,8 +215,7 @@
             re = a_ref[pl.ds(2 * c + b0, 32, stride=64), :]
             im = a_ref[pl.ds(2 * c + b0 + 32, 32, stride=64), :]
             columns.append(jnp.concatenate([re, im], 0))
-        high, low = split(jnp.concatenate(columns, 1))
-        u = dot(t1_ref[...], jnp.concatenate([high, low, high], 0))
+        u = dot3(t1_ref[...], jnp.concatenate(columns, 1))
         rows = []
         for b0 in range(2):
             ur = u[:64, 128 * b0 : 128 * b0 + 128]
@@ -200,37 +226,52 @@
                 )
             )
         z = jnp.concatenate(rows, 0)
-        out = dot3(t2_ref[0], t2_ref[1], z, dot_nt)
+        out = dot3_nt(t2_ref[...], z)
         out_ref[pl.ds(c, 128, stride=32), :] = out[:128]
         out_ref[pl.ds(c + 16, 128, stride=32), :] = out[128:]
+
+    last = pltpu.make_async_copy(out_ref, out_hbm, sent)
+    last.start()
+    last.wait()
 
 
 def x_forward(a):
     t = tables()
     return pl.pallas_call(
         x_forward_kernel,
-        in_specs=[spec_vmem()] * 4,
-        out_specs=spec_vmem(),
-        out_shape=jax.ShapeDtypeStruct((4096, 128), f32),
-        compiler_params=params(),
+        in_specs=[spec_vmem()] + [spec_hbm()] * 3,
+        out_specs=spec_hbm(),
+        out_shape=pltpu.HBM((4096, 128), f32),
+        scratch_shapes=[
+            pltpu.VMEM((128, 192), bf16),
+            pltpu.VMEM((2, 64, 128), f32),
+            pltpu.VMEM((256, 768), bf16),
+            pltpu.VMEM((4096, 128), f32),
+            pltpu.SemaphoreType.DMA((3,)),
+            pltpu.SemaphoreType.DMA,
+        ],
+        compiler_params=params(8),
         cost_estimate=cost(2 * 2048 * 65536 * 4, 4 << 20),
         name="x_forward",
-    )(a, jnp.asarray(t["t1"]), jnp.asarray(t["tw1"]), jnp.asarray(t["t2"]))
+    )(a, *in_hbm(t["t1"], t["tw1"], t["t2"]))
 
 
 def middle_kernel(
-    place_ref, a_ref, r0_ref, r1_ref, r2_ref, r3_ref, t3_ref, tw_ref, step_ref, lane_ref, t4_ref,
-    out_ref, u_ref, now_ref, green_ref, late_ref, arrived,
+    place_ref, a_ref, t3_hbm, tw_hbm, step_hbm, r0_hbm, r1_hbm, r2_hbm, r3_hbm, lane_hbm, t4_hbm,
+    out_hbm, t3_ref, tw_ref, step_ref, green_ref, lane_ref, t4_ref, u_ref, now_ref, out_ref,
+    arrived, sent,
 ):
-    copies = [
-        pltpu.make_async_copy(ref, green_ref.at[k], arrived.at[k])
-        for k, ref in enumerate((r0_ref, r1_ref, r2_ref.at[0], r3_ref))
-    ]
-    copies.append(pltpu.make_async_copy(t4_ref, late_ref, arrived.at[4]))
-    for copy in copies:
-        copy.start()
     flip = place_ref[0]
     upper = place_ref[1]
+    copies = fetch(
+        (t3_hbm, tw_hbm, step_hbm, r0_hbm, r1_hbm, r2_hbm.at[0], r3_hbm, lane_hbm, t4_hbm),
+        (t3_ref, tw_ref, step_ref)
+        + tuple(green_ref.at[g, h] for h in (upper, 1 - upper) for g in range(2))
+        + (lane_ref, t4_ref),
+        arrived,
+    )
+    for copy in copies[:3]:
+        copy.wait()
     sign = 1.0 - 2.0 * flip.astype(f32)
 
     def advance():
@@ -243,14 +284,14 @@
 
     now_ref[...] = tw_ref[...]
 
-    @pl.loop(0, 8, unroll=2)
+    @pl.loop(0, 8, unroll=8)
     def _(cc):
         columns = []
         for half in range(2):
             re = a_ref[pl.ds(2 * cc + half, 128, stride=32), :]
             im = a_ref[pl.ds(2 * cc + half + 16, 128, stride=32), :]
             columns.append(jnp.concatenate([re, im], 0))
-        u = dot3(t3_ref[0], t3_ref[1], jnp.concatenate(columns, 1), dot)
+        u = dot3(t3_ref[...], jnp.concatenate(columns, 1))
         for half in range(2):
             ur = u[:256, 128 * half : 128 * half + 128]
             ui = u[256:, 128 * half : 128 * half + 128]
@@ -260,55 +301,52 @@
             u_ref[2 * cc + half, 1] = ur * ni + ui * nr
             advance()
 
-    for copy in copies:
+    for copy in copies[3:]:
         copy.wait()
 
     lane = lax.broadcasted_iota(jnp.int32, (8, 128), 1)
     low = lane < 64
-    sgn = jnp.where(low, 1.0, -1.0).astype(f32)
-    mine = low == (upper == 0)
-
-    @pl.loop(0, 32, unroll=2)
+
+    def trade(first, second):
+        middle_part = pltpu.roll(jnp.where(low, second, first), 64, 1)
+        return jnp.where(low, first, middle_part), jnp.where(low, middle_part, second)
+
+    @pl.loop(0, 32, unroll=4)
     def _(tile):
         rows = pl.ds(pl.multiple_of(tile * 8, 8), 8)
         values = [(u_ref[c, 0, rows, :], u_ref[c, 1, rows, :]) for c in range(16)]
         spectrum = transform_list(values)
-        back = []
-        for e in range(16):
-            g, q, row_block = e // 8, (e // 4) % 2, e % 4
-            grows = pl.ds(pl.multiple_of(tile * 8 + row_block * 256, 8), 8)
-            green = []
-            for part in range(2):
-                own = green_ref[g, part, grows, :]
-                other = green_ref[g + 2, part, grows, :]
-                green.append(jnp.where(mine, own, other) if q == 0 else jnp.where(mine, other, own))
-            lr = lane_ref[flip, 0, e : e + 1, :]
-            li = lane_ref[flip, 1, e : e + 1, :]
-            sr, si = spectrum[e]
-            vr = sr * lr - si * li
-            vi = sr * li + si * lr
-            rr = pltpu.roll(vr, 64, 1)
-            ri = pltpu.roll(vi, 64, 1)
-            if q == 0:
-                fr, fi = sgn * vr + rr, sgn * vi + ri
-            else:
-                fr, fi = vr - sgn * rr, vi - sgn * ri
-            pr = green[0] * fr - green[1] * fi
-            pi_ = green[0] * fi + green[1] * fr
-            rr = pltpu.roll(pr, 64, 1)
-            ri = pltpu.roll(pi_, 64, 1)
-            if q == 0:
-                vr, vi = sgn * pr + rr, sgn * pi_ + ri
-            else:
-                vr, vi = pr + sgn * rr, pi_ + sgn * ri
-            back.append((vr * lr + vi * li, vi * lr - vr * li))
+        back = [None] * 16
+        for index in range(8):
+            g, r = index // 4, index % 4
+            e = 8 * g + r
+            grows = pl.ds(pl.multiple_of(tile * 8 + r * 256, 8), 8)
+            lr = lane_ref[flip, 0, index : index + 1, :]
+            li = lane_ref[flip, 1, index : index + 1, :]
+            even_r, odd_r = trade(spectrum[e][0], spectrum[e + 4][0])
+            even_i, odd_i = trade(spectrum[e][1], spectrum[e + 4][1])
+            odd_r, odd_i = odd_r * lr - odd_i * li, odd_r * li + odd_i * lr
+            products = []
+            for h, (fr, fi) in enumerate(
+                ((even_r + odd_r, even_i + odd_i), (even_r - odd_r, even_i - odd_i))
+            ):
+                gr = green_ref[g, h, 0, grows, :]
+                gi = green_ref[g, h, 1, grows, :]
+                products.append((gr * fr - gi * fi, gr * fi + gi * fr))
+            (ar, ai), (br, bi) = products
+            odd_r, odd_i = ar - br, ai - bi
+            odd_r, odd_i = odd_r * lr + odd_i * li, odd_i * lr - odd_r * li
+            first_r, second_r = trade(ar + br, odd_r)
+            first_i, second_i = trade(ai + bi, odd_i)
+            back[e] = (first_r, first_i)
+            back[e + 4] = (second_r, second_i)
         for c, (re, im) in enumerate(inverse_list(back)):
             u_ref[c, 0, rows, :] = re
             u_ref[c, 1, rows, :] = im
 
     now_ref[...] = tw_ref[...]
 
-    @pl.loop(0, 8, unroll=2)
+    @pl.loop(0, 8, unroll=8)
     def _(cc):
         columns = []
         for half in range(2):
@@ -318,40 +356,51 @@
             ni = now_ref[1]
             columns.append(jnp.concatenate([ur * nr + ui * ni, ui * nr - ur * ni], 0))
             advance()
-        out = dot3(late_ref[0], late_ref[1], jnp.concatenate(columns, 1), dot)
+        out = dot3(t4_ref[...], jnp.concatenate(columns, 1))
         for half in range(2):
             lanes = slice(128 * half, 128 * half + 128)
             out_ref[pl.ds(2 * cc + half, 128, stride=32), :] = out[:128, lanes]
             out_ref[pl.ds(2 * cc + half + 16, 128, stride=32), :] = out[128:, lanes]
 
+    last = pltpu.make_async_copy(out_ref, out_hbm, sent)
+    last.start()
+    last.wait()
+
 
 def middle(a, greens, place):
     t = tables()
     return pl.pallas_call(
         middle_kernel,
-        in_specs=[pl.BlockSpec(memory_space=pltpu.SMEM), spec_vmem()]
-        + [pl.BlockSpec(memory_space=pl.ANY)] * 4
-        + [spec_vmem()] * 4
-        + [pl.BlockSpec(memory_space=pl.ANY)],
-        out_specs=spec_vmem(),
-        out_shape=jax.ShapeDtypeStruct((4096, 128), f32),
+        in_specs=[pl.BlockSpec(memory_space=pltpu.SMEM), spec_vmem()] + [spec_hbm()] * 9,
+        out_specs=spec_hbm(),
+        out_shape=pltpu.HBM((4096, 128), f32),
         scratch_shapes=[
+            pltpu.VMEM((512, 768), bf16),
+            pltpu.VMEM((2, 256, 128), f32),
+            pltpu.VMEM((2, 256, 128), f32),
+            pltpu.VMEM((2, 2, 2, 1024, 128), f32),
+            pltpu.VMEM((2, 2, 8, 128), f32),
+            pltpu.VMEM((256, 1536), bf16),
             pltpu.VMEM((16, 2, 256, 128), f32),
             pltpu.VMEM((2, 256, 128), f32),
-            pltpu.VMEM((4, 2, 1024, 128), f32),
-            pltpu.VMEM((2, 256, 512), bf16),
-            pltpu.SemaphoreType.DMA((5,)),
+            pltpu.VMEM((4096, 128), f32),
+            pltpu.SemaphoreType.DMA((9,)),
+            pltpu.SemaphoreType.DMA,
         ],
-        compiler_params=params(),
+        compiler_params=params(24),
         cost_estimate=cost(2 * 8 * 2 * 512 * 65536 * 3, 10 << 20),
         name="middle",
     )(
-        place, a, *greens, jnp.asarray(t["t3"]), jnp.asarray(t["tw3"]), jnp.asarray(t["step3"]),
-        jnp.asarray(t["lane3"]), jnp.asarray(t["t4"]),
+        place, a, *in_hbm(t["t3"], t["tw3"], t["step3"], *greens, t["lane3"], t["t4"])
     )
 
 
-def x_inverse_kernel(a_ref, t5_ref, tw_ref, t6_ref, out_ref):
+def x_inverse_kernel(
+    a_ref, t5_hbm, tw_hbm, t6_hbm, out_hbm, t5_ref, tw_ref, t6_ref, out_ref, arrived, sent
+):
+    for copy in fetch((t5_hbm, tw_hbm, t6_hbm), (t5_ref, tw_ref, t6_ref), arrived):
+        copy.wait()
+
     @pl.loop(0, 8, unroll=8)
     def _(cc):
         columns = []
@@ -359,7 +408,7 @@
             re = a_ref[pl.ds(2 * cc + half, 128, stride=32), :]
             im = a_ref[pl.ds(2 * cc + half + 16, 128, stride=32), :]
             columns.append(jnp.concatenate([re, im], 0))
-        u = dot3(t5_ref[0], t5_ref[1], jnp.concatenate(columns, 1), dot)
+        u = dot3(t5_ref[...], jnp.concatenate(columns, 1))
         rows = []
         for half in range(2):
             ur = u[:128, 128 * half : 128 * half + 128]
@@ -369,7 +418,7 @@
                     [ur * tw_ref[0] - ui * tw_ref[1], ur * tw_ref[1] + ui * tw_ref[0]], 1
                 )
             )
-        out = dot3(t6_ref[0], t6_ref[1], jnp.concatenate(rows, 0), dot_nt)
+        out = dot3_nt(t6_ref[...], jnp.concatenate(rows, 0))
         for half in range(2):
             lanes = slice(128 * half, 128 * half + 128)
             for b0 in range(2):
@@ -377,18 +426,30 @@
                 out_ref[pl.ds(b, 32, stride=64), :] = out[64 * b0 : 64 * b0 + 32, lanes]
                 out_ref[pl.ds(b + 32, 32, stride=64), :] = out[64 * b0 + 32 : 64 * b0 + 64, lanes]
 
+    last = pltpu.make_async_copy(out_ref, out_hbm, sent)
+    last.start()
+    last.wait()
+
 
 def x_inverse(a):
     t = tables()
     return pl.pallas_call(
         x_inverse_kernel,
-        in_specs=[spec_vmem()] * 4,
-        out_specs=spec_vmem(),
-        out_shape=jax.ShapeDtypeStruct((2048, 128), f32),
-        compiler_params=params(),
+        in_specs=[spec_vmem()] + [spec_hbm()] * 3,
+        out_specs=spec_hbm(),
+        out_shape=pltpu.HBM((2048, 128), f32),
+        scratch_shapes=[
+            pltpu.VMEM((256, 768), bf16),
+            pltpu.VMEM((2, 128, 128), f32),
+            pltpu.VMEM((128, 768), bf16),
+            pltpu.VMEM((2048, 128), f32),
+            pltpu.SemaphoreType.DMA((3,)),
+            pltpu.SemaphoreType.DMA,
+        ],
+        compiler_params=params(8),
         cost_estimate=cost(2 * 2048 * 65536 * 4, 4 << 20),
         name="x_inverse",
-    )(a, jnp.asarray(t["t5"]), jnp.asarray(t["tw5"]), jnp.asarray(t["t6"]))
+    )(a, *in_hbm(t["t5"], t["tw5"], t["t6"]))
 
 
 def residual_kernel(a_ref, incident_ref, contrast_ref, source_ref, out_ref):
@@ -421,39 +482,49 @@
     )(a, incident, contrast, source)
 
 
-def pack_kernel(across, place_ref, green_ref, out_ref):
+def pack_kernel(across, place_ref, green_ref, *out_refs):
     flip = place_ref[0]
-    upper = place_ref[1]
     lane = lax.broadcasted_iota(jnp.int32, (512, 128), 1)
     low = lane < 64
     pick = low == (flip == 0)
-    swap = upper == 1
-    column = jnp.where(swap, 1 - across, across)
-    lanes = pl.ds(pl.multiple_of(column * 128, 128), 128)
-    chooses_first = low != swap
     for part in range(2):
-        first = green_ref[part, 0, :, lanes]
-        second = green_ref[part, 1, :, lanes]
-        straight = jnp.where(chooses_first, first, second)
-        crossed = pltpu.roll(jnp.where(chooses_first, second, first), 64, 1)
-        out_ref[0, part] = jnp.where(pick, straight, crossed)
-        out_ref[1, part] = jnp.where(pick, crossed, straight)
+        first = green_ref[part, 0]
+        second = green_ref[part, 1]
+        straight = jnp.where(low, first, second)
+        crossed = pltpu.roll(jnp.where(low, second, first), 64, 1)
+        for core, value in enumerate(
+            (jnp.where(pick, straight, crossed), jnp.where(pick, crossed, straight))
+        ):
+            if across:
+                out_refs[0][core, part] = value
+            else:
+                out_refs[core][part] = value
 
 
 def pack_green(green, place, across):
+    if across:
+        out_specs = pl.BlockSpec((2, 2, 512, 128), lambda t, place_ref: (0, 0, t, 0))
+        out_shape = pltpu.HBM((2, 2, 1024, 128), f32)
+    else:
+        out_specs = [pl.BlockSpec((2, 512, 128), lambda t, place_ref: (0, t, 0))] * 2
+        out_shape = [pltpu.HBM((2, 1024, 128), f32)] * 2
+
+    def column(t, place_ref):
+        return 0, 0, t, jnp.where(place_ref[1] == 1, 1 - across, across)
+
     return pl.pallas_call(
         functools.partial(pack_kernel, across),
-        grid=(2,),
-        in_specs=[
-            pl.BlockSpec(memory_space=pltpu.SMEM),
-            pl.BlockSpec((2, 2, 512, 256), lambda t: (0, 0, t, 0)),
-        ],
-        out_specs=pl.BlockSpec((2, 2, 512, 128), lambda t: (0, 0, t, 0)),
-        out_shape=jax.ShapeDtypeStruct((2, 2, 1024, 128), f32),
+        grid_spec=pltpu.PrefetchScalarGridSpec(
+            num_scalar_prefetch=1,
+            grid=(2,),
+            in_specs=[pl.BlockSpec((2, 2, 512, 128), column)],
+            out_specs=out_specs,
+        ),
+        out_shape=out_shape,
         compiler_params=params(),
-        cost_estimate=cost(0, 6 << 20),
+        cost_estimate=cost(0, 4 << 20),
         name="pack_far" if across else "pack_near",
-    )(place, green.reshape(2, 2, 1024, 256))
+    )(place, *in_hbm(green.reshape(2, 2, 1024, 256)))
 
 
 def project_kernel(source_ref, ea_ref, eb_ref, row_ref, out_ref, lhs_ref, rhs_ref):
@@ -583,12 +654,9 @@
     def partner(value, k):
         return lax.ppermute(value, "narrow", [(j, j ^ k) for j in range(NARROW)])
 
-    far = pack_green(green, place, 1)
-    far, source_after, green_after = lax.optimization_barrier((far, source, green))
-    far = partner(far, 2)
-    lines = columns_major(source_after)
-    near = pack_green(green_after, place, 0)
-    near_partner = partner(near[1], 1)
+    lines = columns_major(source)
+    lines, green = lax.optimization_barrier((lines, green))
+    far = partner(pack_green(green, place, 1), 2)
     lines = lax.all_to_all(lines.reshape(WIDE, 64, 128), "wide", 0, 0, tiled=True)
 
     row_position = (wide * 128 + jnp.arange(128, dtype=jnp.int32)).astype(f32) - N // 2 + 0.5
@@ -601,9 +669,14 @@
     partial_value = project(source, ea, eb, rows)
     lines, partial_value = lax.optimization_barrier((lines, partial_value))
     lines = x_forward(lines.reshape(2048, 128))
+    lines, partial_value = lax.optimization_barrier((lines, partial_value))
     lines = lax.all_to_all(lines.reshape(128, 32, 128), ("wide", "narrow"), 0, 0, tiled=True)
 
-    total = sum_over(partial_value, [("wide", WIDE, (1, 2, 3)), ("wide", WIDE, (8, 16, 24))])
+    total = sum_over(partial_value, [("wide", WIDE, (1, 2, 3))])
+    total, green = lax.optimization_barrier((total, green))
+    near = pack_green(green, place, 0)
+    near_partner = partner(near[1], 1)
+    total = sum_over(total, [("wide", WIDE, (8, 16, 24))])
     total, far, near_partner = lax.optimization_barrier((total, far, near_partner))
     total = sum_over(total, [("narrow", NARROW, (1,))])
     greens = [near[0], near_partner, far, partner(far[1], 1)]

time: 189 us -> 177 us (0.937)
  waiting for transfers between devices: 61.6 us -> 73.9 us
  Pallas kernels: 56.4 us -> 47.5 us
  starting transfers between devices: 51.8 us -> 45.6 us
  local copies, waits for them, and re-layouts: 8.87 us -> 3.57 us
  other arithmetic: 8.67 us -> 5.32 us
    ppermute x9, waiting for transfers between devices: 31.6 us -> 44.4 us  [exchange(): lax.ppermute(value, axis, [(j, j ^ stride) for j in range(size)])]
    ppermute x9, starting transfers between devices: 20.9 us -> 14.1 us  [exchange(): lax.ppermute(value, axis, [(j, j ^ stride) for j in range(size)])]
    all_to_all x2, waiting for transfers between devices: 6.18 us -> 10.1 us  [local(): lax.all_to_all(lines.reshape(WIDE, 64, 128), 'wide', 0, 0, tiled=True)]
    unnamed x18 -> x16, local copies, waits for them, and re-layouts: 4.29 us -> 1.26 us
    pallas_call x1, Pallas kernels: 16.9 us -> 13.9 us  [middle(): pl.pallas_call(middle_kernel, in_specs=[pl.BlockSpec(memory_space=pltpu.S...]
    ppermute x3, waiting for transfers between devices: 12.3 us -> 9.32 us  [partner(): return lax.ppermute(value, 'narrow', [(j, j ^ k) for j in range(NARROW)])]
    squeeze x2 -> x1, local copies, waits for them, and re-layouts: 4.53 us -> 2.26 us  [local(): greens = [near[0], near_partner, far, partner(far[1], 1)]]
    pallas_call x1, Pallas kernels: 6.94 us -> 5.04 us  [project(): pl.pallas_call(project_kernel, grid=(R // tile,), in_specs=[whole, pl.Blo...]
  transfers between devices with their start and end apart: 16 -> 16, of which waited for: 10 -> 11; matrix products, arithmetic and copies ran while one was open for 7% -> 4% of each run, Pallas kernels for 16% -> 17%
where the time goes in v3:
time: 177 us
  waiting for transfers between devices  73.9 us (42%)
  Pallas kernels  47.5 us (27%)
  starting transfers between devices  45.6 us (26%)
  other arithmetic  5.32 us (3%)
  local copies, waits for them, and re-layouts  3.57 us (2%)
    ppermute x9, waiting for transfers between devices, exchange(): lax.ppermute(value, axis, [(j, j ^ stride) for j in range(size)])  44.4 us
    all_to_all x2, starting transfers between devices, local(): lax.all_to_all(lines.reshape(WIDE, 64, 128), 'wide', 0, 0, tiled=True)  14.6 us
    ppermute x9, starting transfers between devices, exchange(): lax.ppermute(value, axis, [(j, j ^ stride) for j in range(size)])  14.1 us
    all_to_all x2, starting transfers between devices, local(): lax.all_to_all(lines.reshape(128, 32, 128), ('wide', 'narrow'), 0, 0, til...  14.1 us
    pallas_call x1, Pallas kernels, middle(): pl.pallas_call(middle_kernel, in_specs=[pl.BlockSpec(memory_space=pltpu.S...  13.9 us
    all_to_all x2, waiting for transfers between devices, local(): lax.all_to_all(lines.reshape(WIDE, 64, 128), 'wide', 0, 0, tiled=True)  10.1 us
    all_to_all x2, waiting for transfers between devices, local(): lax.all_to_all(lines.reshape(128, 32, 128), ('wide', 'narrow'), 0, 0, til...  10.1 us
    ppermute x3, waiting for transfers between devices, partner(): return lax.ppermute(value, 'narrow', [(j, j ^ k) for j in range(NARROW)])  9.32 us
  transfers between devices with their start and end apart: 16, of which 11 were waited for; matrix products, arithmetic and copies ran while one was open for 4% of the time, Pallas kernels for 17%

profile of v3, /device:TPU:0, one launch (start us, length us, event | category | flops | bytes accessed | tf_op | source)
XLA Modules:
  0.0 176.8 jit_solution(6109009841171512722)
XLA Ops:
  0.6 2.3 %columns_major.1 = f32[2048,128]{1,0:T(8,128)} custom-call(f32[2,128,1024]{2,1,0:T(8,128)} %bitcast.24), custom_call_target="tpu_custom_call" | custom-call | bytes 2097152 | tf_op jit(solution)/shard_map/columns_major/pallas_call | solution.py:194
  2.9 9.3 %all-to-all-start = ((f32[32,64,128]{2,1,0:T(8,128)}), f32[32,64,128]{2,1,0:T(8,128)S(1)}, u32[]{:S(2)}, u32[]{:S(2)}) async-start(f32[32,64,128]{2,1,0:T(8,128)} %bitcast.34), calls=%async_computation | async-start | bytes 2097152 | tf_op jit(solution)/shard_map/all_to_all | solution.py:660
  12.3 3.3 %pack_far.1 = f32[2,2,1024,128]{3,2,1,0:T(8,128)} custom-call(s32[2]{0:T(128)S(1)} %pad_add_fusion.place_ref, f32[2,2,1024,256]{3,2,1,0:T(8,128)} %bitcast.32), custom_call_target="tpu_custom_call" | custom-call | bytes 4194304 | tf_op jit(solution)/shard_map/pack_far/pallas_call | solution.py:515
  15.6 2.9 %collective-permute-start.6 = (f32[2,2,1024,128]{3,2,1,0:T(8,128)}, f32[2,2,1024,128]{3,2,1,0:T(8,128)}, u32[]{:S(2)}, u32[]{:S(2)}) collective-permute-start(f32[2,2,1024,128]{3,2,1,0:T(8,128)} %pack_far.1), channel_id=1, source_target_pairs={{0,2},{1,3},{2,0},{3,1},{4,6},{5,7},{6,4},{7,5},{8,10},{9,11},{10,... | collective-permute-start | bytes 6291464 | tf_op jit(solution)/shard_map/ppermute | solution.py:655
  21.7 5.0 %project.1 = f32[8,1024]{1,0:T(8,128)S(1)} custom-call(f32[2,128,1024]{2,1,0:T(8,128)S(1)} %bitcast.25, f32[2,32,1024]{2,1,0:T(8,128)S(1)} %get-tuple-element.51.ea_ref, f32[2,32,1024]{2,1,0:T(8,128)S(1)} %get-tuple-element.52.eb_ref, f32[2,128,1024]{2,1,0:T(8,128)S(1)} %pad_maximum_fusion.row_ref), custom_call_target="tpu_custom_call" | custom-call | flops 3221225472 | bytes 4194304 | tf_op jit(solution)/shard_map/project/pallas_call | solution.py:564
  26.7 1.9 %all-to-all-done = f32[32,64,128]{2,1,0:T(8,128)S(1)} async-done(((f32[32,64,128]{2,1,0:T(8,128)}), f32[32,64,128]{2,1,0:T(8,128)S(1)}, u32[]{:S(2)}, u32[]{:S(2)}) %all-to-all-start) | async-done | bytes 1048608 | tf_op jit(solution)/shard_map/all_to_all | solution.py:660
  28.7 7.1 %x_forward.1 = f32[4096,128]{1,0:T(8,128)} custom-call(f32[2048,128]{1,0:T(8,128)S(1)} %bitcast.31, bf16[128,192]{1,0:T(8,128)(2,1)} %constant.77.clone.t1_hbm, f32[2,64,128]{2,1,0:T(8,128)} %constant.78.clone.tw_hbm, bf16[256,768]{1,0:T(8,128)(2,1)} %constant.79.clone.t2_hbm), custom_call_target="tpu_custom_call" | custom-call | flops 1073741824 | bytes 4194304 | tf_op jit(solution)/shard_map/x_forward/pallas_call | solution.py:240
  42.8 3.3 %pack_near.1 = (f32[2,1024,128]{2,1,0:T(8,128)}, f32[2,1024,128]{2,1,0:T(8,128)}) custom-call(s32[2]{0:T(128)S(1)} %pad_add_fusion.place_ref, f32[2,2,1024,256]{3,2,1,0:T(8,128)} %bitcast.33), custom_call_target="tpu_custom_call" | custom-call | bytes 4194304 | tf_op jit(solution)/shard_map/pack_near/pallas_call | solution.py:515
  46.1 8.3 %all-to-all-start.1 = ((f32[128,32,128]{2,1,0:T(8,128)}), f32[128,32,128]{2,1,0:T(8,128)S(1)}, u32[]{:S(2)}, u32[]{:S(2)}) async-start(f32[128,32,128]{2,1,0:T(8,128)} %bitcast.35), calls=%async_computation.1 | async-start | bytes 4194304 | tf_op jit(solution)/shard_map/all_to_all | solution.py:673
  54.4 2.3 %collective-permute-start.5 = (f32[8,1024]{1,0:T(8,128)S(1)}, f32[8,1024]{1,0:T(8,128)S(1)}, u32[]{:S(2)}, u32[]{:S(2)}) collective-permute-start(f32[8,1024]{1,0:T(8,128)S(1)} %add_add_fusion.1), channel_id=1, source_target_pairs={{0,96},{4,100},{8,104},{12,108},{16,112},{20,116},{24,120},{28,124... | collective-permute-start | bytes 98312 | tf_op jit(solution)/shard_map/ppermute | solution.py:637
  58.6 22.2 %collective-permute-done.5 = f32[8,1024]{1,0:T(8,128)S(1)} collective-permute-done((f32[8,1024]{1,0:T(8,128)S(1)}, f32[8,1024]{1,0:T(8,128)S(1)}, u32[]{:S(2)}, u32[]{:S(2)}) %collective-permute-start.5) | collective-permute-done | bytes 32800 | tf_op jit(solution)/shard_map/ppermute | solution.py:637
  80.8 9.3 %collective-permute-done.6.r2_hbm = f32[2,2,1024,128]{3,2,1,0:T(8,128)} collective-permute-done((f32[2,2,1024,128]{3,2,1,0:T(8,128)}, f32[2,2,1024,128]{3,2,1,0:T(8,128)}, u32[]{:S(2)}, u32[]{:S(2)}) %collective-permute-start.6) | collective-permute-done | bytes 2097184 | tf_op jit(solution)/shard_map/ppermute | solution.py:655
  90.2 2.3 %slice_bitcast_fusion = f32[2,1024,128]{2,1,0:T(8,128)} fusion(f32[2,2,1024,128]{3,2,1,0:T(8,128)} %collective-permute-done.6.r2_hbm), kind=kLoop, calls=%fused_computation.2 | loop fusion | bytes 2097152 | tf_op jit(solution)/shard_map/squeeze | solution.py:682
  94.8 3.1 %all-to-all-done.1 = f32[128,32,128]{2,1,0:T(8,128)S(1)} async-done(((f32[128,32,128]{2,1,0:T(8,128)}), f32[128,32,128]{2,1,0:T(8,128)S(1)}, u32[]{:S(2)}, u32[]{:S(2)}) %all-to-all-start.1) | async-done | bytes 2097184 | tf_op jit(solution)/shard_map/all_to_all | solution.py:673
  97.9 13.9 %middle.1 = f32[4096,128]{1,0:T(8,128)} custom-call(s32[2]{0:T(128)S(1)} %pad_add_fusion.place_ref, f32[4096,128]{1,0:T(8,128)S(1)} %bitcast.28, bf16[512,768]{1,0:T(8,128)(2,1)} %constant.80.clone.t3_hbm, f32[2,256,128]{2,1,0:T(8,128)} %constant.81.clone.tw_hbm, f32[2,256,128]{2,1,0:T(8,128)} %constant.82.clone.step_hbm, ...), custom_call_target="tpu_custom_call" | custom-call | flops 3221225472 | bytes 10485760 | tf_op jit(solution)/shard_map/middle/pallas_call | solution.py:372
  111.8 5.8 %all-to-all-start.2 = ((f32[128,32,128]{2,1,0:T(8,128)}), f32[128,32,128]{2,1,0:T(8,128)S(1)}, u32[]{:S(2)}, u32[]{:S(2)}) async-start(f32[128,32,128]{2,1,0:T(8,128)} %bitcast.36), calls=%async_computation.2 | async-start | bytes 4194304 | tf_op jit(solution)/shard_map/all_to_all | solution.py:686
  118.6 17.5 %collective-permute-done.10 = f32[8,1024]{1,0:T(8,128)S(1)} collective-permute-done((f32[8,1024]{1,0:T(8,128)S(1)}, f32[8,1024]{1,0:T(8,128)S(1)}, u32[]{:S(2)}, u32[]{:S(2)}) %collective-permute-start.10) | collective-permute-done | bytes 32800 | tf_op jit(solution)/shard_map/ppermute | solution.py:637
  136.1 4.2 %collective-permute-start.11 = (f32[8,1024]{1,0:T(8,128)S(1)}, f32[8,1024]{1,0:T(8,128)S(1)}, u32[]{:S(2)}, u32[]{:S(2)}) collective-permute-start(f32[8,1024]{1,0:T(8,128)S(1)} %add.106), channel_id=1, source_target_pairs={{0,2},{1,3},{2,0},{3,1},{4,6},{5,7},{6,4},{7,5},{8,10},{9,11},{10,... | collective-permute-start | bytes 98312 | tf_op jit(solution)/shard_map/ppermute | solution.py:637
  140.3 7.0 %all-to-all-done.2 = f32[128,32,128]{2,1,0:T(8,128)S(1)} async-done(((f32[128,32,128]{2,1,0:T(8,128)}), f32[128,32,128]{2,1,0:T(8,128)S(1)}, u32[]{:S(2)}, u32[]{:S(2)}) %all-to-all-start.2) | async-done | bytes 2097184 | tf_op jit(solution)/shard_map/all_to_all | solution.py:686
  147.3 5.4 %x_inverse.1 = f32[2048,128]{1,0:T(8,128)} custom-call(f32[4096,128]{1,0:T(8,128)S(1)} %bitcast.29, bf16[256,768]{1,0:T(8,128)(2,1)} %constant.85.clone.t5_hbm, f32[2,128,128]{2,1,0:T(8,128)} %constant.86.clone.tw_hbm, bf16[128,768]{1,0:T(8,128)(2,1)} %constant.87.clone.t6_hbm), custom_call_target="tpu_custom_call" | custom-call | flops 1073741824 | bytes 4194304 | tf_op jit(solution)/shard_map/x_inverse/pallas_call | solution.py:436
  152.6 5.3 %all-to-all-start.3 = ((f32[32,64,128]{2,1,0:T(8,128)}), f32[32,64,128]{2,1,0:T(8,128)S(1)}, u32[]{:S(2)}, u32[]{:S(2)}) async-start(f32[32,64,128]{2,1,0:T(8,128)} %bitcast.38), calls=%async_computation.3 | async-start | bytes 2097152 | tf_op jit(solution)/shard_map/all_to_all | solution.py:689
  158.1 2.0 %add_multiply_fusion = (f32[1,128,1024]{2,1,0:T(8,128)S(1)}, f32[1,128,1024]{2,1,0:T(8,128)S(1)}) fusion(f32[1024]{0:T(1024)S(1)} %bitcast.40, f32[1024]{0:T(1024)S(1)} %bitcast.39, f32[1024]{0:T(1024)S(1)} %get-tuple-element.47, f32[128]{0:T(128)S(1)} %add_multiply_fusion.1), kind=kLoop, calls=%fused_computation.7 | loop fusion | flops 1310720 | bytes 1061376 | tf_op jit(solution)/shard_map/mul | solution.py:698
  160.2 5.6 %backproject.1 = f32[2,128,1024]{2,1,0:T(8,128)} custom-call(f32[2,128,1024]{2,1,0:T(8,128)S(1)} %pad_maximum_fusion.1.weight_ref, f32[2,32,1024]{2,1,0:T(8,128)S(1)} %get-tuple-element.51.ea_ref, f32[2,32,1024]{2,1,0:T(8,128)S(1)} %copy-done.4), custom_call_target="tpu_custom_call" | custom-call | flops 3221225472 | bytes 4194304 | tf_op jit(solution)/shard_map/backproject/pallas_call | solution.py:612
  165.9 8.2 %all-to-all-done.3 = f32[32,64,128]{2,1,0:T(8,128)S(1)} async-done(((f32[32,64,128]{2,1,0:T(8,128)}), f32[32,64,128]{2,1,0:T(8,128)S(1)}, u32[]{:S(2)}, u32[]{:S(2)}) %all-to-all-start.3) | async-done | bytes 1048608 | tf_op jit(solution)/shard_map/all_to_all | solution.py:689
  (51 shorter events, 18.4 us)
Async XLA Ops:
  2.9 25.8 %all-to-all-start = ((f32[32,64,128]{2,1,0:T(8,128)}), f32[32,64,128]{2,1,0:T(8,128)S(1)}, u32[]{:S(2)}, u32[]{:S(2)}) async-start(f32[32,64,128]{2,1,0:T(8,128)} %bitcast.34), calls=%async_computation | async-start | bytes 2097152 | tf_op jit(solution)/shard_map/all_to_all | solution.py:660
  12.3 6.3 %copy-start.7 = (f32[1024]{0:T(1024)S(1)}, f32[1024]{0:T(1024)}, u32[]{:S(2)}) copy-start(f32[1024]{0:T(1024)} %param.21) | copy-start | bytes 12292
  15.6 74.5 %collective-permute-start.6 = (f32[2,2,1024,128]{3,2,1,0:T(8,128)}, f32[2,2,1024,128]{3,2,1,0:T(8,128)}, u32[]{:S(2)}, u32[]{:S(2)}) collective-permute-start(f32[2,2,1024,128]{3,2,1,0:T(8,128)} %pack_far.1), channel_id=1, source_target_pairs={{0,2},{1,3},{2,0},{3,1},{4,6},{5,7},{6,4},{7,5},{8,10},{9,11},{10,... | collective-permute-start | bytes 6291464 | tf_op jit(solution)/shard_map/ppermute | solution.py:655
  19.6 2.1 %copy-start = (f32[1,2,128,1024]{3,2,1,0:T(8,128)S(1)}, f32[1,2,128,1024]{3,2,1,0:T(8,128)}, u32[]{:S(2)}) copy-start(f32[1,2,128,1024]{3,2,1,0:T(8,128)} %param.17) | copy-start | bytes 3145732
  19.6 7.1 %copy-start.3 = (f32[2,32,1024]{2,1,0:T(8,128)}, f32[2,32,1024]{2,1,0:T(8,128)S(1)}, u32[]{:S(2)}) copy-start(f32[2,32,1024]{2,1,0:T(8,128)S(1)} %get-tuple-element.52.eb_ref) | copy-start | bytes 786436
  35.8 5.2 %collective-permute-start.2 = (f32[8,1024]{1,0:T(8,128)S(1)}, f32[8,1024]{1,0:T(8,128)S(1)}, u32[]{:S(2)}, u32[]{:S(2)}) collective-permute-start(f32[8,1024]{1,0:T(8,128)S(1)} %project.1), channel_id=1, source_target_pairs={{0,12},{4,8},{8,4},{12,0},{16,28},{20,24},{24,20},{28,16},{32,44},... | collective-permute-start | bytes 98312 | tf_op jit(solution)/shard_map/ppermute | solution.py:637
  37.0 5.4 %collective-permute-start.1 = (f32[8,1024]{1,0:T(8,128)S(1)}, f32[8,1024]{1,0:T(8,128)S(1)}, u32[]{:S(2)}, u32[]{:S(2)}) collective-permute-start(f32[8,1024]{1,0:T(8,128)S(1)} %project.1), channel_id=1, source_target_pairs={{0,8},{4,12},{8,0},{12,4},{16,24},{20,28},{24,16},{28,20},{32,40},... | collective-permute-start | bytes 98312 | tf_op jit(solution)/shard_map/ppermute | solution.py:637
  38.9 3.9 %collective-permute-start = (f32[8,1024]{1,0:T(8,128)S(1)}, f32[8,1024]{1,0:T(8,128)S(1)}, u32[]{:S(2)}, u32[]{:S(2)}) collective-permute-start(f32[8,1024]{1,0:T(8,128)S(1)} %project.1), channel_id=1, source_target_pairs={{0,4},{4,0},{8,12},{12,8},{16,20},{20,16},{24,28},{28,24},{32,36},... | collective-permute-start | bytes 98312 | tf_op jit(solution)/shard_map/ppermute | solution.py:637
  46.1 44.0 %collective-permute-start.7 = (f32[2,1024,128]{2,1,0:T(8,128)}, f32[2,1024,128]{2,1,0:T(8,128)}, u32[]{:S(2)}, u32[]{:S(2)}) collective-permute-start(f32[2,1024,128]{2,1,0:T(8,128)} %get-tuple-element.27), channel_id=1, source_target_pairs={{0,1},{1,0},{2,3},{3,2},{4,5},{5,4},{6,7},{7,6},{8,9},{9,8},{10,11... | collective-permute-start | bytes 3145736 | tf_op jit(solution)/shard_map/ppermute | solution.py:655
  46.1 51.7 %all-to-all-start.1 = ((f32[128,32,128]{2,1,0:T(8,128)}), f32[128,32,128]{2,1,0:T(8,128)S(1)}, u32[]{:S(2)}, u32[]{:S(2)}) async-start(f32[128,32,128]{2,1,0:T(8,128)} %bitcast.35), calls=%async_computation.1 | async-start | bytes 4194304 | tf_op jit(solution)/shard_map/all_to_all | solution.py:673
  54.4 26.4 %collective-permute-start.5 = (f32[8,1024]{1,0:T(8,128)S(1)}, f32[8,1024]{1,0:T(8,128)S(1)}, u32[]{:S(2)}, u32[]{:S(2)}) collective-permute-start(f32[8,1024]{1,0:T(8,128)S(1)} %add_add_fusion.1), channel_id=1, source_target_pairs={{0,96},{4,100},{8,104},{12,108},{16,112},{20,116},{24,120},{28,124... | collective-permute-start | bytes 98312 | tf_op jit(solution)/shard_map/ppermute | solution.py:637
  56.7 24.1 %collective-permute-start.4 = (f32[8,1024]{1,0:T(8,128)S(1)}, f32[8,1024]{1,0:T(8,128)S(1)}, u32[]{:S(2)}, u32[]{:S(2)}) collective-permute-start(f32[8,1024]{1,0:T(8,128)S(1)} %add_add_fusion.1), channel_id=1, source_target_pairs={{0,64},{4,68},{8,72},{12,76},{16,80},{20,84},{24,88},{28,92},{32,9... | collective-permute-start | bytes 98312 | tf_op jit(solution)/shard_map/ppermute | solution.py:637
  57.5 23.3 %collective-permute-start.3 = (f32[8,1024]{1,0:T(8,128)S(1)}, f32[8,1024]{1,0:T(8,128)S(1)}, u32[]{:S(2)}, u32[]{:S(2)}) collective-permute-start(f32[8,1024]{1,0:T(8,128)S(1)} %add_add_fusion.1), channel_id=1, source_target_pairs={{0,32},{4,36},{8,40},{12,44},{16,48},{20,52},{24,56},{28,60},{32,0... | collective-permute-start | bytes 98312 | tf_op jit(solution)/shard_map/ppermute | solution.py:637
  92.4 5.4 %collective-permute-start.9 = (f32[2,1024,128]{2,1,0:T(8,128)}, f32[2,1024,128]{2,1,0:T(8,128)}, u32[]{:S(2)}, u32[]{:S(2)}) collective-permute-start(f32[2,1024,128]{2,1,0:T(8,128)} %slice_bitcast_fusion), channel_id=1, source_target_pairs={{0,1},{1,0},{2,3},{3,2},{4,5},{5,4},{6,7},{7,6},{8,9},{9,8},{10,11... | collective-permute-start | bytes 3145736 | tf_op jit(solution)/shard_map/ppermute | solution.py:655
  92.4 2.3 %collective-permute-start.8 = (f32[8,1024]{1,0:T(8,128)S(1)}, f32[8,1024]{1,0:T(8,128)S(1)}, u32[]{:S(2)}, u32[]{:S(2)}) collective-permute-start(f32[8,1024]{1,0:T(8,128)S(1)} %add_add_fusion), channel_id=1, source_target_pairs={{0,1},{1,0},{2,3},{3,2},{4,5},{5,4},{6,7},{7,6},{8,9},{9,8},{10,11... | collective-permute-start | bytes 98312 | tf_op jit(solution)/shard_map/ppermute | solution.py:637
  111.8 35.5 %all-to-all-start.2 = ((f32[128,32,128]{2,1,0:T(8,128)}), f32[128,32,128]{2,1,0:T(8,128)S(1)}, u32[]{:S(2)}, u32[]{:S(2)}) async-start(f32[128,32,128]{2,1,0:T(8,128)} %bitcast.36), calls=%async_computation.2 | async-start | bytes 4194304 | tf_op jit(solution)/shard_map/all_to_all | solution.py:686
  117.5 18.5 %collective-permute-start.10 = (f32[8,1024]{1,0:T(8,128)S(1)}, f32[8,1024]{1,0:T(8,128)S(1)}, u32[]{:S(2)}, u32[]{:S(2)}) collective-permute-start(f32[8,1024]{1,0:T(8,128)S(1)} %add.105), channel_id=1, source_target_pairs={{0,16},{4,20},{8,24},{12,28},{16,0},{20,4},{24,8},{28,12},{32,48},... | collective-permute-start | bytes 98312 | tf_op jit(solution)/shard_map/ppermute | solution.py:637
  136.1 21.9 %collective-permute-start.11 = (f32[8,1024]{1,0:T(8,128)S(1)}, f32[8,1024]{1,0:T(8,128)S(1)}, u32[]{:S(2)}, u32[]{:S(2)}) collective-permute-start(f32[8,1024]{1,0:T(8,128)S(1)} %add.106), channel_id=1, source_target_pairs={{0,2},{1,3},{2,0},{3,1},{4,6},{5,7},{6,4},{7,5},{8,10},{9,11},{10,... | collective-permute-start | bytes 98312 | tf_op jit(solution)/shard_map/ppermute | solution.py:637
  147.3 10.7 %copy-start.6 = (f32[1,2,1024]{2,1,0:T(2,128)S(1)}, f32[1,2,1024]{2,1,0:T(2,128)}, u32[]{:S(2)}) copy-start(f32[1,2,1024]{2,1,0:T(2,128)} %param.22) | copy-start | bytes 24580
  152.6 21.4 %all-to-all-start.3 = ((f32[32,64,128]{2,1,0:T(8,128)}), f32[32,64,128]{2,1,0:T(8,128)S(1)}, u32[]{:S(2)}, u32[]{:S(2)}) async-start(f32[32,64,128]{2,1,0:T(8,128)} %bitcast.38), calls=%async_computation.3 | async-start | bytes 2097152 | tf_op jit(solution)/shard_map/all_to_all | solution.py:689
  158.0 2.2 %copy-start.4 = (f32[2,32,1024]{2,1,0:T(8,128)S(1)}, f32[2,32,1024]{2,1,0:T(8,128)}, u32[]{:S(2)}) copy-start(f32[2,32,1024]{2,1,0:T(8,128)} %copy-done.3) | copy-start | bytes 786436
  158.0 7.9 %copy-start.5 = (f32[1,2,1024]{2,1,0:T(2,128)}, f32[1,2,1024]{2,1,0:T(2,128)S(1)}, u32[]{:S(2)}) copy-start(f32[1,2,1024]{2,1,0:T(2,128)S(1)} %fusion.5) | copy-start | bytes 24580
  160.2 13.9 %copy-start.1 = (f32[1,2,128,1024]{3,2,1,0:T(8,128)S(1)}, f32[1,2,128,1024]{3,2,1,0:T(8,128)}, u32[]{:S(2)}) copy-start(f32[1,2,128,1024]{3,2,1,0:T(8,128)} %param.18) | copy-start | bytes 3145732
  174.1 1.2 copy-start.2

commit v4 on v3

--- a/solution.py
+++ b/solution.py
@@ -256,6 +256,10 @@
     )(a, *in_hbm(t["t1"], t["tw1"], t["t2"]))
 
 
+def line_row(c):
+    return c // 8 * 16 + c % 8
+
+
 def middle_kernel(
     place_ref, a_ref, t3_hbm, tw_hbm, step_hbm, r0_hbm, r1_hbm, r2_hbm, r3_hbm, lane_hbm, t4_hbm,
     out_hbm, t3_ref, tw_ref, step_ref, green_ref, lane_ref, t4_ref, u_ref, now_ref, out_ref,
@@ -346,8 +350,8 @@
 
     now_ref[...] = tw_ref[...]
 
-    @pl.loop(0, 8, unroll=8)
-    def _(cc):
+    halves = []
+    for cc in range(8):
         columns = []
         for half in range(2):
             ur = u_ref[2 * cc + half, 0]
@@ -359,12 +363,19 @@
         out = dot3(t4_ref[...], jnp.concatenate(columns, 1))
         for half in range(2):
             lanes = slice(128 * half, 128 * half + 128)
-            out_ref[pl.ds(2 * cc + half, 128, stride=32), :] = out[:128, lanes]
-            out_ref[pl.ds(2 * cc + half + 16, 128, stride=32), :] = out[128:, lanes]
-
-    last = pltpu.make_async_copy(out_ref, out_hbm, sent)
-    last.start()
-    last.wait()
+            row = line_row(2 * cc + half)
+            out_ref[pl.ds(row, 128, stride=32), :] = out[:128, lanes]
+            out_ref[pl.ds(row + 8, 128, stride=32), :] = out[128:, lanes]
+        if cc % 4 == 3:
+            rows = pl.ds(cc // 4 * 16, 16)
+            halves.append(
+                pltpu.make_async_copy(
+                    out_ref.reshape(128, 32, 128).at[:, rows], out_hbm.at[:, rows], sent.at[cc // 4]
+                )
+            )
+            halves[-1].start()
+    for copy in halves:
+        copy.wait()
 
 
 def middle(a, greens, place):
@@ -373,7 +384,7 @@
         middle_kernel,
         in_specs=[pl.BlockSpec(memory_space=pltpu.SMEM), spec_vmem()] + [spec_hbm()] * 9,
         out_specs=spec_hbm(),
-        out_shape=pltpu.HBM((4096, 128), f32),
+        out_shape=pltpu.HBM((128, 32, 128), f32),
         scratch_shapes=[
             pltpu.VMEM((512, 768), bf16),
             pltpu.VMEM((2, 256, 128), f32),
@@ -385,7 +396,7 @@
             pltpu.VMEM((2, 256, 128), f32),
             pltpu.VMEM((4096, 128), f32),
             pltpu.SemaphoreType.DMA((9,)),
-            pltpu.SemaphoreType.DMA,
+            pltpu.SemaphoreType.DMA((2,)),
         ],
         compiler_params=params(24),
         cost_estimate=cost(2 * 8 * 2 * 512 * 65536 * 3, 10 << 20),
@@ -401,12 +412,13 @@
     for copy in fetch((t5_hbm, tw_hbm, t6_hbm), (t5_ref, tw_ref, t6_ref), arrived):
         copy.wait()
 
-    @pl.loop(0, 8, unroll=8)
-    def _(cc):
+    blocks = []
+    for cc in range(8):
         columns = []
         for half in range(2):
-            re = a_ref[pl.ds(2 * cc + half, 128, stride=32), :]
-            im = a_ref[pl.ds(2 * cc + half + 16, 128, stride=32), :]
+            row = line_row(2 * cc + half)
+            re = a_ref[pl.ds(row, 128, stride=32), :]
+            im = a_ref[pl.ds(row + 8, 128, stride=32), :]
             columns.append(jnp.concatenate([re, im], 0))
         u = dot3(t5_ref[...], jnp.concatenate(columns, 1))
         rows = []
@@ -422,13 +434,19 @@
         for half in range(2):
             lanes = slice(128 * half, 128 * half + 128)
             for b0 in range(2):
-                b = 2 * (2 * cc + half) + b0
-                out_ref[pl.ds(b, 32, stride=64), :] = out[64 * b0 : 64 * b0 + 32, lanes]
-                out_ref[pl.ds(b + 32, 32, stride=64), :] = out[64 * b0 + 32 : 64 * b0 + 64, lanes]
-
-    last = pltpu.make_async_copy(out_ref, out_hbm, sent)
-    last.start()
-    last.wait()
+                row = line_row(4 * cc + 2 * half + b0)
+                out_ref[pl.ds(row, 32, stride=64), :] = out[64 * b0 : 64 * b0 + 32, lanes]
+                out_ref[pl.ds(row + 8, 32, stride=64), :] = out[64 * b0 + 32 : 64 * b0 + 64, lanes]
+        if cc % 2 == 1:
+            rows = pl.ds(cc // 2 * 16, 16)
+            blocks.append(
+                pltpu.make_async_copy(
+                    out_ref.reshape(32, 64, 128).at[:, rows], out_hbm.at[:, rows], sent.at[cc // 2]
+                )
+            )
+            blocks[-1].start()
+    for copy in blocks:
+        copy.wait()
 
 
 def x_inverse(a):
@@ -437,14 +455,14 @@
         x_inverse_kernel,
         in_specs=[spec_vmem()] + [spec_hbm()] * 3,
         out_specs=spec_hbm(),
-        out_shape=pltpu.HBM((2048, 128), f32),
+        out_shape=pltpu.HBM((32, 64, 128), f32),
         scratch_shapes=[
             pltpu.VMEM((256, 768), bf16),
             pltpu.VMEM((2, 128, 128), f32),
             pltpu.VMEM((128, 768), bf16),
             pltpu.VMEM((2048, 128), f32),
             pltpu.SemaphoreType.DMA((3,)),
-            pltpu.SemaphoreType.DMA,
+            pltpu.SemaphoreType.DMA((4,)),
         ],
         compiler_params=params(8),
         cost_estimate=cost(2 * 2048 * 65536 * 4, 4 << 20),
@@ -452,34 +470,34 @@
     )(a, *in_hbm(t["t5"], t["tw5"], t["t6"]))
 
 
-def residual_kernel(a_ref, incident_ref, contrast_ref, source_ref, out_ref):
+def residual_kernel(a_ref, contrast_ref, known_ref, out_ref):
     for tile in range(4):
         lanes = slice(128 * tile, 128 * tile + 128)
-        field = []
+        scattered = []
         for part in range(2):
             rows = []
-            for block in range(4):
-                first = 256 * tile + block * 64 + part * 32
-                rows.append(a_ref[first : first + 32, :])
-            field.append(incident_ref[part, :, lanes] + jnp.concatenate(rows, 0).T)
+            for block in range(16):
+                first = 256 * tile + block * 16 + part * 8
+                rows.append(a_ref[first : first + 8, :])
+            scattered.append(jnp.concatenate(rows, 0).T)
         cr = contrast_ref[0, :, lanes]
         ci = contrast_ref[1, :, lanes]
-        out_ref[0, :, lanes] = cr * field[0] - ci * field[1] - source_ref[0, :, lanes]
-        out_ref[1, :, lanes] = cr * field[1] + ci * field[0] - source_ref[1, :, lanes]
-
-
-def residual_of(a, incident, contrast, source):
+        out_ref[0, :, lanes] = cr * scattered[0] - ci * scattered[1] + known_ref[0, :, lanes]
+        out_ref[1, :, lanes] = cr * scattered[1] + ci * scattered[0] + known_ref[1, :, lanes]
+
+
+def residual_of(a, contrast, known):
     tile = pl.BlockSpec((2, 128, 512), lambda t: (0, 0, t))
     return pl.pallas_call(
         residual_kernel,
         grid=(2,),
-        in_specs=[pl.BlockSpec((1024, 128), lambda t: (t, 0)), tile, tile, tile],
+        in_specs=[pl.BlockSpec((1024, 128), lambda t: (t, 0)), tile, tile],
         out_specs=tile,
         out_shape=jax.ShapeDtypeStruct((2, 128, 1024), f32),
         compiler_params=params(),
-        cost_estimate=cost(0, 5 << 20),
+        cost_estimate=cost(0, 4 << 20),
         name="residual",
-    )(a, incident, contrast, source)
+    )(a, contrast, known)
 
 
 def pack_kernel(across, place_ref, green_ref, *out_refs):
@@ -527,6 +545,23 @@
     )(place, *in_hbm(green.reshape(2, 2, 1024, 256)))
 
 
+def second_kernel(in_ref, out_ref):
+    out_ref[...] = in_ref[0]
+
+
+def second_of(values):
+    return pl.pallas_call(
+        second_kernel,
+        grid=(2,),
+        in_specs=[pl.BlockSpec((1, 1, 1024, 128), lambda t: (1, t, 0, 0))],
+        out_specs=pl.BlockSpec((1, 1024, 128), lambda t: (t, 0, 0)),
+        out_shape=pltpu.HBM(values.shape[1:], f32),
+        compiler_params=params(8),
+        cost_estimate=cost(0, 2 << 20),
+        name="second",
+    )(*in_hbm(values))
+
+
 def project_kernel(source_ref, ea_ref, eb_ref, row_ref, out_ref, lhs_ref, rhs_ref):
     @pl.when(pl.program_id(0) == 0)
     def _():
@@ -679,15 +714,24 @@
     total = sum_over(total, [("wide", WIDE, (8, 16, 24))])
     total, far, near_partner = lax.optimization_barrier((total, far, near_partner))
     total = sum_over(total, [("narrow", NARROW, (1,))])
-    greens = [near[0], near_partner, far, partner(far[1], 1)]
+    greens = [near[0], near_partner, far, partner(second_of(far), 1)]
     total, lines = lax.optimization_barrier((total, lines))
     lines = middle(lines.reshape(4096, 128), greens, place)
     total, lines = lax.optimization_barrier((total, lines))
     lines = lax.all_to_all(lines.reshape(128, 32, 128), ("wide", "narrow"), 0, 0, tiled=True)
-    total = sum_over(total, [("wide", WIDE, (4,)), ("narrow", NARROW, (2,))])[:2]
+    total = sum_over(
+        total, [(("wide", "narrow"), WIDE * NARROW, (2, 4 * NARROW, 4 * NARROW + 2))]
+    )[:2]
     lines = x_inverse(lines.reshape(4096, 128))
+    lines, contrast = lax.optimization_barrier((lines, contrast))
+    known = jnp.stack(
+        [
+            contrast[0] * incident[0, 0] - contrast[1] * incident[0, 1] - source[0],
+            contrast[0] * incident[0, 1] + contrast[1] * incident[0, 0] - source[1],
+        ]
+    )
     lines = lax.all_to_all(lines.reshape(WIDE, 64, 128), "wide", 0, 0, tiled=True)
-    residual = residual_of(lines.reshape(2048, 128), incident[0], contrast, source)
+    residual = residual_of(lines.reshape(2048, 128), contrast, known)
 
     data_residual = measured - total[None] * (1.0 / N)
     rho_real = data_residual[0, 0][None, :]

time: 177 us -> 175 us (0.989)
  local copies, waits for them, and re-layouts: 3.57 us -> 0.09 us
    ppermute x9 -> x10, waiting for transfers between devices: 44.4 us -> 48 us  [exchange(): lax.ppermute(value, axis, [(j, j ^ stride) for j in range(size)])]
    all_to_all x2, waiting for transfers between devices: 10.1 us -> 7.04 us  [local(): lax.all_to_all(lines.reshape(128, 32, 128), ('wide', 'narrow'), 0, 0, til...]
    squeeze x1 -> x0, local copies, waits for them, and re-layouts: 2.26 us -> none  [local(): greens = [near[0], near_partner, far, partner(far[1], 1)]]
    pallas_call x0 -> x1, Pallas kernels: none -> 2.04 us  [second_of(): pl.pallas_call(second_kernel, grid=(2,), in_specs=[pl.BlockSpec((1, 1, 10...]
    ppermute x9 -> x10, starting transfers between devices: 14.1 us -> 13.6 us  [exchange(): lax.ppermute(value, axis, [(j, j ^ stride) for j in range(size)])]
  transfers between devices with their start and end apart: 16 -> 17, of which waited for: 11 -> 11; matrix products, arithmetic and copies ran while one was open for 4% -> 3% of each run, Pallas kernels for 17% -> 15%
where the time goes in v4:
time: 175 us
  waiting for transfers between devices  74.3 us (42%)
  Pallas kernels  48.9 us (28%)
  starting transfers between devices  44.5 us (25%)
  other arithmetic  5.76 us (3%)
    ppermute x10, waiting for transfers between devices, exchange(): lax.ppermute(value, axis, [(j, j ^ stride) for j in range(size)])  48 us
    all_to_all x2, starting transfers between devices, local(): lax.all_to_all(lines.reshape(WIDE, 64, 128), 'wide', 0, 0, tiled=True)  14.2 us
    all_to_all x2, starting transfers between devices, local(): lax.all_to_all(lines.reshape(128, 32, 128), ('wide', 'narrow'), 0, 0, til...  13.8 us
    ppermute x10, starting transfers between devices, exchange(): lax.ppermute(value, axis, [(j, j ^ stride) for j in range(size)])  13.6 us
    pallas_call x1, Pallas kernels, middle(): pl.pallas_call(middle_kernel, in_specs=[pl.BlockSpec(memory_space=pltpu.S...  13.6 us
    all_to_all x2, waiting for transfers between devices, local(): lax.all_to_all(lines.reshape(WIDE, 64, 128), 'wide', 0, 0, tiled=True)  9.93 us
    ppermute x3, waiting for transfers between devices, partner(): return lax.ppermute(value, 'narrow', [(j, j ^ k) for j in range(NARROW)])  9.36 us
    pallas_call x1, Pallas kernels, x_forward(): pl.pallas_call(x_forward_kernel, in_specs=[spec_vmem()] + [spec_hbm()] *...  7.09 us
  transfers between devices with their start and end apart: 17, of which 11 were waited for; matrix products, arithmetic and copies ran while one was open for 3% of the time, Pallas kernels for 15%

profile of v4, /device:TPU:0, one launch (start us, length us, event | category | flops | bytes accessed | tf_op | source)
XLA Modules:
  0.0 174.5 jit_solution(5690791203772233648)
XLA Ops:
  0.6 2.3 %columns_major.1 = f32[2048,128]{1,0:T(8,128)} custom-call(f32[2,128,1024]{2,1,0:T(8,128)} %bitcast.41), custom_call_target="tpu_custom_call" | custom-call | bytes 2097152 | tf_op jit(solution)/shard_map/columns_major/pallas_call | solution.py:194
  2.9 9.3 %all-to-all-start = ((f32[32,64,128]{2,1,0:T(8,128)}), f32[32,64,128]{2,1,0:T(8,128)S(1)}, u32[]{:S(2)}, u32[]{:S(2)}) async-start(f32[32,64,128]{2,1,0:T(8,128)} %bitcast.49), calls=%async_computation | async-start | bytes 2097152 | tf_op jit(solution)/shard_map/all_to_all | solution.py:695
  12.3 3.4 %pack_far.1 = f32[2,2,1024,128]{3,2,1,0:T(8,128)} custom-call(s32[2]{0:T(128)S(1)} %pad_add_fusion.place_ref, f32[2,2,1024,256]{3,2,1,0:T(8,128)} %bitcast.47), custom_call_target="tpu_custom_call" | custom-call | bytes 4194304 | tf_op jit(solution)/shard_map/pack_far/pallas_call | solution.py:533
  15.6 2.9 %collective-permute-start.6 = (f32[2,2,1024,128]{3,2,1,0:T(8,128)}, f32[2,2,1024,128]{3,2,1,0:T(8,128)}, u32[]{:S(2)}, u32[]{:S(2)}) collective-permute-start(f32[2,2,1024,128]{3,2,1,0:T(8,128)} %pack_far.1), channel_id=1, source_target_pairs={{0,2},{1,3},{2,0},{3,1},{4,6},{5,7},{6,4},{7,5},{8,10},{9,11},{10,... | collective-permute-start | bytes 6291464 | tf_op jit(solution)/shard_map/ppermute | solution.py:690
  21.7 5.0 %project.1 = f32[8,1024]{1,0:T(8,128)S(1)} custom-call(f32[2,128,1024]{2,1,0:T(8,128)S(1)} %bitcast.42, f32[2,32,1024]{2,1,0:T(8,128)S(1)} %get-tuple-element.57.ea_ref, f32[2,32,1024]{2,1,0:T(8,128)S(1)} %get-tuple-element.58.eb_ref, f32[2,128,1024]{2,1,0:T(8,128)S(1)} %pad_maximum_fusion.row_ref), custom_call_target="tpu_custom_call" | custom-call | flops 3221225472 | bytes 4194304 | tf_op jit(solution)/shard_map/project/pallas_call | solution.py:599
  28.7 7.1 %x_forward.1 = f32[4096,128]{1,0:T(8,128)} custom-call(f32[2048,128]{1,0:T(8,128)S(1)} %bitcast.46, bf16[128,192]{1,0:T(8,128)(2,1)} %constant.77.clone.t1_hbm, f32[2,64,128]{2,1,0:T(8,128)} %constant.78.clone.tw_hbm, bf16[256,768]{1,0:T(8,128)(2,1)} %constant.79.clone.t2_hbm), custom_call_target="tpu_custom_call" | custom-call | flops 1073741824 | bytes 4194304 | tf_op jit(solution)/shard_map/x_forward/pallas_call | solution.py:240
  42.8 3.3 %pack_near.1 = (f32[2,1024,128]{2,1,0:T(8,128)}, f32[2,1024,128]{2,1,0:T(8,128)}) custom-call(s32[2]{0:T(128)S(1)} %pad_add_fusion.place_ref, f32[2,2,1024,256]{3,2,1,0:T(8,128)} %bitcast.48), custom_call_target="tpu_custom_call" | custom-call | bytes 4194304 | tf_op jit(solution)/shard_map/pack_near/pallas_call | solution.py:533
  46.1 8.3 %all-to-all-start.1 = ((f32[128,32,128]{2,1,0:T(8,128)}), f32[128,32,128]{2,1,0:T(8,128)S(1)}, u32[]{:S(2)}, u32[]{:S(2)}) async-start(f32[128,32,128]{2,1,0:T(8,128)} %bitcast.50), calls=%async_computation.1 | async-start | bytes 4194304 | tf_op jit(solution)/shard_map/all_to_all | solution.py:708
  54.4 2.3 %collective-permute-start.5 = (f32[8,1024]{1,0:T(8,128)S(1)}, f32[8,1024]{1,0:T(8,128)S(1)}, u32[]{:S(2)}, u32[]{:S(2)}) collective-permute-start(f32[8,1024]{1,0:T(8,128)S(1)} %add_add_fusion.1), channel_id=1, source_target_pairs={{0,96},{4,100},{8,104},{12,108},{16,112},{20,116},{24,120},{28,124... | collective-permute-start | bytes 98312 | tf_op jit(solution)/shard_map/ppermute | solution.py:672
  58.6 22.2 %collective-permute-done.5 = f32[8,1024]{1,0:T(8,128)S(1)} collective-permute-done((f32[8,1024]{1,0:T(8,128)S(1)}, f32[8,1024]{1,0:T(8,128)S(1)}, u32[]{:S(2)}, u32[]{:S(2)}) %collective-permute-start.5) | collective-permute-done | bytes 32800 | tf_op jit(solution)/shard_map/ppermute | solution.py:672
  80.8 9.4 %collective-permute-done.6.in_ref.r2_hbm = f32[2,2,1024,128]{3,2,1,0:T(8,128)} collective-permute-done((f32[2,2,1024,128]{3,2,1,0:T(8,128)}, f32[2,2,1024,128]{3,2,1,0:T(8,128)}, u32[]{:S(2)}, u32[]{:S(2)}) %collective-permute-start.6) | collective-permute-done | bytes 2097184 | tf_op jit(solution)/shard_map/ppermute | solution.py:690
  90.2 2.0 %second.1 = f32[2,1024,128]{2,1,0:T(8,128)} custom-call(f32[2,2,1024,128]{3,2,1,0:T(8,128)} %collective-permute-done.6.in_ref.r2_hbm), custom_call_target="tpu_custom_call" | custom-call | bytes 2097152 | tf_op jit(solution)/shard_map/second/pallas_call | solution.py:553
  94.5 3.3 %all-to-all-done.1 = f32[128,32,128]{2,1,0:T(8,128)S(1)} async-done(((f32[128,32,128]{2,1,0:T(8,128)}), f32[128,32,128]{2,1,0:T(8,128)S(1)}, u32[]{:S(2)}, u32[]{:S(2)}) %all-to-all-start.1) | async-done | bytes 2097184 | tf_op jit(solution)/shard_map/all_to_all | solution.py:708
  97.9 13.6 %middle.1 = f32[128,32,128]{2,1,0:T(8,128)} custom-call(s32[2]{0:T(128)S(1)} %pad_add_fusion.place_ref, f32[4096,128]{1,0:T(8,128)S(1)} %bitcast.44, bf16[512,768]{1,0:T(8,128)(2,1)} %constant.80.clone.t3_hbm, f32[2,256,128]{2,1,0:T(8,128)} %constant.81.clone.tw_hbm, f32[2,256,128]{2,1,0:T(8,128)} %constant.82.clone.step_hbm, ...), custom_call_target="tpu_custom_call" | custom-call | flops 3221225472 | bytes 10485760 | tf_op jit(solution)/shard_map/middle/pallas_call | solution.py:383
  111.5 5.5 %all-to-all-start.2 = ((f32[128,32,128]{2,1,0:T(8,128)}), f32[128,32,128]{2,1,0:T(8,128)S(1)}, u32[]{:S(2)}, u32[]{:S(2)}) async-start(f32[128,32,128]{2,1,0:T(8,128)} %middle.1), calls=%async_computation.2 | async-start | bytes 4194304 | tf_op jit(solution)/shard_map/all_to_all | solution.py:721
  117.1 2.3 %collective-permute-start.12 = (f32[8,1024]{1,0:T(8,128)S(1)}, f32[8,1024]{1,0:T(8,128)S(1)}, u32[]{:S(2)}, u32[]{:S(2)}) collective-permute-start(f32[8,1024]{1,0:T(8,128)S(1)} %add.112), channel_id=1, source_target_pairs={{0,18},{1,19},{2,16},{3,17},{4,22},{5,23},{6,20},{7,21},{8,26},{9,... | collective-permute-start | bytes 98312 | tf_op jit(solution)/shard_map/ppermute | solution.py:672
  119.6 2.3 %collective-permute-start.10 = (f32[8,1024]{1,0:T(8,128)S(1)}, f32[8,1024]{1,0:T(8,128)S(1)}, u32[]{:S(2)}, u32[]{:S(2)}) collective-permute-start(f32[8,1024]{1,0:T(8,128)S(1)} %add.112), channel_id=1, source_target_pairs={{0,2},{1,3},{2,0},{3,1},{4,6},{5,7},{6,4},{7,5},{8,10},{9,11},{10,... | collective-permute-start | bytes 98312 | tf_op jit(solution)/shard_map/ppermute | solution.py:672
  121.8 21.1 %collective-permute-done.12 = f32[8,1024]{1,0:T(8,128)S(1)} collective-permute-done((f32[8,1024]{1,0:T(8,128)S(1)}, f32[8,1024]{1,0:T(8,128)S(1)}, u32[]{:S(2)}, u32[]{:S(2)}) %collective-permute-start.12) | collective-permute-done | bytes 32800 | tf_op jit(solution)/shard_map/ppermute | solution.py:672
  143.0 3.7 %all-to-all-done.2 = f32[128,32,128]{2,1,0:T(8,128)S(1)} async-done(((f32[128,32,128]{2,1,0:T(8,128)}), f32[128,32,128]{2,1,0:T(8,128)S(1)}, u32[]{:S(2)}, u32[]{:S(2)}) %all-to-all-start.2) | async-done | bytes 2097184 | tf_op jit(solution)/shard_map/all_to_all | solution.py:721
  146.8 5.1 %x_inverse.1 = f32[32,64,128]{2,1,0:T(8,128)} custom-call(f32[4096,128]{1,0:T(8,128)S(1)} %bitcast.45, bf16[256,768]{1,0:T(8,128)(2,1)} %constant.85.clone.t5_hbm, f32[2,128,128]{2,1,0:T(8,128)} %constant.86.clone.tw_hbm, bf16[128,768]{1,0:T(8,128)(2,1)} %constant.87.clone.t6_hbm), custom_call_target="tpu_custom_call" | custom-call | flops 1073741824 | bytes 4194304 | tf_op jit(solution)/shard_map/x_inverse/pallas_call | solution.py:454
  151.9 4.9 %all-to-all-start.3 = ((f32[32,64,128]{2,1,0:T(8,128)}), f32[32,64,128]{2,1,0:T(8,128)S(1)}, u32[]{:S(2)}, u32[]{:S(2)}) async-start(f32[32,64,128]{2,1,0:T(8,128)} %x_inverse.1), calls=%async_computation.3 | async-start | bytes 2097152 | tf_op jit(solution)/shard_map/all_to_all | solution.py:733
  156.8 2.0 %add_multiply_fusion = (f32[1,128,1024]{2,1,0:T(8,128)S(1)}, f32[1,128,1024]{2,1,0:T(8,128)S(1)}) fusion(f32[1024]{0:T(1024)S(1)} %bitcast.53, f32[1024]{0:T(1024)S(1)} %bitcast.52, f32[1024]{0:T(1024)S(1)} %get-tuple-element.53, f32[128]{0:T(128)S(1)} %add_multiply_fusion.1), kind=kLoop, calls=%fused_computation.15 | loop fusion | flops 1310720 | bytes 1061376 | tf_op jit(solution)/shard_map/mul | solution.py:742
  159.0 5.6 %backproject.1 = f32[2,128,1024]{2,1,0:T(8,128)} custom-call(f32[2,128,1024]{2,1,0:T(8,128)S(1)} %pad_maximum_fusion.2.weight_ref, f32[2,32,1024]{2,1,0:T(8,128)S(1)} %get-tuple-element.57.ea_ref, f32[2,32,1024]{2,1,0:T(8,128)S(1)} %copy-done.3), custom_call_target="tpu_custom_call" | custom-call | flops 3221225472 | bytes 4194304 | tf_op jit(solution)/shard_map/backproject/pallas_call | solution.py:647
  165.1 8.0 %all-to-all-done.3 = f32[32,64,128]{2,1,0:T(8,128)S(1)} async-done(((f32[32,64,128]{2,1,0:T(8,128)}), f32[32,64,128]{2,1,0:T(8,128)S(1)}, u32[]{:S(2)}, u32[]{:S(2)}) %all-to-all-start.3) | async-done | bytes 1048608 | tf_op jit(solution)/shard_map/all_to_all | solution.py:733
  (54 shorter events, 18.6 us)
Async XLA Ops:
  2.9 25.8 %all-to-all-start = ((f32[32,64,128]{2,1,0:T(8,128)}), f32[32,64,128]{2,1,0:T(8,128)S(1)}, u32[]{:S(2)}, u32[]{:S(2)}) async-start(f32[32,64,128]{2,1,0:T(8,128)} %bitcast.49), calls=%async_computation | async-start | bytes 2097152 | tf_op jit(solution)/shard_map/all_to_all | solution.py:695
  12.3 6.3 %copy-start.7 = (f32[1024]{0:T(1024)S(1)}, f32[1024]{0:T(1024)}, u32[]{:S(2)}) copy-start(f32[1024]{0:T(1024)} %param.21) | copy-start | bytes 12292
  15.6 74.5 %collective-permute-start.6 = (f32[2,2,1024,128]{3,2,1,0:T(8,128)}, f32[2,2,1024,128]{3,2,1,0:T(8,128)}, u32[]{:S(2)}, u32[]{:S(2)}) collective-permute-start(f32[2,2,1024,128]{3,2,1,0:T(8,128)} %pack_far.1), channel_id=1, source_target_pairs={{0,2},{1,3},{2,0},{3,1},{4,6},{5,7},{6,4},{7,5},{8,10},{9,11},{10,... | collective-permute-start | bytes 6291464 | tf_op jit(solution)/shard_map/ppermute | solution.py:690
  19.6 7.1 %copy-start.2 = (f32[2,32,1024]{2,1,0:T(8,128)}, f32[2,32,1024]{2,1,0:T(8,128)S(1)}, u32[]{:S(2)}) copy-start(f32[2,32,1024]{2,1,0:T(8,128)S(1)} %get-tuple-element.58.eb_ref) | copy-start | bytes 786436
  35.8 5.2 %collective-permute-start.2 = (f32[8,1024]{1,0:T(8,128)S(1)}, f32[8,1024]{1,0:T(8,128)S(1)}, u32[]{:S(2)}, u32[]{:S(2)}) collective-permute-start(f32[8,1024]{1,0:T(8,128)S(1)} %project.1), channel_id=1, source_target_pairs={{0,12},{4,8},{8,4},{12,0},{16,28},{20,24},{24,20},{28,16},{32,44},... | collective-permute-start | bytes 98312 | tf_op jit(solution)/shard_map/ppermute | solution.py:672
  37.0 5.4 %collective-permute-start.1 = (f32[8,1024]{1,0:T(8,128)S(1)}, f32[8,1024]{1,0:T(8,128)S(1)}, u32[]{:S(2)}, u32[]{:S(2)}) collective-permute-start(f32[8,1024]{1,0:T(8,128)S(1)} %project.1), channel_id=1, source_target_pairs={{0,8},{4,12},{8,0},{12,4},{16,24},{20,28},{24,16},{28,20},{32,40},... | collective-permute-start | bytes 98312 | tf_op jit(solution)/shard_map/ppermute | solution.py:672
  38.9 3.9 %collective-permute-start = (f32[8,1024]{1,0:T(8,128)S(1)}, f32[8,1024]{1,0:T(8,128)S(1)}, u32[]{:S(2)}, u32[]{:S(2)}) collective-permute-start(f32[8,1024]{1,0:T(8,128)S(1)} %project.1), channel_id=1, source_target_pairs={{0,4},{4,0},{8,12},{12,8},{16,20},{20,16},{24,28},{28,24},{32,36},... | collective-permute-start | bytes 98312 | tf_op jit(solution)/shard_map/ppermute | solution.py:672
  46.1 44.0 %collective-permute-start.7 = (f32[2,1024,128]{2,1,0:T(8,128)}, f32[2,1024,128]{2,1,0:T(8,128)}, u32[]{:S(2)}, u32[]{:S(2)}) collective-permute-start(f32[2,1024,128]{2,1,0:T(8,128)} %get-tuple-element.29), channel_id=1, source_target_pairs={{0,1},{1,0},{2,3},{3,2},{4,5},{5,4},{6,7},{7,6},{8,9},{9,8},{10,11... | collective-permute-start | bytes 3145736 | tf_op jit(solution)/shard_map/ppermute | solution.py:690
  46.1 51.7 %all-to-all-start.1 = ((f32[128,32,128]{2,1,0:T(8,128)}), f32[128,32,128]{2,1,0:T(8,128)S(1)}, u32[]{:S(2)}, u32[]{:S(2)}) async-start(f32[128,32,128]{2,1,0:T(8,128)} %bitcast.50), calls=%async_computation.1 | async-start | bytes 4194304 | tf_op jit(solution)/shard_map/all_to_all | solution.py:708
  54.4 26.4 %collective-permute-start.5 = (f32[8,1024]{1,0:T(8,128)S(1)}, f32[8,1024]{1,0:T(8,128)S(1)}, u32[]{:S(2)}, u32[]{:S(2)}) collective-permute-start(f32[8,1024]{1,0:T(8,128)S(1)} %add_add_fusion.1), channel_id=1, source_target_pairs={{0,96},{4,100},{8,104},{12,108},{16,112},{20,116},{24,120},{28,124... | collective-permute-start | bytes 98312 | tf_op jit(solution)/shard_map/ppermute | solution.py:672
  56.7 24.1 %collective-permute-start.4 = (f32[8,1024]{1,0:T(8,128)S(1)}, f32[8,1024]{1,0:T(8,128)S(1)}, u32[]{:S(2)}, u32[]{:S(2)}) collective-permute-start(f32[8,1024]{1,0:T(8,128)S(1)} %add_add_fusion.1), channel_id=1, source_target_pairs={{0,64},{4,68},{8,72},{12,76},{16,80},{20,84},{24,88},{28,92},{32,9... | collective-permute-start | bytes 98312 | tf_op jit(solution)/shard_map/ppermute | solution.py:672
  57.5 23.3 %collective-permute-start.3 = (f32[8,1024]{1,0:T(8,128)S(1)}, f32[8,1024]{1,0:T(8,128)S(1)}, u32[]{:S(2)}, u32[]{:S(2)}) collective-permute-start(f32[8,1024]{1,0:T(8,128)S(1)} %add_add_fusion.1), channel_id=1, source_target_pairs={{0,32},{4,36},{8,40},{12,44},{16,48},{20,52},{24,56},{28,60},{32,0... | collective-permute-start | bytes 98312 | tf_op jit(solution)/shard_map/ppermute | solution.py:672
  92.2 5.7 %collective-permute-start.9 = (f32[2,1024,128]{2,1,0:T(8,128)}, f32[2,1024,128]{2,1,0:T(8,128)}, u32[]{:S(2)}, u32[]{:S(2)}) collective-permute-start(f32[2,1024,128]{2,1,0:T(8,128)} %second.1), channel_id=1, source_target_pairs={{0,1},{1,0},{2,3},{3,2},{4,5},{5,4},{6,7},{7,6},{8,9},{9,8},{10,11... | collective-permute-start | bytes 3145736 | tf_op jit(solution)/shard_map/ppermute | solution.py:690
  92.2 2.3 %collective-permute-start.8 = (f32[8,1024]{1,0:T(8,128)S(1)}, f32[8,1024]{1,0:T(8,128)S(1)}, u32[]{:S(2)}, u32[]{:S(2)}) collective-permute-start(f32[8,1024]{1,0:T(8,128)S(1)} %add_add_fusion), channel_id=1, source_target_pairs={{0,1},{1,0},{2,3},{3,2},{4,5},{5,4},{6,7},{7,6},{8,9},{9,8},{10,11... | collective-permute-start | bytes 98312 | tf_op jit(solution)/shard_map/ppermute | solution.py:672
  111.5 31.5 %copy-start.6 = (f32[1,2,1024]{2,1,0:T(2,128)S(1)}, f32[1,2,1024]{2,1,0:T(2,128)}, u32[]{:S(2)}) copy-start(f32[1,2,1024]{2,1,0:T(2,128)} %param.22) | copy-start | bytes 24580
  111.5 35.3 %all-to-all-start.2 = ((f32[128,32,128]{2,1,0:T(8,128)}), f32[128,32,128]{2,1,0:T(8,128)S(1)}, u32[]{:S(2)}, u32[]{:S(2)}) async-start(f32[128,32,128]{2,1,0:T(8,128)} %middle.1), calls=%async_computation.2 | async-start | bytes 4194304 | tf_op jit(solution)/shard_map/all_to_all | solution.py:721
  117.1 25.9 %collective-permute-start.12 = (f32[8,1024]{1,0:T(8,128)S(1)}, f32[8,1024]{1,0:T(8,128)S(1)}, u32[]{:S(2)}, u32[]{:S(2)}) collective-permute-start(f32[8,1024]{1,0:T(8,128)S(1)} %add.112), channel_id=1, source_target_pairs={{0,18},{1,19},{2,16},{3,17},{4,22},{5,23},{6,20},{7,21},{8,26},{9,... | collective-permute-start | bytes 98312 | tf_op jit(solution)/shard_map/ppermute | solution.py:672
  119.4 23.6 %collective-permute-start.11 = (f32[8,1024]{1,0:T(8,128)S(1)}, f32[8,1024]{1,0:T(8,128)S(1)}, u32[]{:S(2)}, u32[]{:S(2)}) collective-permute-start(f32[8,1024]{1,0:T(8,128)S(1)} %add.112), channel_id=1, source_target_pairs={{0,16},{1,17},{2,18},{3,19},{4,20},{5,21},{6,22},{7,23},{8,24},{9,... | collective-permute-start | bytes 98312 | tf_op jit(solution)/shard_map/ppermute | solution.py:672
  119.6 23.4 %collective-permute-start.10 = (f32[8,1024]{1,0:T(8,128)S(1)}, f32[8,1024]{1,0:T(8,128)S(1)}, u32[]{:S(2)}, u32[]{:S(2)}) collective-permute-start(f32[8,1024]{1,0:T(8,128)S(1)} %add.112), channel_id=1, source_target_pairs={{0,2},{1,3},{2,0},{3,1},{4,6},{5,7},{6,4},{7,5},{8,10},{9,11},{10,... | collective-permute-start | bytes 98312 | tf_op jit(solution)/shard_map/ppermute | solution.py:672
  143.0 8.9 %copy-start.5 = (f32[1,2,1024]{2,1,0:T(2,128)}, f32[1,2,1024]{2,1,0:T(2,128)S(1)}, u32[]{:S(2)}) copy-start(f32[1,2,1024]{2,1,0:T(2,128)S(1)} %fusion.8) | copy-start | bytes 24580
  151.9 21.2 %all-to-all-start.3 = ((f32[32,64,128]{2,1,0:T(8,128)}), f32[32,64,128]{2,1,0:T(8,128)S(1)}, u32[]{:S(2)}, u32[]{:S(2)}) async-start(f32[32,64,128]{2,1,0:T(8,128)} %x_inverse.1), calls=%async_computation.3 | async-start | bytes 2097152 | tf_op jit(solution)/shard_map/all_to_all | solution.py:733
  156.8 2.2 %copy-start.3 = (f32[2,32,1024]{2,1,0:T(8,128)S(1)}, f32[2,32,1024]{2,1,0:T(8,128)}, u32[]{:S(2)}) copy-start(f32[2,32,1024]{2,1,0:T(8,128)} %copy-done.2) | copy-start | bytes 786436
  159.0 5.7 %copy-start.1 = (f32[2,128,1024]{2,1,0:T(8,128)S(1)}, f32[2,128,1024]{2,1,0:T(8,128)}, u32[]{:S(2)}) copy-start(f32[2,128,1024]{2,1,0:T(8,128)} %contrast_ref) | copy-start | bytes 3145732
  159.0 5.7 %copy-start.4 = (f32[1,2,128,1024]{3,2,1,0:T(8,128)S(1)}, f32[1,2,128,1024]{3,2,1,0:T(8,128)}, u32[]{:S(2)}) copy-start(f32[1,2,128,1024]{3,2,1,0:T(8,128)} %param.18) | copy-start | bytes 3145732
  (1 other events, 2.1 us)

commit v5 on v4

--- a/solution.py
+++ b/solution.py
@@ -277,19 +277,10 @@
     for copy in copies[:3]:
         copy.wait()
     sign = 1.0 - 2.0 * flip.astype(f32)
-
-    def advance():
-        sr = step_ref[0] * sign
-        si = step_ref[1] * sign
-        nr = now_ref[0]
-        ni = now_ref[1]
-        now_ref[0] = nr * sr - ni * si
-        now_ref[1] = nr * si + ni * sr
-
-    now_ref[...] = tw_ref[...]
-
-    @pl.loop(0, 8, unroll=8)
-    def _(cc):
+    step_ref[...] = step_ref[...] * sign
+    now_ref[0] = tw_ref[...]
+
+    for cc in range(8):
         columns = []
         for half in range(2):
             re = a_ref[pl.ds(2 * cc + half, 128, stride=32), :]
@@ -299,11 +290,14 @@
         for half in range(2):
             ur = u[:256, 128 * half : 128 * half + 128]
             ui = u[256:, 128 * half : 128 * half + 128]
-            nr = now_ref[0]
-            ni = now_ref[1]
-            u_ref[2 * cc + half, 0] = ur * nr - ui * ni
-            u_ref[2 * cc + half, 1] = ur * ni + ui * nr
-            advance()
+            c = 2 * cc + half
+            nr = now_ref[c, 0]
+            ni = now_ref[c, 1]
+            u_ref[c, 0, :256, :] = ur * nr - ui * ni
+            u_ref[c, 1, :256, :] = ur * ni + ui * nr
+            if c < 15:
+                now_ref[c + 1, 0] = nr * step_ref[0] - ni * step_ref[1]
+                now_ref[c + 1, 1] = nr * step_ref[1] + ni * step_ref[0]
 
     for copy in copies[3:]:
         copy.wait()
@@ -348,29 +342,26 @@
             u_ref[c, 0, rows, :] = re
             u_ref[c, 1, rows, :] = im
 
-    now_ref[...] = tw_ref[...]
-
     halves = []
     for cc in range(8):
         columns = []
         for half in range(2):
-            ur = u_ref[2 * cc + half, 0]
-            ui = u_ref[2 * cc + half, 1]
-            nr = now_ref[0]
-            ni = now_ref[1]
+            ur = u_ref[2 * cc + half, 0, :256, :]
+            ui = u_ref[2 * cc + half, 1, :256, :]
+            nr = now_ref[2 * cc + half, 0]
+            ni = now_ref[2 * cc + half, 1]
             columns.append(jnp.concatenate([ur * nr + ui * ni, ui * nr - ur * ni], 0))
-            advance()
         out = dot3(t4_ref[...], jnp.concatenate(columns, 1))
         for half in range(2):
             lanes = slice(128 * half, 128 * half + 128)
             row = line_row(2 * cc + half)
-            out_ref[pl.ds(row, 128, stride=32), :] = out[:128, lanes]
-            out_ref[pl.ds(row + 8, 128, stride=32), :] = out[128:, lanes]
+            out_ref[pl.ds(row, 128, stride=40), :] = out[:128, lanes]
+            out_ref[pl.ds(row + 8, 128, stride=40), :] = out[128:, lanes]
         if cc % 4 == 3:
             rows = pl.ds(cc // 4 * 16, 16)
             halves.append(
                 pltpu.make_async_copy(
-                    out_ref.reshape(128, 32, 128).at[:, rows], out_hbm.at[:, rows], sent.at[cc // 4]
+                    out_ref.reshape(128, 40, 128).at[:, rows], out_hbm.at[:, rows], sent.at[cc // 4]
                 )
             )
             halves[-1].start()
@@ -392,13 +383,13 @@
             pltpu.VMEM((2, 2, 2, 1024, 128), f32),
             pltpu.VMEM((2, 2, 8, 128), f32),
             pltpu.VMEM((256, 1536), bf16),
+            pltpu.VMEM((16, 2, 264, 128), f32),
             pltpu.VMEM((16, 2, 256, 128), f32),
-            pltpu.VMEM((2, 256, 128), f32),
-            pltpu.VMEM((4096, 128), f32),
+            pltpu.VMEM((5120, 128), f32),
             pltpu.SemaphoreType.DMA((9,)),
             pltpu.SemaphoreType.DMA((2,)),
         ],
-        compiler_params=params(24),
+        compiler_params=params(28),
         cost_estimate=cost(2 * 8 * 2 * 512 * 65536 * 3, 10 << 20),
         name="middle",
     )(
@@ -435,13 +426,13 @@
             lanes = slice(128 * half, 128 * half + 128)
             for b0 in range(2):
                 row = line_row(4 * cc + 2 * half + b0)
-                out_ref[pl.ds(row, 32, stride=64), :] = out[64 * b0 : 64 * b0 + 32, lanes]
-                out_ref[pl.ds(row + 8, 32, stride=64), :] = out[64 * b0 + 32 : 64 * b0 + 64, lanes]
+                out_ref[pl.ds(row, 32, stride=72), :] = out[64 * b0 : 64 * b0 + 32, lanes]
+                out_ref[pl.ds(row + 8, 32, stride=72), :] = out[64 * b0 + 32 : 64 * b0 + 64, lanes]
         if cc % 2 == 1:
             rows = pl.ds(cc // 2 * 16, 16)
             blocks.append(
                 pltpu.make_async_copy(
-                    out_ref.reshape(32, 64, 128).at[:, rows], out_hbm.at[:, rows], sent.at[cc // 2]
+                    out_ref.reshape(32, 72, 128).at[:, rows], out_hbm.at[:, rows], sent.at[cc // 2]
                 )
             )
             blocks[-1].start()
@@ -460,7 +451,7 @@
             pltpu.VMEM((256, 768), bf16),
             pltpu.VMEM((2, 128, 128), f32),
             pltpu.VMEM((128, 768), bf16),
-            pltpu.VMEM((2048, 128), f32),
+            pltpu.VMEM((2304, 128), f32),
             pltpu.SemaphoreType.DMA((3,)),
             pltpu.SemaphoreType.DMA((4,)),
         ],

time: 175 us -> 173 us (0.989)
  Pallas kernels: 48.9 us -> 46.7 us
    pallas_call x1, Pallas kernels: 13.6 us -> 11.9 us  [middle(): pl.pallas_call(middle_kernel, in_specs=[pl.BlockSpec(memory_space=pltpu.S...]
where the time goes in v5:
time: 173 us; the launch traced here: 172 us
  waiting for transfers between devices  74.3 us (43%)
  Pallas kernels  46.7 us (27%)
  starting transfers between devices  44.5 us (26%)
  other arithmetic  5.76 us (3%)
    ppermute x10, waiting for transfers between devices, exchange(): lax.ppermute(value, axis, [(j, j ^ stride) for j in range(size)])  48 us
    all_to_all x2, starting transfers between devices, local(): lax.all_to_all(lines.reshape(WIDE, 64, 128), 'wide', 0, 0, tiled=True)  14.2 us
    all_to_all x2, starting transfers between devices, local(): lax.all_to_all(lines.reshape(128, 32, 128), ('wide', 'narrow'), 0, 0, til...  13.8 us
    ppermute x10, starting transfers between devices, exchange(): lax.ppermute(value, axis, [(j, j ^ stride) for j in range(size)])  13.6 us
    pallas_call x1, Pallas kernels, middle(): pl.pallas_call(middle_kernel, in_specs=[pl.BlockSpec(memory_space=pltpu.S...  11.9 us
    all_to_all x2, waiting for transfers between devices, local(): lax.all_to_all(lines.reshape(WIDE, 64, 128), 'wide', 0, 0, tiled=True)  9.94 us
    ppermute x3, waiting for transfers between devices, partner(): return lax.ppermute(value, 'narrow', [(j, j ^ k) for j in range(NARROW)])  9.36 us
    pallas_call x1, Pallas kernels, x_forward(): pl.pallas_call(x_forward_kernel, in_specs=[spec_vmem()] + [spec_hbm()] *...  7.09 us
  transfers between devices with their start and end apart: 17, of which 11 were waited for; matrix products, arithmetic and copies ran while one was open for 3% of the time, Pallas kernels for 15%

profile of v5, /device:TPU:0, one launch (start us, length us, event | category | flops | bytes accessed | tf_op | source)
XLA Modules:
  0.0 172.3 jit_solution(7664750181374445000)
XLA Ops:
  0.6 2.3 %columns_major.1 = f32[2048,128]{1,0:T(8,128)} custom-call(f32[2,128,1024]{2,1,0:T(8,128)} %bitcast.41), custom_call_target="tpu_custom_call" | custom-call | bytes 2097152 | tf_op jit(solution)/shard_map/columns_major/pallas_call | solution.py:194
  2.9 9.3 %all-to-all-start = ((f32[32,64,128]{2,1,0:T(8,128)}), f32[32,64,128]{2,1,0:T(8,128)S(1)}, u32[]{:S(2)}, u32[]{:S(2)}) async-start(f32[32,64,128]{2,1,0:T(8,128)} %bitcast.49), calls=%async_computation | async-start | bytes 2097152 | tf_op jit(solution)/shard_map/all_to_all | solution.py:686
  12.3 3.4 %pack_far.1 = f32[2,2,1024,128]{3,2,1,0:T(8,128)} custom-call(s32[2]{0:T(128)S(1)} %pad_add_fusion.place_ref, f32[2,2,1024,256]{3,2,1,0:T(8,128)} %bitcast.47), custom_call_target="tpu_custom_call" | custom-call | bytes 4194304 | tf_op jit(solution)/shard_map/pack_far/pallas_call | solution.py:524
  15.6 2.9 %collective-permute-start.6 = (f32[2,2,1024,128]{3,2,1,0:T(8,128)}, f32[2,2,1024,128]{3,2,1,0:T(8,128)}, u32[]{:S(2)}, u32[]{:S(2)}) collective-permute-start(f32[2,2,1024,128]{3,2,1,0:T(8,128)} %pack_far.1), channel_id=1, source_target_pairs={{0,2},{1,3},{2,0},{3,1},{4,6},{5,7},{6,4},{7,5},{8,10},{9,11},{10,... | collective-permute-start | bytes 6291464 | tf_op jit(solution)/shard_map/ppermute | solution.py:681
  21.7 5.0 %project.1 = f32[8,1024]{1,0:T(8,128)S(1)} custom-call(f32[2,128,1024]{2,1,0:T(8,128)S(1)} %bitcast.42, f32[2,32,1024]{2,1,0:T(8,128)S(1)} %get-tuple-element.57.ea_ref, f32[2,32,1024]{2,1,0:T(8,128)S(1)} %get-tuple-element.58.eb_ref, f32[2,128,1024]{2,1,0:T(8,128)S(1)} %pad_maximum_fusion.row_ref), custom_call_target="tpu_custom_call" | custom-call | flops 3221225472 | bytes 4194304 | tf_op jit(solution)/shard_map/project/pallas_call | solution.py:590
  28.7 7.1 %x_forward.1 = f32[4096,128]{1,0:T(8,128)} custom-call(f32[2048,128]{1,0:T(8,128)S(1)} %bitcast.46, bf16[128,192]{1,0:T(8,128)(2,1)} %constant.77.clone.t1_hbm, f32[2,64,128]{2,1,0:T(8,128)} %constant.78.clone.tw_hbm, bf16[256,768]{1,0:T(8,128)(2,1)} %constant.79.clone.t2_hbm), custom_call_target="tpu_custom_call" | custom-call | flops 1073741824 | bytes 4194304 | tf_op jit(solution)/shard_map/x_forward/pallas_call | solution.py:240
  42.8 3.3 %pack_near.1 = (f32[2,1024,128]{2,1,0:T(8,128)}, f32[2,1024,128]{2,1,0:T(8,128)}) custom-call(s32[2]{0:T(128)S(1)} %pad_add_fusion.place_ref, f32[2,2,1024,256]{3,2,1,0:T(8,128)} %bitcast.48), custom_call_target="tpu_custom_call" | custom-call | bytes 4194304 | tf_op jit(solution)/shard_map/pack_near/pallas_call | solution.py:524
  46.1 8.3 %all-to-all-start.1 = ((f32[128,32,128]{2,1,0:T(8,128)}), f32[128,32,128]{2,1,0:T(8,128)S(1)}, u32[]{:S(2)}, u32[]{:S(2)}) async-start(f32[128,32,128]{2,1,0:T(8,128)} %bitcast.50), calls=%async_computation.1 | async-start | bytes 4194304 | tf_op jit(solution)/shard_map/all_to_all | solution.py:699
  54.4 2.3 %collective-permute-start.5 = (f32[8,1024]{1,0:T(8,128)S(1)}, f32[8,1024]{1,0:T(8,128)S(1)}, u32[]{:S(2)}, u32[]{:S(2)}) collective-permute-start(f32[8,1024]{1,0:T(8,128)S(1)} %add_add_fusion.1), channel_id=1, source_target_pairs={{0,96},{4,100},{8,104},{12,108},{16,112},{20,116},{24,120},{28,124... | collective-permute-start | bytes 98312 | tf_op jit(solution)/shard_map/ppermute | solution.py:663
  58.6 22.2 %collective-permute-done.5 = f32[8,1024]{1,0:T(8,128)S(1)} collective-permute-done((f32[8,1024]{1,0:T(8,128)S(1)}, f32[8,1024]{1,0:T(8,128)S(1)}, u32[]{:S(2)}, u32[]{:S(2)}) %collective-permute-start.5) | collective-permute-done | bytes 32800 | tf_op jit(solution)/shard_map/ppermute | solution.py:663
  80.8 9.4 %collective-permute-done.6.in_ref.r2_hbm = f32[2,2,1024,128]{3,2,1,0:T(8,128)} collective-permute-done((f32[2,2,1024,128]{3,2,1,0:T(8,128)}, f32[2,2,1024,128]{3,2,1,0:T(8,128)}, u32[]{:S(2)}, u32[]{:S(2)}) %collective-permute-start.6) | collective-permute-done | bytes 2097184 | tf_op jit(solution)/shard_map/ppermute | solution.py:681
  90.2 2.0 %second.1 = f32[2,1024,128]{2,1,0:T(8,128)} custom-call(f32[2,2,1024,128]{3,2,1,0:T(8,128)} %collective-permute-done.6.in_ref.r2_hbm), custom_call_target="tpu_custom_call" | custom-call | bytes 2097152 | tf_op jit(solution)/shard_map/second/pallas_call | solution.py:544
  94.5 3.3 %all-to-all-done.1 = f32[128,32,128]{2,1,0:T(8,128)S(1)} async-done(((f32[128,32,128]{2,1,0:T(8,128)}), f32[128,32,128]{2,1,0:T(8,128)S(1)}, u32[]{:S(2)}, u32[]{:S(2)}) %all-to-all-start.1) | async-done | bytes 2097184 | tf_op jit(solution)/shard_map/all_to_all | solution.py:699
  97.9 11.9 %middle.1 = f32[128,32,128]{2,1,0:T(8,128)} custom-call(s32[2]{0:T(128)S(1)} %pad_add_fusion.place_ref, f32[4096,128]{1,0:T(8,128)S(1)} %bitcast.44, bf16[512,768]{1,0:T(8,128)(2,1)} %constant.80.clone.t3_hbm, f32[2,256,128]{2,1,0:T(8,128)} %constant.81.clone.tw_hbm, f32[2,256,128]{2,1,0:T(8,128)} %constant.82.clone.step_hbm, ...), custom_call_target="tpu_custom_call" | custom-call | flops 3221225472 | bytes 10485760 | tf_op jit(solution)/shard_map/middle/pallas_call | solution.py:374
  109.7 5.5 %all-to-all-start.2 = ((f32[128,32,128]{2,1,0:T(8,128)}), f32[128,32,128]{2,1,0:T(8,128)S(1)}, u32[]{:S(2)}, u32[]{:S(2)}) async-start(f32[128,32,128]{2,1,0:T(8,128)} %middle.1), calls=%async_computation.2 | async-start | bytes 4194304 | tf_op jit(solution)/shard_map/all_to_all | solution.py:712
  115.3 2.3 %collective-permute-start.12 = (f32[8,1024]{1,0:T(8,128)S(1)}, f32[8,1024]{1,0:T(8,128)S(1)}, u32[]{:S(2)}, u32[]{:S(2)}) collective-permute-start(f32[8,1024]{1,0:T(8,128)S(1)} %add.112), channel_id=1, source_target_pairs={{0,18},{1,19},{2,16},{3,17},{4,22},{5,23},{6,20},{7,21},{8,26},{9,... | collective-permute-start | bytes 98312 | tf_op jit(solution)/shard_map/ppermute | solution.py:663
  117.8 2.3 %collective-permute-start.10 = (f32[8,1024]{1,0:T(8,128)S(1)}, f32[8,1024]{1,0:T(8,128)S(1)}, u32[]{:S(2)}, u32[]{:S(2)}) collective-permute-start(f32[8,1024]{1,0:T(8,128)S(1)} %add.112), channel_id=1, source_target_pairs={{0,2},{1,3},{2,0},{3,1},{4,6},{5,7},{6,4},{7,5},{8,10},{9,11},{10,... | collective-permute-start | bytes 98312 | tf_op jit(solution)/shard_map/ppermute | solution.py:663
  120.1 21.1 %collective-permute-done.12 = f32[8,1024]{1,0:T(8,128)S(1)} collective-permute-done((f32[8,1024]{1,0:T(8,128)S(1)}, f32[8,1024]{1,0:T(8,128)S(1)}, u32[]{:S(2)}, u32[]{:S(2)}) %collective-permute-start.12) | collective-permute-done | bytes 32800 | tf_op jit(solution)/shard_map/ppermute | solution.py:663
  141.3 3.7 %all-to-all-done.2 = f32[128,32,128]{2,1,0:T(8,128)S(1)} async-done(((f32[128,32,128]{2,1,0:T(8,128)}), f32[128,32,128]{2,1,0:T(8,128)S(1)}, u32[]{:S(2)}, u32[]{:S(2)}) %all-to-all-start.2) | async-done | bytes 2097184 | tf_op jit(solution)/shard_map/all_to_all | solution.py:712
  145.0 4.7 %x_inverse.1 = f32[32,64,128]{2,1,0:T(8,128)} custom-call(f32[4096,128]{1,0:T(8,128)S(1)} %bitcast.45, bf16[256,768]{1,0:T(8,128)(2,1)} %constant.85.clone.t5_hbm, f32[2,128,128]{2,1,0:T(8,128)} %constant.86.clone.tw_hbm, bf16[128,768]{1,0:T(8,128)(2,1)} %constant.87.clone.t6_hbm), custom_call_target="tpu_custom_call" | custom-call | flops 1073741824 | bytes 4194304 | tf_op jit(solution)/shard_map/x_inverse/pallas_call | solution.py:445
  149.7 4.9 %all-to-all-start.3 = ((f32[32,64,128]{2,1,0:T(8,128)}), f32[32,64,128]{2,1,0:T(8,128)S(1)}, u32[]{:S(2)}, u32[]{:S(2)}) async-start(f32[32,64,128]{2,1,0:T(8,128)} %x_inverse.1), calls=%async_computation.3 | async-start | bytes 2097152 | tf_op jit(solution)/shard_map/all_to_all | solution.py:724
  154.7 2.0 %add_multiply_fusion = (f32[1,128,1024]{2,1,0:T(8,128)S(1)}, f32[1,128,1024]{2,1,0:T(8,128)S(1)}) fusion(f32[1024]{0:T(1024)S(1)} %bitcast.53, f32[1024]{0:T(1024)S(1)} %bitcast.52, f32[1024]{0:T(1024)S(1)} %get-tuple-element.53, f32[128]{0:T(128)S(1)} %add_multiply_fusion.1), kind=kLoop, calls=%fused_computation.15 | loop fusion | flops 1310720 | bytes 1061376 | tf_op jit(solution)/shard_map/mul | solution.py:733
  156.9 5.6 %backproject.1 = f32[2,128,1024]{2,1,0:T(8,128)} custom-call(f32[2,128,1024]{2,1,0:T(8,128)S(1)} %pad_maximum_fusion.2.weight_ref, f32[2,32,1024]{2,1,0:T(8,128)S(1)} %get-tuple-element.57.ea_ref, f32[2,32,1024]{2,1,0:T(8,128)S(1)} %copy-done.3), custom_call_target="tpu_custom_call" | custom-call | flops 3221225472 | bytes 4194304 | tf_op jit(solution)/shard_map/backproject/pallas_call | solution.py:638
  163.0 8.0 %all-to-all-done.3 = f32[32,64,128]{2,1,0:T(8,128)S(1)} async-done(((f32[32,64,128]{2,1,0:T(8,128)}), f32[32,64,128]{2,1,0:T(8,128)S(1)}, u32[]{:S(2)}, u32[]{:S(2)}) %all-to-all-start.3) | async-done | bytes 1048608 | tf_op jit(solution)/shard_map/all_to_all | solution.py:724
  (54 shorter events, 18.6 us)
Async XLA Ops:
  2.9 25.8 %all-to-all-start = ((f32[32,64,128]{2,1,0:T(8,128)}), f32[32,64,128]{2,1,0:T(8,128)S(1)}, u32[]{:S(2)}, u32[]{:S(2)}) async-start(f32[32,64,128]{2,1,0:T(8,128)} %bitcast.49), calls=%async_computation | async-start | bytes 2097152 | tf_op jit(solution)/shard_map/all_to_all | solution.py:686
  12.3 6.3 %copy-start.7 = (f32[1024]{0:T(1024)S(1)}, f32[1024]{0:T(1024)}, u32[]{:S(2)}) copy-start(f32[1024]{0:T(1024)} %param.21) | copy-start | bytes 12292
  15.6 74.5 %collective-permute-start.6 = (f32[2,2,1024,128]{3,2,1,0:T(8,128)}, f32[2,2,1024,128]{3,2,1,0:T(8,128)}, u32[]{:S(2)}, u32[]{:S(2)}) collective-permute-start(f32[2,2,1024,128]{3,2,1,0:T(8,128)} %pack_far.1), channel_id=1, source_target_pairs={{0,2},{1,3},{2,0},{3,1},{4,6},{5,7},{6,4},{7,5},{8,10},{9,11},{10,... | collective-permute-start | bytes 6291464 | tf_op jit(solution)/shard_map/ppermute | solution.py:681
  19.6 7.1 %copy-start.2 = (f32[2,32,1024]{2,1,0:T(8,128)}, f32[2,32,1024]{2,1,0:T(8,128)S(1)}, u32[]{:S(2)}) copy-start(f32[2,32,1024]{2,1,0:T(8,128)S(1)} %get-tuple-element.58.eb_ref) | copy-start | bytes 786436
  35.8 5.2 %collective-permute-start.2 = (f32[8,1024]{1,0:T(8,128)S(1)}, f32[8,1024]{1,0:T(8,128)S(1)}, u32[]{:S(2)}, u32[]{:S(2)}) collective-permute-start(f32[8,1024]{1,0:T(8,128)S(1)} %project.1), channel_id=1, source_target_pairs={{0,12},{4,8},{8,4},{12,0},{16,28},{20,24},{24,20},{28,16},{32,44},... | collective-permute-start | bytes 98312 | tf_op jit(solution)/shard_map/ppermute | solution.py:663
  37.0 5.4 %collective-permute-start.1 = (f32[8,1024]{1,0:T(8,128)S(1)}, f32[8,1024]{1,0:T(8,128)S(1)}, u32[]{:S(2)}, u32[]{:S(2)}) collective-permute-start(f32[8,1024]{1,0:T(8,128)S(1)} %project.1), channel_id=1, source_target_pairs={{0,8},{4,12},{8,0},{12,4},{16,24},{20,28},{24,16},{28,20},{32,40},... | collective-permute-start | bytes 98312 | tf_op jit(solution)/shard_map/ppermute | solution.py:663
  38.9 3.9 %collective-permute-start = (f32[8,1024]{1,0:T(8,128)S(1)}, f32[8,1024]{1,0:T(8,128)S(1)}, u32[]{:S(2)}, u32[]{:S(2)}) collective-permute-start(f32[8,1024]{1,0:T(8,128)S(1)} %project.1), channel_id=1, source_target_pairs={{0,4},{4,0},{8,12},{12,8},{16,20},{20,16},{24,28},{28,24},{32,36},... | collective-permute-start | bytes 98312 | tf_op jit(solution)/shard_map/ppermute | solution.py:663
  46.1 44.0 %collective-permute-start.7 = (f32[2,1024,128]{2,1,0:T(8,128)}, f32[2,1024,128]{2,1,0:T(8,128)}, u32[]{:S(2)}, u32[]{:S(2)}) collective-permute-start(f32[2,1024,128]{2,1,0:T(8,128)} %get-tuple-element.29), channel_id=1, source_target_pairs={{0,1},{1,0},{2,3},{3,2},{4,5},{5,4},{6,7},{7,6},{8,9},{9,8},{10,11... | collective-permute-start | bytes 3145736 | tf_op jit(solution)/shard_map/ppermute | solution.py:681
  46.1 51.7 %all-to-all-start.1 = ((f32[128,32,128]{2,1,0:T(8,128)}), f32[128,32,128]{2,1,0:T(8,128)S(1)}, u32[]{:S(2)}, u32[]{:S(2)}) async-start(f32[128,32,128]{2,1,0:T(8,128)} %bitcast.50), calls=%async_computation.1 | async-start | bytes 4194304 | tf_op jit(solution)/shard_map/all_to_all | solution.py:699
  54.4 26.4 %collective-permute-start.5 = (f32[8,1024]{1,0:T(8,128)S(1)}, f32[8,1024]{1,0:T(8,128)S(1)}, u32[]{:S(2)}, u32[]{:S(2)}) collective-permute-start(f32[8,1024]{1,0:T(8,128)S(1)} %add_add_fusion.1), channel_id=1, source_target_pairs={{0,96},{4,100},{8,104},{12,108},{16,112},{20,116},{24,120},{28,124... | collective-permute-start | bytes 98312 | tf_op jit(solution)/shard_map/ppermute | solution.py:663
  56.7 24.1 %collective-permute-start.4 = (f32[8,1024]{1,0:T(8,128)S(1)}, f32[8,1024]{1,0:T(8,128)S(1)}, u32[]{:S(2)}, u32[]{:S(2)}) collective-permute-start(f32[8,1024]{1,0:T(8,128)S(1)} %add_add_fusion.1), channel_id=1, source_target_pairs={{0,64},{4,68},{8,72},{12,76},{16,80},{20,84},{24,88},{28,92},{32,9... | collective-permute-start | bytes 98312 | tf_op jit(solution)/shard_map/ppermute | solution.py:663
  57.5 23.3 %collective-permute-start.3 = (f32[8,1024]{1,0:T(8,128)S(1)}, f32[8,1024]{1,0:T(8,128)S(1)}, u32[]{:S(2)}, u32[]{:S(2)}) collective-permute-start(f32[8,1024]{1,0:T(8,128)S(1)} %add_add_fusion.1), channel_id=1, source_target_pairs={{0,32},{4,36},{8,40},{12,44},{16,48},{20,52},{24,56},{28,60},{32,0... | collective-permute-start | bytes 98312 | tf_op jit(solution)/shard_map/ppermute | solution.py:663
  92.2 5.7 %collective-permute-start.9 = (f32[2,1024,128]{2,1,0:T(8,128)}, f32[2,1024,128]{2,1,0:T(8,128)}, u32[]{:S(2)}, u32[]{:S(2)}) collective-permute-start(f32[2,1024,128]{2,1,0:T(8,128)} %second.1), channel_id=1, source_target_pairs={{0,1},{1,0},{2,3},{3,2},{4,5},{5,4},{6,7},{7,6},{8,9},{9,8},{10,11... | collective-permute-start | bytes 3145736 | tf_op jit(solution)/shard_map/ppermute | solution.py:681
  92.2 2.3 %collective-permute-start.8 = (f32[8,1024]{1,0:T(8,128)S(1)}, f32[8,1024]{1,0:T(8,128)S(1)}, u32[]{:S(2)}, u32[]{:S(2)}) collective-permute-start(f32[8,1024]{1,0:T(8,128)S(1)} %add_add_fusion), channel_id=1, source_target_pairs={{0,1},{1,0},{2,3},{3,2},{4,5},{5,4},{6,7},{7,6},{8,9},{9,8},{10,11... | collective-permute-start | bytes 98312 | tf_op jit(solution)/shard_map/ppermute | solution.py:663
  109.7 31.5 %copy-start.6 = (f32[1,2,1024]{2,1,0:T(2,128)S(1)}, f32[1,2,1024]{2,1,0:T(2,128)}, u32[]{:S(2)}) copy-start(f32[1,2,1024]{2,1,0:T(2,128)} %param.22) | copy-start | bytes 24580
  109.7 35.3 %all-to-all-start.2 = ((f32[128,32,128]{2,1,0:T(8,128)}), f32[128,32,128]{2,1,0:T(8,128)S(1)}, u32[]{:S(2)}, u32[]{:S(2)}) async-start(f32[128,32,128]{2,1,0:T(8,128)} %middle.1), calls=%async_computation.2 | async-start | bytes 4194304 | tf_op jit(solution)/shard_map/all_to_all | solution.py:712
  115.3 25.9 %collective-permute-start.12 = (f32[8,1024]{1,0:T(8,128)S(1)}, f32[8,1024]{1,0:T(8,128)S(1)}, u32[]{:S(2)}, u32[]{:S(2)}) collective-permute-start(f32[8,1024]{1,0:T(8,128)S(1)} %add.112), channel_id=1, source_target_pairs={{0,18},{1,19},{2,16},{3,17},{4,22},{5,23},{6,20},{7,21},{8,26},{9,... | collective-permute-start | bytes 98312 | tf_op jit(solution)/shard_map/ppermute | solution.py:663
  117.6 23.6 %collective-permute-start.11 = (f32[8,1024]{1,0:T(8,128)S(1)}, f32[8,1024]{1,0:T(8,128)S(1)}, u32[]{:S(2)}, u32[]{:S(2)}) collective-permute-start(f32[8,1024]{1,0:T(8,128)S(1)} %add.112), channel_id=1, source_target_pairs={{0,16},{1,17},{2,18},{3,19},{4,20},{5,21},{6,22},{7,23},{8,24},{9,... | collective-permute-start | bytes 98312 | tf_op jit(solution)/shard_map/ppermute | solution.py:663
  117.8 23.4 %collective-permute-start.10 = (f32[8,1024]{1,0:T(8,128)S(1)}, f32[8,1024]{1,0:T(8,128)S(1)}, u32[]{:S(2)}, u32[]{:S(2)}) collective-permute-start(f32[8,1024]{1,0:T(8,128)S(1)} %add.112), channel_id=1, source_target_pairs={{0,2},{1,3},{2,0},{3,1},{4,6},{5,7},{6,4},{7,5},{8,10},{9,11},{10,... | collective-permute-start | bytes 98312 | tf_op jit(solution)/shard_map/ppermute | solution.py:663
  141.2 8.5 %copy-start.5 = (f32[1,2,1024]{2,1,0:T(2,128)}, f32[1,2,1024]{2,1,0:T(2,128)S(1)}, u32[]{:S(2)}) copy-start(f32[1,2,1024]{2,1,0:T(2,128)S(1)} %fusion.8) | copy-start | bytes 24580
  149.7 21.2 %all-to-all-start.3 = ((f32[32,64,128]{2,1,0:T(8,128)}), f32[32,64,128]{2,1,0:T(8,128)S(1)}, u32[]{:S(2)}, u32[]{:S(2)}) async-start(f32[32,64,128]{2,1,0:T(8,128)} %x_inverse.1), calls=%async_computation.3 | async-start | bytes 2097152 | tf_op jit(solution)/shard_map/all_to_all | solution.py:724
  154.6 2.2 %copy-start.3 = (f32[2,32,1024]{2,1,0:T(8,128)S(1)}, f32[2,32,1024]{2,1,0:T(8,128)}, u32[]{:S(2)}) copy-start(f32[2,32,1024]{2,1,0:T(8,128)} %copy-done.2) | copy-start | bytes 786436
  156.8 5.7 %copy-start.1 = (f32[2,128,1024]{2,1,0:T(8,128)S(1)}, f32[2,128,1024]{2,1,0:T(8,128)}, u32[]{:S(2)}) copy-start(f32[2,128,1024]{2,1,0:T(8,128)} %contrast_ref) | copy-start | bytes 3145732
  156.8 5.7 %copy-start.4 = (f32[1,2,128,1024]{3,2,1,0:T(8,128)S(1)}, f32[1,2,128,1024]{3,2,1,0:T(8,128)}, u32[]{:S(2)}) copy-start(f32[1,2,128,1024]{3,2,1,0:T(8,128)} %param.18) | copy-start | bytes 3145732
  (1 other events, 2.1 us)

commit v6 on v5

--- a/solution.py
+++ b/solution.py
@@ -263,10 +263,14 @@
 def middle_kernel(
     place_ref, a_ref, t3_hbm, tw_hbm, step_hbm, r0_hbm, r1_hbm, r2_hbm, r3_hbm, lane_hbm, t4_hbm,
     out_hbm, t3_ref, tw_ref, step_ref, green_ref, lane_ref, t4_ref, u_ref, now_ref, out_ref,
-    arrived, sent,
+    spread_ref, arrived, sent, moved,
 ):
     flip = place_ref[0]
     upper = place_ref[1]
+    spread = pltpu.make_async_copy(
+        a_ref.reshape(128, 32, 128), spread_ref.reshape(128, 40, 128).at[:, pl.ds(0, 32)], moved
+    )
+    spread.start()
     copies = fetch(
         (t3_hbm, tw_hbm, step_hbm, r0_hbm, r1_hbm, r2_hbm.at[0], r3_hbm, lane_hbm, t4_hbm),
         (t3_ref, tw_ref, step_ref)
@@ -276,6 +280,7 @@
     )
     for copy in copies[:3]:
         copy.wait()
+    spread.wait()
     sign = 1.0 - 2.0 * flip.astype(f32)
     step_ref[...] = step_ref[...] * sign
     now_ref[0] = tw_ref[...]
@@ -283,8 +288,8 @@
     for cc in range(8):
         columns = []
         for half in range(2):
-            re = a_ref[pl.ds(2 * cc + half, 128, stride=32), :]
-            im = a_ref[pl.ds(2 * cc + half + 16, 128, stride=32), :]
+            re = spread_ref[pl.ds(2 * cc + half, 128, stride=40), :]
+            im = spread_ref[pl.ds(2 * cc + half + 16, 128, stride=40), :]
             columns.append(jnp.concatenate([re, im], 0))
         u = dot3(t3_ref[...], jnp.concatenate(columns, 1))
         for half in range(2):
@@ -386,10 +391,12 @@
             pltpu.VMEM((16, 2, 264, 128), f32),
             pltpu.VMEM((16, 2, 256, 128), f32),
             pltpu.VMEM((5120, 128), f32),
+            pltpu.VMEM((5120, 128), f32),
             pltpu.SemaphoreType.DMA((9,)),
             pltpu.SemaphoreType.DMA((2,)),
+            pltpu.SemaphoreType.DMA,
         ],
-        compiler_params=params(28),
+        compiler_params=params(32),
         cost_estimate=cost(2 * 8 * 2 * 512 * 65536 * 3, 10 << 20),
         name="middle",
     )(
@@ -398,18 +405,24 @@
 
 
 def x_inverse_kernel(
-    a_ref, t5_hbm, tw_hbm, t6_hbm, out_hbm, t5_ref, tw_ref, t6_ref, out_ref, arrived, sent
+    a_ref, t5_hbm, tw_hbm, t6_hbm, out_hbm, t5_ref, tw_ref, t6_ref, spread_ref, out_ref, arrived,
+    sent, moved,
 ):
+    spread = pltpu.make_async_copy(
+        a_ref.reshape(128, 32, 128), spread_ref.reshape(128, 40, 128).at[:, pl.ds(0, 32)], moved
+    )
+    spread.start()
     for copy in fetch((t5_hbm, tw_hbm, t6_hbm), (t5_ref, tw_ref, t6_ref), arrived):
         copy.wait()
+    spread.wait()
 
     blocks = []
     for cc in range(8):
         columns = []
         for half in range(2):
             row = line_row(2 * cc + half)
-            re = a_ref[pl.ds(row, 128, stride=32), :]
-            im = a_ref[pl.ds(row + 8, 128, stride=32), :]
+            re = spread_ref[pl.ds(row, 128, stride=40), :]
+            im = spread_ref[pl.ds(row + 8, 128, stride=40), :]
             columns.append(jnp.concatenate([re, im], 0))
         u = dot3(t5_ref[...], jnp.concatenate(columns, 1))
         rows = []
@@ -451,11 +464,13 @@
             pltpu.VMEM((256, 768), bf16),
             pltpu.VMEM((2, 128, 128), f32),
             pltpu.VMEM((128, 768), bf16),
+            pltpu.VMEM((5120, 128), f32),
             pltpu.VMEM((2304, 128), f32),
             pltpu.SemaphoreType.DMA((3,)),
             pltpu.SemaphoreType.DMA((4,)),
+            pltpu.SemaphoreType.DMA,
         ],
-        compiler_params=params(8),
+        compiler_params=params(12),
         cost_estimate=cost(2 * 2048 * 65536 * 4, 4 << 20),
         name="x_inverse",
     )(a, *in_hbm(t["t5"], t["tw5"], t["t6"]))
@@ -698,11 +713,10 @@
     lines, partial_value = lax.optimization_barrier((lines, partial_value))
     lines = lax.all_to_all(lines.reshape(128, 32, 128), ("wide", "narrow"), 0, 0, tiled=True)
 
-    total = sum_over(partial_value, [("wide", WIDE, (1, 2, 3))])
+    total = sum_over(partial_value, [("wide", WIDE, (1, 2, 3)), ("wide", WIDE, (8, 16, 24))])
     total, green = lax.optimization_barrier((total, green))
     near = pack_green(green, place, 0)
     near_partner = partner(near[1], 1)
-    total = sum_over(total, [("wide", WIDE, (8, 16, 24))])
     total, far, near_partner = lax.optimization_barrier((total, far, near_partner))
     total = sum_over(total, [("narrow", NARROW, (1,))])
     greens = [near[0], near_partner, far, partner(second_of(far), 1)]

time: 173 us -> 172 us (level)
    ppermute x3, waiting for transfers between devices: 9.36 us -> 28.3 us  [partner(): return lax.ppermute(value, 'narrow', [(j, j ^ k) for j in range(NARROW)])]
    ppermute x10, waiting for transfers between devices: 48 us -> 29.5 us  [exchange(): lax.ppermute(value, axis, [(j, j ^ stride) for j in range(size)])]
  transfers between devices with their start and end apart: 17 -> 17, of which waited for: 11 -> 12; matrix products, arithmetic and copies ran while one was open for 3% -> 3% of each run, Pallas kernels for 15% -> 15%
where the time goes in v6:
time: 172 us
  waiting for transfers between devices  74.7 us (43%)
  Pallas kernels  45.9 us (27%)
  starting transfers between devices  44.1 us (26%)
  other arithmetic  5.76 us (3%)
    ppermute x10, waiting for transfers between devices, exchange(): lax.ppermute(value, axis, [(j, j ^ stride) for j in range(size)])  29.5 us
    ppermute x3, waiting for transfers between devices, partner(): return lax.ppermute(value, 'narrow', [(j, j ^ k) for j in range(NARROW)])  28.3 us
    all_to_all x2, starting transfers between devices, local(): lax.all_to_all(lines.reshape(WIDE, 64, 128), 'wide', 0, 0, tiled=True)  14.2 us
    ppermute x10, starting transfers between devices, exchange(): lax.ppermute(value, axis, [(j, j ^ stride) for j in range(size)])  13.6 us
    all_to_all x2, starting transfers between devices, local(): lax.all_to_all(lines.reshape(128, 32, 128), ('wide', 'narrow'), 0, 0, til...  13.4 us
    pallas_call x1, Pallas kernels, middle(): pl.pallas_call(middle_kernel, in_specs=[pl.BlockSpec(memory_space=pltpu.S...  11.3 us
    all_to_all x2, waiting for transfers between devices, local(): lax.all_to_all(lines.reshape(WIDE, 64, 128), 'wide', 0, 0, tiled=True)  9.91 us
    pallas_call x1, Pallas kernels, x_forward(): pl.pallas_call(x_forward_kernel, in_specs=[spec_vmem()] + [spec_hbm()] *...  7.09 us
  transfers between devices with their start and end apart: 17, of which 12 were waited for; matrix products, arithmetic and copies ran while one was open for 3% of the time, Pallas kernels for 15%

profile of v6, /device:TPU:0, one launch (start us, length us, event | category | flops | bytes accessed | tf_op | source)
XLA Modules:
  0.0 171.5 jit_solution(6370459529339086189)
XLA Ops:
  0.6 2.3 %columns_major.1 = f32[2048,128]{1,0:T(8,128)} custom-call(f32[2,128,1024]{2,1,0:T(8,128)} %bitcast.41), custom_call_target="tpu_custom_call" | custom-call | bytes 2097152 | tf_op jit(solution)/shard_map/columns_major/pallas_call | solution.py:194
  2.9 9.3 %all-to-all-start = ((f32[32,64,128]{2,1,0:T(8,128)}), f32[32,64,128]{2,1,0:T(8,128)S(1)}, u32[]{:S(2)}, u32[]{:S(2)}) async-start(f32[32,64,128]{2,1,0:T(8,128)} %bitcast.49), calls=%async_computation | async-start | bytes 2097152 | tf_op jit(solution)/shard_map/all_to_all | solution.py:701
  12.3 3.4 %pack_far.1 = f32[2,2,1024,128]{3,2,1,0:T(8,128)} custom-call(s32[2]{0:T(128)S(1)} %pad_add_fusion.place_ref, f32[2,2,1024,256]{3,2,1,0:T(8,128)} %bitcast.47), custom_call_target="tpu_custom_call" | custom-call | bytes 4194304 | tf_op jit(solution)/shard_map/pack_far/pallas_call | solution.py:539
  15.6 2.9 %collective-permute-start.6 = (f32[2,2,1024,128]{3,2,1,0:T(8,128)}, f32[2,2,1024,128]{3,2,1,0:T(8,128)}, u32[]{:S(2)}, u32[]{:S(2)}) collective-permute-start(f32[2,2,1024,128]{3,2,1,0:T(8,128)} %pack_far.1), channel_id=1, source_target_pairs={{0,2},{1,3},{2,0},{3,1},{4,6},{5,7},{6,4},{7,5},{8,10},{9,11},{10,... | collective-permute-start | bytes 6291464 | tf_op jit(solution)/shard_map/ppermute | solution.py:696
  21.7 5.0 %project.1 = f32[8,1024]{1,0:T(8,128)S(1)} custom-call(f32[2,128,1024]{2,1,0:T(8,128)S(1)} %bitcast.42, f32[2,32,1024]{2,1,0:T(8,128)S(1)} %get-tuple-element.57.ea_ref, f32[2,32,1024]{2,1,0:T(8,128)S(1)} %get-tuple-element.58.eb_ref, f32[2,128,1024]{2,1,0:T(8,128)S(1)} %pad_maximum_fusion.row_ref), custom_call_target="tpu_custom_call" | custom-call | flops 3221225472 | bytes 4194304 | tf_op jit(solution)/shard_map/project/pallas_call | solution.py:605
  28.7 7.1 %x_forward.1 = f32[4096,128]{1,0:T(8,128)} custom-call(f32[2048,128]{1,0:T(8,128)S(1)} %bitcast.46, bf16[128,192]{1,0:T(8,128)(2,1)} %constant.77.clone.t1_hbm, f32[2,64,128]{2,1,0:T(8,128)} %constant.78.clone.tw_hbm, bf16[256,768]{1,0:T(8,128)(2,1)} %constant.79.clone.t2_hbm), custom_call_target="tpu_custom_call" | custom-call | flops 1073741824 | bytes 4194304 | tf_op jit(solution)/shard_map/x_forward/pallas_call | solution.py:240
  42.8 2.5 %collective-permute-start.5 = (f32[8,1024]{1,0:T(8,128)S(1)}, f32[8,1024]{1,0:T(8,128)S(1)}, u32[]{:S(2)}, u32[]{:S(2)}) collective-permute-start(f32[8,1024]{1,0:T(8,128)S(1)} %add_add_fusion.1), channel_id=1, source_target_pairs={{0,96},{4,100},{8,104},{12,108},{16,112},{20,116},{24,120},{28,124... | collective-permute-start | bytes 98312 | tf_op jit(solution)/shard_map/ppermute | solution.py:678
  48.0 2.7 %collective-permute-done.4 = f32[8,1024]{1,0:T(8,128)S(1)} collective-permute-done((f32[8,1024]{1,0:T(8,128)S(1)}, f32[8,1024]{1,0:T(8,128)S(1)}, u32[]{:S(2)}, u32[]{:S(2)}) %collective-permute-start.4) | collective-permute-done | bytes 32800 | tf_op jit(solution)/shard_map/ppermute | solution.py:678
  50.7 3.3 %pack_near.1 = (f32[2,1024,128]{2,1,0:T(8,128)}, f32[2,1024,128]{2,1,0:T(8,128)}) custom-call(s32[2]{0:T(128)S(1)} %pad_add_fusion.place_ref, f32[2,2,1024,256]{3,2,1,0:T(8,128)} %bitcast.48), custom_call_target="tpu_custom_call" | custom-call | bytes 4194304 | tf_op jit(solution)/shard_map/pack_near/pallas_call | solution.py:539
  54.0 7.9 %all-to-all-start.1 = ((f32[128,32,128]{2,1,0:T(8,128)}), f32[128,32,128]{2,1,0:T(8,128)S(1)}, u32[]{:S(2)}, u32[]{:S(2)}) async-start(f32[128,32,128]{2,1,0:T(8,128)} %bitcast.50), calls=%async_computation.1 | async-start | bytes 4194304 | tf_op jit(solution)/shard_map/all_to_all | solution.py:714
  61.9 28.3 %collective-permute-done.6.in_ref.r2_hbm = f32[2,2,1024,128]{3,2,1,0:T(8,128)} collective-permute-done((f32[2,2,1024,128]{3,2,1,0:T(8,128)}, f32[2,2,1024,128]{3,2,1,0:T(8,128)}, u32[]{:S(2)}, u32[]{:S(2)}) %collective-permute-start.6) | collective-permute-done | bytes 2097184 | tf_op jit(solution)/shard_map/ppermute | solution.py:696
  90.2 2.0 %second.1 = f32[2,1024,128]{2,1,0:T(8,128)} custom-call(f32[2,2,1024,128]{3,2,1,0:T(8,128)} %collective-permute-done.6.in_ref.r2_hbm), custom_call_target="tpu_custom_call" | custom-call | bytes 2097152 | tf_op jit(solution)/shard_map/second/pallas_call | solution.py:559
  94.5 3.3 %all-to-all-done.1 = f32[128,32,128]{2,1,0:T(8,128)S(1)} async-done(((f32[128,32,128]{2,1,0:T(8,128)}), f32[128,32,128]{2,1,0:T(8,128)S(1)}, u32[]{:S(2)}, u32[]{:S(2)}) %all-to-all-start.1) | async-done | bytes 2097184 | tf_op jit(solution)/shard_map/all_to_all | solution.py:714
  97.9 11.3 %middle.1 = f32[128,32,128]{2,1,0:T(8,128)} custom-call(s32[2]{0:T(128)S(1)} %pad_add_fusion.place_ref, f32[4096,128]{1,0:T(8,128)S(1)} %bitcast.44, bf16[512,768]{1,0:T(8,128)(2,1)} %constant.80.clone.t3_hbm, f32[2,256,128]{2,1,0:T(8,128)} %constant.81.clone.tw_hbm, f32[2,256,128]{2,1,0:T(8,128)} %constant.82.clone.step_hbm, ...), custom_call_target="tpu_custom_call" | custom-call | flops 3221225472 | bytes 10485760 | tf_op jit(solution)/shard_map/middle/pallas_call | solution.py:379
  109.2 5.6 %all-to-all-start.2 = ((f32[128,32,128]{2,1,0:T(8,128)}), f32[128,32,128]{2,1,0:T(8,128)S(1)}, u32[]{:S(2)}, u32[]{:S(2)}) async-start(f32[128,32,128]{2,1,0:T(8,128)} %middle.1), calls=%async_computation.2 | async-start | bytes 4194304 | tf_op jit(solution)/shard_map/all_to_all | solution.py:726
  114.7 2.3 %collective-permute-start.12 = (f32[8,1024]{1,0:T(8,128)S(1)}, f32[8,1024]{1,0:T(8,128)S(1)}, u32[]{:S(2)}, u32[]{:S(2)}) collective-permute-start(f32[8,1024]{1,0:T(8,128)S(1)} %add.112), channel_id=1, source_target_pairs={{0,18},{1,19},{2,16},{3,17},{4,22},{5,23},{6,20},{7,21},{8,26},{9,... | collective-permute-start | bytes 98312 | tf_op jit(solution)/shard_map/ppermute | solution.py:678
  117.3 2.3 %collective-permute-start.10 = (f32[8,1024]{1,0:T(8,128)S(1)}, f32[8,1024]{1,0:T(8,128)S(1)}, u32[]{:S(2)}, u32[]{:S(2)}) collective-permute-start(f32[8,1024]{1,0:T(8,128)S(1)} %add.112), channel_id=1, source_target_pairs={{0,2},{1,3},{2,0},{3,1},{4,6},{5,7},{6,4},{7,5},{8,10},{9,11},{10,... | collective-permute-start | bytes 98312 | tf_op jit(solution)/shard_map/ppermute | solution.py:678
  119.5 21.1 %collective-permute-done.12 = f32[8,1024]{1,0:T(8,128)S(1)} collective-permute-done((f32[8,1024]{1,0:T(8,128)S(1)}, f32[8,1024]{1,0:T(8,128)S(1)}, u32[]{:S(2)}, u32[]{:S(2)}) %collective-permute-start.12) | collective-permute-done | bytes 32800 | tf_op jit(solution)/shard_map/ppermute | solution.py:678
  140.7 3.7 %all-to-all-done.2 = f32[128,32,128]{2,1,0:T(8,128)S(1)} async-done(((f32[128,32,128]{2,1,0:T(8,128)}), f32[128,32,128]{2,1,0:T(8,128)S(1)}, u32[]{:S(2)}, u32[]{:S(2)}) %all-to-all-start.2) | async-done | bytes 2097184 | tf_op jit(solution)/shard_map/all_to_all | solution.py:726
  144.5 4.4 %x_inverse.1 = f32[32,64,128]{2,1,0:T(8,128)} custom-call(f32[4096,128]{1,0:T(8,128)S(1)} %bitcast.45, bf16[256,768]{1,0:T(8,128)(2,1)} %constant.85.clone.t5_hbm, f32[2,128,128]{2,1,0:T(8,128)} %constant.86.clone.tw_hbm, bf16[128,768]{1,0:T(8,128)(2,1)} %constant.87.clone.t6_hbm), custom_call_target="tpu_custom_call" | custom-call | flops 1073741824 | bytes 4194304 | tf_op jit(solution)/shard_map/x_inverse/pallas_call | solution.py:458
  148.9 4.9 %all-to-all-start.3 = ((f32[32,64,128]{2,1,0:T(8,128)}), f32[32,64,128]{2,1,0:T(8,128)S(1)}, u32[]{:S(2)}, u32[]{:S(2)}) async-start(f32[32,64,128]{2,1,0:T(8,128)} %x_inverse.1), calls=%async_computation.3 | async-start | bytes 2097152 | tf_op jit(solution)/shard_map/all_to_all | solution.py:738
  153.9 2.0 %add_multiply_fusion = (f32[1,128,1024]{2,1,0:T(8,128)S(1)}, f32[1,128,1024]{2,1,0:T(8,128)S(1)}) fusion(f32[1024]{0:T(1024)S(1)} %bitcast.53, f32[1024]{0:T(1024)S(1)} %bitcast.52, f32[1024]{0:T(1024)S(1)} %get-tuple-element.53, f32[128]{0:T(128)S(1)} %add_multiply_fusion.1), kind=kLoop, calls=%fused_computation.15 | loop fusion | flops 1310720 | bytes 1061376 | tf_op jit(solution)/shard_map/mul | solution.py:747
  156.0 5.6 %backproject.1 = f32[2,128,1024]{2,1,0:T(8,128)} custom-call(f32[2,128,1024]{2,1,0:T(8,128)S(1)} %pad_maximum_fusion.2.weight_ref, f32[2,32,1024]{2,1,0:T(8,128)S(1)} %get-tuple-element.57.ea_ref, f32[2,32,1024]{2,1,0:T(8,128)S(1)} %copy-done.3), custom_call_target="tpu_custom_call" | custom-call | flops 3221225472 | bytes 4194304 | tf_op jit(solution)/shard_map/backproject/pallas_call | solution.py:653
  162.2 8.0 %all-to-all-done.3 = f32[32,64,128]{2,1,0:T(8,128)S(1)} async-done(((f32[32,64,128]{2,1,0:T(8,128)}), f32[32,64,128]{2,1,0:T(8,128)S(1)}, u32[]{:S(2)}, u32[]{:S(2)}) %all-to-all-start.3) | async-done | bytes 1048608 | tf_op jit(solution)/shard_map/all_to_all | solution.py:738
  (54 shorter events, 19.4 us)
Async XLA Ops:
  2.9 25.8 %all-to-all-start = ((f32[32,64,128]{2,1,0:T(8,128)}), f32[32,64,128]{2,1,0:T(8,128)S(1)}, u32[]{:S(2)}, u32[]{:S(2)}) async-start(f32[32,64,128]{2,1,0:T(8,128)} %bitcast.49), calls=%async_computation | async-start | bytes 2097152 | tf_op jit(solution)/shard_map/all_to_all | solution.py:701
  12.3 6.3 %copy-start.7 = (f32[1024]{0:T(1024)S(1)}, f32[1024]{0:T(1024)}, u32[]{:S(2)}) copy-start(f32[1024]{0:T(1024)} %param.21) | copy-start | bytes 12292
  15.6 74.5 %collective-permute-start.6 = (f32[2,2,1024,128]{3,2,1,0:T(8,128)}, f32[2,2,1024,128]{3,2,1,0:T(8,128)}, u32[]{:S(2)}, u32[]{:S(2)}) collective-permute-start(f32[2,2,1024,128]{3,2,1,0:T(8,128)} %pack_far.1), channel_id=1, source_target_pairs={{0,2},{1,3},{2,0},{3,1},{4,6},{5,7},{6,4},{7,5},{8,10},{9,11},{10,... | collective-permute-start | bytes 6291464 | tf_op jit(solution)/shard_map/ppermute | solution.py:696
  21.7 5.1 %copy-start.2 = (f32[2,32,1024]{2,1,0:T(8,128)}, f32[2,32,1024]{2,1,0:T(8,128)S(1)}, u32[]{:S(2)}) copy-start(f32[2,32,1024]{2,1,0:T(8,128)S(1)} %get-tuple-element.58.eb_ref) | copy-start | bytes 786436
  35.8 5.2 %collective-permute-start.2 = (f32[8,1024]{1,0:T(8,128)S(1)}, f32[8,1024]{1,0:T(8,128)S(1)}, u32[]{:S(2)}, u32[]{:S(2)}) collective-permute-start(f32[8,1024]{1,0:T(8,128)S(1)} %project.1), channel_id=1, source_target_pairs={{0,12},{4,8},{8,4},{12,0},{16,28},{20,24},{24,20},{28,16},{32,44},... | collective-permute-start | bytes 98312 | tf_op jit(solution)/shard_map/ppermute | solution.py:678
  37.0 5.4 %collective-permute-start.1 = (f32[8,1024]{1,0:T(8,128)S(1)}, f32[8,1024]{1,0:T(8,128)S(1)}, u32[]{:S(2)}, u32[]{:S(2)}) collective-permute-start(f32[8,1024]{1,0:T(8,128)S(1)} %project.1), channel_id=1, source_target_pairs={{0,8},{4,12},{8,0},{12,4},{16,24},{20,28},{24,16},{28,20},{32,40},... | collective-permute-start | bytes 98312 | tf_op jit(solution)/shard_map/ppermute | solution.py:678
  38.9 3.9 %collective-permute-start = (f32[8,1024]{1,0:T(8,128)S(1)}, f32[8,1024]{1,0:T(8,128)S(1)}, u32[]{:S(2)}, u32[]{:S(2)}) collective-permute-start(f32[8,1024]{1,0:T(8,128)S(1)} %project.1), channel_id=1, source_target_pairs={{0,4},{4,0},{8,12},{12,8},{16,20},{20,16},{24,28},{28,24},{32,36},... | collective-permute-start | bytes 98312 | tf_op jit(solution)/shard_map/ppermute | solution.py:678
  42.8 5.2 %collective-permute-start.5 = (f32[8,1024]{1,0:T(8,128)S(1)}, f32[8,1024]{1,0:T(8,128)S(1)}, u32[]{:S(2)}, u32[]{:S(2)}) collective-permute-start(f32[8,1024]{1,0:T(8,128)S(1)} %add_add_fusion.1), channel_id=1, source_target_pairs={{0,96},{4,100},{8,104},{12,108},{16,112},{20,116},{24,120},{28,124... | collective-permute-start | bytes 98312 | tf_op jit(solution)/shard_map/ppermute | solution.py:678
  45.2 5.4 %collective-permute-start.4 = (f32[8,1024]{1,0:T(8,128)S(1)}, f32[8,1024]{1,0:T(8,128)S(1)}, u32[]{:S(2)}, u32[]{:S(2)}) collective-permute-start(f32[8,1024]{1,0:T(8,128)S(1)} %add_add_fusion.1), channel_id=1, source_target_pairs={{0,64},{4,68},{8,72},{12,76},{16,80},{20,84},{24,88},{28,92},{32,9... | collective-permute-start | bytes 98312 | tf_op jit(solution)/shard_map/ppermute | solution.py:678
  46.2 4.5 %collective-permute-start.3 = (f32[8,1024]{1,0:T(8,128)S(1)}, f32[8,1024]{1,0:T(8,128)S(1)}, u32[]{:S(2)}, u32[]{:S(2)}) collective-permute-start(f32[8,1024]{1,0:T(8,128)S(1)} %add_add_fusion.1), channel_id=1, source_target_pairs={{0,32},{4,36},{8,40},{12,44},{16,48},{20,52},{24,56},{28,60},{32,0... | collective-permute-start | bytes 98312 | tf_op jit(solution)/shard_map/ppermute | solution.py:678
  54.0 36.2 %collective-permute-start.7 = (f32[2,1024,128]{2,1,0:T(8,128)}, f32[2,1024,128]{2,1,0:T(8,128)}, u32[]{:S(2)}, u32[]{:S(2)}) collective-permute-start(f32[2,1024,128]{2,1,0:T(8,128)} %get-tuple-element.29), channel_id=1, source_target_pairs={{0,1},{1,0},{2,3},{3,2},{4,5},{5,4},{6,7},{7,6},{8,9},{9,8},{10,11... | collective-permute-start | bytes 3145736 | tf_op jit(solution)/shard_map/ppermute | solution.py:696
  54.0 43.8 %all-to-all-start.1 = ((f32[128,32,128]{2,1,0:T(8,128)}), f32[128,32,128]{2,1,0:T(8,128)S(1)}, u32[]{:S(2)}, u32[]{:S(2)}) async-start(f32[128,32,128]{2,1,0:T(8,128)} %bitcast.50), calls=%async_computation.1 | async-start | bytes 4194304 | tf_op jit(solution)/shard_map/all_to_all | solution.py:714
  92.2 5.7 %collective-permute-start.9 = (f32[2,1024,128]{2,1,0:T(8,128)}, f32[2,1024,128]{2,1,0:T(8,128)}, u32[]{:S(2)}, u32[]{:S(2)}) collective-permute-start(f32[2,1024,128]{2,1,0:T(8,128)} %second.1), channel_id=1, source_target_pairs={{0,1},{1,0},{2,3},{3,2},{4,5},{5,4},{6,7},{7,6},{8,9},{9,8},{10,11... | collective-permute-start | bytes 3145736 | tf_op jit(solution)/shard_map/ppermute | solution.py:696
  92.2 2.3 %collective-permute-start.8 = (f32[8,1024]{1,0:T(8,128)S(1)}, f32[8,1024]{1,0:T(8,128)S(1)}, u32[]{:S(2)}, u32[]{:S(2)}) collective-permute-start(f32[8,1024]{1,0:T(8,128)S(1)} %add_add_fusion), channel_id=1, source_target_pairs={{0,1},{1,0},{2,3},{3,2},{4,5},{5,4},{6,7},{7,6},{8,9},{9,8},{10,11... | collective-permute-start | bytes 98312 | tf_op jit(solution)/shard_map/ppermute | solution.py:678
  109.2 31.5 %copy-start.6 = (f32[1,2,1024]{2,1,0:T(2,128)S(1)}, f32[1,2,1024]{2,1,0:T(2,128)}, u32[]{:S(2)}) copy-start(f32[1,2,1024]{2,1,0:T(2,128)} %param.22) | copy-start | bytes 24580
  109.2 35.3 %all-to-all-start.2 = ((f32[128,32,128]{2,1,0:T(8,128)}), f32[128,32,128]{2,1,0:T(8,128)S(1)}, u32[]{:S(2)}, u32[]{:S(2)}) async-start(f32[128,32,128]{2,1,0:T(8,128)} %middle.1), calls=%async_computation.2 | async-start | bytes 4194304 | tf_op jit(solution)/shard_map/all_to_all | solution.py:726
  114.7 25.9 %collective-permute-start.12 = (f32[8,1024]{1,0:T(8,128)S(1)}, f32[8,1024]{1,0:T(8,128)S(1)}, u32[]{:S(2)}, u32[]{:S(2)}) collective-permute-start(f32[8,1024]{1,0:T(8,128)S(1)} %add.112), channel_id=1, source_target_pairs={{0,18},{1,19},{2,16},{3,17},{4,22},{5,23},{6,20},{7,21},{8,26},{9,... | collective-permute-start | bytes 98312 | tf_op jit(solution)/shard_map/ppermute | solution.py:678
  117.0 23.6 %collective-permute-start.11 = (f32[8,1024]{1,0:T(8,128)S(1)}, f32[8,1024]{1,0:T(8,128)S(1)}, u32[]{:S(2)}, u32[]{:S(2)}) collective-permute-start(f32[8,1024]{1,0:T(8,128)S(1)} %add.112), channel_id=1, source_target_pairs={{0,16},{1,17},{2,18},{3,19},{4,20},{5,21},{6,22},{7,23},{8,24},{9,... | collective-permute-start | bytes 98312 | tf_op jit(solution)/shard_map/ppermute | solution.py:678
  117.3 23.4 %collective-permute-start.10 = (f32[8,1024]{1,0:T(8,128)S(1)}, f32[8,1024]{1,0:T(8,128)S(1)}, u32[]{:S(2)}, u32[]{:S(2)}) collective-permute-start(f32[8,1024]{1,0:T(8,128)S(1)} %add.112), channel_id=1, source_target_pairs={{0,2},{1,3},{2,0},{3,1},{4,6},{5,7},{6,4},{7,5},{8,10},{9,11},{10,... | collective-permute-start | bytes 98312 | tf_op jit(solution)/shard_map/ppermute | solution.py:678
  140.7 8.2 %copy-start.5 = (f32[1,2,1024]{2,1,0:T(2,128)}, f32[1,2,1024]{2,1,0:T(2,128)S(1)}, u32[]{:S(2)}) copy-start(f32[1,2,1024]{2,1,0:T(2,128)S(1)} %fusion.8) | copy-start | bytes 24580
  148.9 21.2 %all-to-all-start.3 = ((f32[32,64,128]{2,1,0:T(8,128)}), f32[32,64,128]{2,1,0:T(8,128)S(1)}, u32[]{:S(2)}, u32[]{:S(2)}) async-start(f32[32,64,128]{2,1,0:T(8,128)} %x_inverse.1), calls=%async_computation.3 | async-start | bytes 2097152 | tf_op jit(solution)/shard_map/all_to_all | solution.py:738
  153.8 2.2 %copy-start.3 = (f32[2,32,1024]{2,1,0:T(8,128)S(1)}, f32[2,32,1024]{2,1,0:T(8,128)}, u32[]{:S(2)}) copy-start(f32[2,32,1024]{2,1,0:T(8,128)} %copy-done.2) | copy-start | bytes 786436
  156.0 5.7 %copy-start.1 = (f32[2,128,1024]{2,1,0:T(8,128)S(1)}, f32[2,128,1024]{2,1,0:T(8,128)}, u32[]{:S(2)}) copy-start(f32[2,128,1024]{2,1,0:T(8,128)} %contrast_ref) | copy-start | bytes 3145732
  156.0 5.7 %copy-start.4 = (f32[1,2,128,1024]{3,2,1,0:T(8,128)S(1)}, f32[1,2,128,1024]{3,2,1,0:T(8,128)}, u32[]{:S(2)}) copy-start(f32[1,2,128,1024]{3,2,1,0:T(8,128)} %param.18) | copy-start | bytes 3145732
  (1 other events, 1.2 us)

commit v7 on v6

--- a/solution.py
+++ b/solution.py
@@ -151,6 +151,11 @@
     return [(re, im) for im, re in swapped]
 
 
+def place():
+    narrow = lax.axis_index("narrow")
+    return lax.rem(narrow, 2), lax.div(narrow, 2)
+
+
 def spec_vmem():
     return pl.BlockSpec(memory_space=pltpu.VMEM)
 
@@ -261,12 +266,11 @@
 
 
 def middle_kernel(
-    place_ref, a_ref, t3_hbm, tw_hbm, step_hbm, r0_hbm, r1_hbm, r2_hbm, r3_hbm, lane_hbm, t4_hbm,
+    a_ref, t3_hbm, tw_hbm, step_hbm, r0_hbm, r1_hbm, r2_hbm, r3_hbm, lane_hbm, t4_hbm,
     out_hbm, t3_ref, tw_ref, step_ref, green_ref, lane_ref, t4_ref, u_ref, now_ref, out_ref,
     spread_ref, arrived, sent, moved,
 ):
-    flip = place_ref[0]
-    upper = place_ref[1]
+    flip, upper = place()
     spread = pltpu.make_async_copy(
         a_ref.reshape(128, 32, 128), spread_ref.reshape(128, 40, 128).at[:, pl.ds(0, 32)], moved
     )
@@ -374,11 +378,11 @@
         copy.wait()
 
 
-def middle(a, greens, place):
+def middle(a, greens):
     t = tables()
     return pl.pallas_call(
         middle_kernel,
-        in_specs=[pl.BlockSpec(memory_space=pltpu.SMEM), spec_vmem()] + [spec_hbm()] * 9,
+        in_specs=[spec_vmem()] + [spec_hbm()] * 9,
         out_specs=spec_hbm(),
         out_shape=pltpu.HBM((128, 32, 128), f32),
         scratch_shapes=[
@@ -400,7 +404,7 @@
         cost_estimate=cost(2 * 8 * 2 * 512 * 65536 * 3, 10 << 20),
         name="middle",
     )(
-        place, a, *in_hbm(t["t3"], t["tw3"], t["step3"], *greens, t["lane3"], t["t4"])
+        a, *in_hbm(t["t3"], t["tw3"], t["step3"], *greens, t["lane3"], t["t4"])
     )
 
 
@@ -506,49 +510,63 @@
     )(a, contrast, known)
 
 
-def pack_kernel(across, place_ref, green_ref, *out_refs):
-    flip = place_ref[0]
+def pack_kernel(across, green_hbm, *refs):
+    out_hbms, (green_ref, out_ref, arrived, sent) = refs[:-4], refs[-4:]
+    flip, upper = place()
+    column = jnp.where(upper == 1, 1 - across, across)
+    lanes = pl.ds(pl.multiple_of(column * 128, 128), 128)
     lane = lax.broadcasted_iota(jnp.int32, (512, 128), 1)
     low = lane < 64
     pick = low == (flip == 0)
-    for part in range(2):
-        first = green_ref[part, 0]
-        second = green_ref[part, 1]
+    pieces = [(part, pl.ds(first, 512)) for first in (0, 512) for part in range(2)]
+    copies = fetch(
+        [green_hbm.at[part, :, rows, lanes] for part, rows in pieces],
+        [green_ref.at[part, :, rows] for part, rows in pieces],
+        arrived,
+    )
+    leaving = []
+    for k, (part, rows) in enumerate(pieces):
+        copies[k].wait()
+        first = green_ref[part, 0, rows]
+        second = green_ref[part, 1, rows]
         straight = jnp.where(low, first, second)
         crossed = pltpu.roll(jnp.where(low, second, first), 64, 1)
         for core, value in enumerate(
             (jnp.where(pick, straight, crossed), jnp.where(pick, crossed, straight))
         ):
-            if across:
-                out_refs[0][core, part] = value
-            else:
-                out_refs[core][part] = value
-
-
-def pack_green(green, place, across):
+            out_ref[core, part, rows] = value
+            target = out_hbms[0].at[core] if across else out_hbms[core]
+            leaving.append(
+                pltpu.make_async_copy(
+                    out_ref.at[core, part, rows], target.at[part, rows], sent.at[k, core]
+                )
+            )
+            leaving[-1].start()
+    for copy in leaving:
+        copy.wait()
+
+
+def pack_green(green, across):
     if across:
-        out_specs = pl.BlockSpec((2, 2, 512, 128), lambda t, place_ref: (0, 0, t, 0))
-        out_shape = pltpu.HBM((2, 2, 1024, 128), f32)
+        out_shape = [pltpu.HBM((2, 2, 1024, 128), f32)]
     else:
-        out_specs = [pl.BlockSpec((2, 512, 128), lambda t, place_ref: (0, t, 0))] * 2
         out_shape = [pltpu.HBM((2, 1024, 128), f32)] * 2
-
-    def column(t, place_ref):
-        return 0, 0, t, jnp.where(place_ref[1] == 1, 1 - across, across)
-
-    return pl.pallas_call(
+    out = pl.pallas_call(
         functools.partial(pack_kernel, across),
-        grid_spec=pltpu.PrefetchScalarGridSpec(
-            num_scalar_prefetch=1,
-            grid=(2,),
-            in_specs=[pl.BlockSpec((2, 2, 512, 128), column)],
-            out_specs=out_specs,
-        ),
+        in_specs=[spec_hbm()],
+        out_specs=[spec_hbm()] * len(out_shape),
         out_shape=out_shape,
-        compiler_params=params(),
+        scratch_shapes=[
+            pltpu.VMEM((2, 2, 1024, 128), f32),
+            pltpu.VMEM((2, 2, 1024, 128), f32),
+            pltpu.SemaphoreType.DMA((4,)),
+            pltpu.SemaphoreType.DMA((4, 2)),
+        ],
+        compiler_params=params(12),
         cost_estimate=cost(0, 4 << 20),
         name="pack_far" if across else "pack_near",
-    )(place, *in_hbm(green.reshape(2, 2, 1024, 256)))
+    )(*in_hbm(green.reshape(2, 2, 1024, 256)))
+    return out[0] if across else out
 
 
 def second_kernel(in_ref, out_ref):
@@ -689,7 +707,6 @@
 def local(sources, incident, contrast, green, angles, measured):
     wide = lax.axis_index("wide")
     narrow = lax.axis_index("narrow")
-    place = jnp.stack([narrow % 2, narrow // 2]).astype(jnp.int32)
     source = sources[0]
 
     def partner(value, k):
@@ -697,7 +714,7 @@
 
     lines = columns_major(source)
     lines, green = lax.optimization_barrier((lines, green))
-    far = partner(pack_green(green, place, 1), 2)
+    far = partner(pack_green(green, 1), 2)
     lines = lax.all_to_all(lines.reshape(WIDE, 64, 128), "wide", 0, 0, tiled=True)
 
     row_position = (wide * 128 + jnp.arange(128, dtype=jnp.int32)).astype(f32) - N // 2 + 0.5
@@ -715,13 +732,13 @@
 
     total = sum_over(partial_value, [("wide", WIDE, (1, 2, 3)), ("wide", WIDE, (8, 16, 24))])
     total, green = lax.optimization_barrier((total, green))
-    near = pack_green(green, place, 0)
+    near = pack_green(green, 0)
     near_partner = partner(near[1], 1)
     total, far, near_partner = lax.optimization_barrier((total, far, near_partner))
     total = sum_over(total, [("narrow", NARROW, (1,))])
     greens = [near[0], near_partner, far, partner(second_of(far), 1)]
     total, lines = lax.optimization_barrier((total, lines))
-    lines = middle(lines.reshape(4096, 128), greens, place)
+    lines = middle(lines.reshape(4096, 128), greens)
     total, lines = lax.optimization_barrier((total, lines))
     lines = lax.all_to_all(lines.reshape(128, 32, 128), ("wide", "narrow"), 0, 0, tiled=True)
     total = sum_over(

time: 172 us -> 172 us (level)
  Pallas kernels: 45.9 us -> 43.9 us
    pallas_call x3, Pallas kernels: 18 us -> 16 us  [the longest x1 10.8 us: middle(): pl.pallas_call(middle_kernel, in_specs=[spec_vmem()] + [spec_hbm()] * 9,...]
where the time goes in v7:
time: 172 us; the launch traced here: 171 us
  waiting for transfers between devices  75.9 us (44%)
  starting transfers between devices  44.6 us (26%)
  Pallas kernels  43.9 us (26%)
  other arithmetic  5.65 us (3%)
    ppermute x10, waiting for transfers between devices, exchange(): lax.ppermute(value, axis, [(j, j ^ stride) for j in range(size)])  29.3 us
    ppermute x3, waiting for transfers between devices, partner(): return lax.ppermute(value, 'narrow', [(j, j ^ k) for j in range(NARROW)])  28.7 us
    all_to_all x2, starting transfers between devices, local(): lax.all_to_all(lines.reshape(WIDE, 64, 128), 'wide', 0, 0, tiled=True)  14.2 us
    all_to_all x2, starting transfers between devices, local(): lax.all_to_all(lines.reshape(128, 32, 128), ('wide', 'narrow'), 0, 0, til...  13.7 us
    ppermute x10, starting transfers between devices, exchange(): lax.ppermute(value, axis, [(j, j ^ stride) for j in range(size)])  13.6 us
    pallas_call x1, Pallas kernels, middle(): pl.pallas_call(middle_kernel, in_specs=[spec_vmem()] + [spec_hbm()] * 9,...  10.8 us
    all_to_all x2, waiting for transfers between devices, local(): lax.all_to_all(lines.reshape(WIDE, 64, 128), 'wide', 0, 0, tiled=True)  10.7 us
    all_to_all x2, waiting for transfers between devices, local(): lax.all_to_all(lines.reshape(128, 32, 128), ('wide', 'narrow'), 0, 0, til...  7.19 us
  transfers between devices with their start and end apart: 17, of which 12 were waited for; matrix products, arithmetic and copies ran while one was open for 3% of the time, Pallas kernels for 15%

profile of v7, /device:TPU:0, one launch (start us, length us, event | category | flops | bytes accessed | tf_op | source)
XLA Modules:
  0.0 171.0 jit_solution(5419242114188533198)
XLA Ops:
  0.6 2.3 %columns_major.1 = f32[2048,128]{1,0:T(8,128)} custom-call(f32[2,128,1024]{2,1,0:T(8,128)} %bitcast.39), custom_call_target="tpu_custom_call" | custom-call | bytes 2097152 | tf_op jit(solution)/shard_map/columns_major/pallas_call | solution.py:199
  2.9 9.3 %all-to-all-start = ((f32[32,64,128]{2,1,0:T(8,128)}), f32[32,64,128]{2,1,0:T(8,128)S(1)}, u32[]{:S(2)}, u32[]{:S(2)}) async-start(f32[32,64,128]{2,1,0:T(8,128)} %bitcast.47), calls=%async_computation | async-start | bytes 2097152 | tf_op jit(solution)/shard_map/all_to_all | solution.py:718
  12.2 2.7 %pack_far.1 = f32[2,2,1024,128]{3,2,1,0:T(8,128)} custom-call(f32[2,2,1024,256]{3,2,1,0:T(8,128)} %bitcast.45), custom_call_target="tpu_custom_call" | custom-call | bytes 4194304 | tf_op jit(solution)/shard_map/pack_far/pallas_call | solution.py:554
  14.8 3.0 %collective-permute-start.6 = (f32[2,2,1024,128]{3,2,1,0:T(8,128)}, f32[2,2,1024,128]{3,2,1,0:T(8,128)}, u32[]{:S(2)}, u32[]{:S(2)}) collective-permute-start(f32[2,2,1024,128]{3,2,1,0:T(8,128)} %pack_far.1), channel_id=1, source_target_pairs={{0,2},{1,3},{2,0},{3,1},{4,6},{5,7},{6,4},{7,5},{8,10},{9,11},{10,... | collective-permute-start | bytes 6291464 | tf_op jit(solution)/shard_map/ppermute | solution.py:713
  21.0 5.0 %project.1 = f32[8,1024]{1,0:T(8,128)S(1)} custom-call(f32[2,128,1024]{2,1,0:T(8,128)S(1)} %bitcast.40, f32[2,32,1024]{2,1,0:T(8,128)S(1)} %get-tuple-element.57.ea_ref, f32[2,32,1024]{2,1,0:T(8,128)S(1)} %get-tuple-element.58.eb_ref, f32[2,128,1024]{2,1,0:T(8,128)S(1)} %pad_maximum_fusion.row_ref), custom_call_target="tpu_custom_call" | custom-call | flops 3221225472 | bytes 4194304 | tf_op jit(solution)/shard_map/project/pallas_call | solution.py:623
  26.1 2.6 %all-to-all-done = f32[32,64,128]{2,1,0:T(8,128)S(1)} async-done(((f32[32,64,128]{2,1,0:T(8,128)}), f32[32,64,128]{2,1,0:T(8,128)S(1)}, u32[]{:S(2)}, u32[]{:S(2)}) %all-to-all-start) | async-done | bytes 1048608 | tf_op jit(solution)/shard_map/all_to_all | solution.py:718
  28.7 7.1 %x_forward.1 = f32[4096,128]{1,0:T(8,128)} custom-call(f32[2048,128]{1,0:T(8,128)S(1)} %bitcast.44, bf16[128,192]{1,0:T(8,128)(2,1)} %constant.53.clone.t1_hbm, f32[2,64,128]{2,1,0:T(8,128)} %constant.54.clone.tw_hbm, bf16[256,768]{1,0:T(8,128)(2,1)} %constant.55.clone.t2_hbm), custom_call_target="tpu_custom_call" | custom-call | flops 1073741824 | bytes 4194304 | tf_op jit(solution)/shard_map/x_forward/pallas_call | solution.py:245
  42.8 2.2 %collective-permute-start.5 = (f32[8,1024]{1,0:T(8,128)S(1)}, f32[8,1024]{1,0:T(8,128)S(1)}, u32[]{:S(2)}, u32[]{:S(2)}) collective-permute-start(f32[8,1024]{1,0:T(8,128)S(1)} %add_add_fusion.1), channel_id=1, source_target_pairs={{0,96},{4,100},{8,104},{12,108},{16,112},{20,116},{24,120},{28,124... | collective-permute-start | bytes 98312 | tf_op jit(solution)/shard_map/ppermute | solution.py:696
  48.0 2.4 %collective-permute-done.4 = f32[8,1024]{1,0:T(8,128)S(1)} collective-permute-done((f32[8,1024]{1,0:T(8,128)S(1)}, f32[8,1024]{1,0:T(8,128)S(1)}, u32[]{:S(2)}, u32[]{:S(2)}) %collective-permute-start.4) | collective-permute-done | bytes 32800 | tf_op jit(solution)/shard_map/ppermute | solution.py:696
  50.4 2.6 %pack_near.1 = (f32[2,1024,128]{2,1,0:T(8,128)}, f32[2,1024,128]{2,1,0:T(8,128)}) custom-call(f32[2,2,1024,256]{3,2,1,0:T(8,128)} %bitcast.46), custom_call_target="tpu_custom_call" | custom-call | bytes 4194304 | tf_op jit(solution)/shard_map/pack_near/pallas_call | solution.py:554
  53.2 8.1 %all-to-all-start.1 = ((f32[128,32,128]{2,1,0:T(8,128)}), f32[128,32,128]{2,1,0:T(8,128)S(1)}, u32[]{:S(2)}, u32[]{:S(2)}) async-start(f32[128,32,128]{2,1,0:T(8,128)} %bitcast.48), calls=%async_computation.1 | async-start | bytes 4194304 | tf_op jit(solution)/shard_map/all_to_all | solution.py:731
  61.3 28.7 %collective-permute-done.6.in_ref.r2_hbm = f32[2,2,1024,128]{3,2,1,0:T(8,128)} collective-permute-done((f32[2,2,1024,128]{3,2,1,0:T(8,128)}, f32[2,2,1024,128]{3,2,1,0:T(8,128)}, u32[]{:S(2)}, u32[]{:S(2)}) %collective-permute-start.6) | collective-permute-done | bytes 2097184 | tf_op jit(solution)/shard_map/ppermute | solution.py:713
  90.0 2.0 %second.1 = f32[2,1024,128]{2,1,0:T(8,128)} custom-call(f32[2,2,1024,128]{3,2,1,0:T(8,128)} %collective-permute-done.6.in_ref.r2_hbm), custom_call_target="tpu_custom_call" | custom-call | bytes 2097152 | tf_op jit(solution)/shard_map/second/pallas_call | solution.py:577
  94.4 3.5 %all-to-all-done.1 = f32[128,32,128]{2,1,0:T(8,128)S(1)} async-done(((f32[128,32,128]{2,1,0:T(8,128)}), f32[128,32,128]{2,1,0:T(8,128)S(1)}, u32[]{:S(2)}, u32[]{:S(2)}) %all-to-all-start.1) | async-done | bytes 2097184 | tf_op jit(solution)/shard_map/all_to_all | solution.py:731
  97.9 10.8 %middle.1 = f32[128,32,128]{2,1,0:T(8,128)} custom-call(f32[4096,128]{1,0:T(8,128)S(1)} %bitcast.42, bf16[512,768]{1,0:T(8,128)(2,1)} %constant.56.clone.t3_hbm, f32[2,256,128]{2,1,0:T(8,128)} %constant.57.clone.tw_hbm, f32[2,256,128]{2,1,0:T(8,128)} %constant.58.clone.step_hbm, f32[2,1024,128]{2,1,0:T(8,128)} %get-tuple-element.34.r0_hbm, ...), custom_call_target="tpu_custom_call" | custom-call | flops 3221225472 | bytes 10485760 | tf_op jit(solution)/shard_map/middle/pallas_call | solution.py:383
  108.6 5.6 %all-to-all-start.2 = ((f32[128,32,128]{2,1,0:T(8,128)}), f32[128,32,128]{2,1,0:T(8,128)S(1)}, u32[]{:S(2)}, u32[]{:S(2)}) async-start(f32[128,32,128]{2,1,0:T(8,128)} %middle.1), calls=%async_computation.2 | async-start | bytes 4194304 | tf_op jit(solution)/shard_map/all_to_all | solution.py:743
  114.2 2.3 %collective-permute-start.12 = (f32[8,1024]{1,0:T(8,128)S(1)}, f32[8,1024]{1,0:T(8,128)S(1)}, u32[]{:S(2)}, u32[]{:S(2)}) collective-permute-start(f32[8,1024]{1,0:T(8,128)S(1)} %add.106), channel_id=1, source_target_pairs={{0,18},{1,19},{2,16},{3,17},{4,22},{5,23},{6,20},{7,21},{8,26},{9,... | collective-permute-start | bytes 98312 | tf_op jit(solution)/shard_map/ppermute | solution.py:696
  116.7 2.3 %collective-permute-start.10 = (f32[8,1024]{1,0:T(8,128)S(1)}, f32[8,1024]{1,0:T(8,128)S(1)}, u32[]{:S(2)}, u32[]{:S(2)}) collective-permute-start(f32[8,1024]{1,0:T(8,128)S(1)} %add.106), channel_id=1, source_target_pairs={{0,2},{1,3},{2,0},{3,1},{4,6},{5,7},{6,4},{7,5},{8,10},{9,11},{10,... | collective-permute-start | bytes 98312 | tf_op jit(solution)/shard_map/ppermute | solution.py:696
  119.0 21.1 %collective-permute-done.12 = f32[8,1024]{1,0:T(8,128)S(1)} collective-permute-done((f32[8,1024]{1,0:T(8,128)S(1)}, f32[8,1024]{1,0:T(8,128)S(1)}, u32[]{:S(2)}, u32[]{:S(2)}) %collective-permute-start.12) | collective-permute-done | bytes 32800 | tf_op jit(solution)/shard_map/ppermute | solution.py:696
  140.2 3.7 %all-to-all-done.2 = f32[128,32,128]{2,1,0:T(8,128)S(1)} async-done(((f32[128,32,128]{2,1,0:T(8,128)}), f32[128,32,128]{2,1,0:T(8,128)S(1)}, u32[]{:S(2)}, u32[]{:S(2)}) %all-to-all-start.2) | async-done | bytes 2097184 | tf_op jit(solution)/shard_map/all_to_all | solution.py:743
  143.9 4.4 %x_inverse.1 = f32[32,64,128]{2,1,0:T(8,128)} custom-call(f32[4096,128]{1,0:T(8,128)S(1)} %bitcast.43, bf16[256,768]{1,0:T(8,128)(2,1)} %constant.61.clone.t5_hbm, f32[2,128,128]{2,1,0:T(8,128)} %constant.62.clone.tw_hbm, bf16[128,768]{1,0:T(8,128)(2,1)} %constant.63.clone.t6_hbm), custom_call_target="tpu_custom_call" | custom-call | flops 1073741824 | bytes 4194304 | tf_op jit(solution)/shard_map/x_inverse/pallas_call | solution.py:462
  148.4 4.9 %all-to-all-start.3 = ((f32[32,64,128]{2,1,0:T(8,128)}), f32[32,64,128]{2,1,0:T(8,128)S(1)}, u32[]{:S(2)}, u32[]{:S(2)}) async-start(f32[32,64,128]{2,1,0:T(8,128)} %x_inverse.1), calls=%async_computation.3 | async-start | bytes 2097152 | tf_op jit(solution)/shard_map/all_to_all | solution.py:755
  155.5 5.6 %backproject.1 = f32[2,128,1024]{2,1,0:T(8,128)} custom-call(f32[2,128,1024]{2,1,0:T(8,128)S(1)} %pad_maximum_fusion.2.weight_ref, f32[2,32,1024]{2,1,0:T(8,128)S(1)} %get-tuple-element.57.ea_ref, f32[2,32,1024]{2,1,0:T(8,128)S(1)} %copy-done.3), custom_call_target="tpu_custom_call" | custom-call | flops 3221225472 | bytes 4194304 | tf_op jit(solution)/shard_map/backproject/pallas_call | solution.py:671
  161.6 8.0 %all-to-all-done.3 = f32[32,64,128]{2,1,0:T(8,128)S(1)} async-done(((f32[32,64,128]{2,1,0:T(8,128)}), f32[32,64,128]{2,1,0:T(8,128)S(1)}, u32[]{:S(2)}, u32[]{:S(2)}) %all-to-all-start.3) | async-done | bytes 1048608 | tf_op jit(solution)/shard_map/all_to_all | solution.py:755
  (53 shorter events, 19.8 us)
Async XLA Ops:
  2.9 25.8 %all-to-all-start = ((f32[32,64,128]{2,1,0:T(8,128)}), f32[32,64,128]{2,1,0:T(8,128)S(1)}, u32[]{:S(2)}, u32[]{:S(2)}) async-start(f32[32,64,128]{2,1,0:T(8,128)} %bitcast.47), calls=%async_computation | async-start | bytes 2097152 | tf_op jit(solution)/shard_map/all_to_all | solution.py:718
  12.2 5.7 %copy-start.7 = (f32[1024]{0:T(1024)S(1)}, f32[1024]{0:T(1024)}, u32[]{:S(2)}) copy-start(f32[1024]{0:T(1024)} %param.21) | copy-start | bytes 12292
  14.8 75.2 %collective-permute-start.6 = (f32[2,2,1024,128]{3,2,1,0:T(8,128)}, f32[2,2,1024,128]{3,2,1,0:T(8,128)}, u32[]{:S(2)}, u32[]{:S(2)}) collective-permute-start(f32[2,2,1024,128]{3,2,1,0:T(8,128)} %pack_far.1), channel_id=1, source_target_pairs={{0,2},{1,3},{2,0},{3,1},{4,6},{5,7},{6,4},{7,5},{8,10},{9,11},{10,... | collective-permute-start | bytes 6291464 | tf_op jit(solution)/shard_map/ppermute | solution.py:713
  21.0 5.1 %copy-start.2 = (f32[2,32,1024]{2,1,0:T(8,128)}, f32[2,32,1024]{2,1,0:T(8,128)S(1)}, u32[]{:S(2)}) copy-start(f32[2,32,1024]{2,1,0:T(8,128)S(1)} %get-tuple-element.58.eb_ref) | copy-start | bytes 786436
  35.8 5.2 %collective-permute-start.2 = (f32[8,1024]{1,0:T(8,128)S(1)}, f32[8,1024]{1,0:T(8,128)S(1)}, u32[]{:S(2)}, u32[]{:S(2)}) collective-permute-start(f32[8,1024]{1,0:T(8,128)S(1)} %project.1), channel_id=1, source_target_pairs={{0,12},{4,8},{8,4},{12,0},{16,28},{20,24},{24,20},{28,16},{32,44},... | collective-permute-start | bytes 98312 | tf_op jit(solution)/shard_map/ppermute | solution.py:696
  37.0 5.4 %collective-permute-start.1 = (f32[8,1024]{1,0:T(8,128)S(1)}, f32[8,1024]{1,0:T(8,128)S(1)}, u32[]{:S(2)}, u32[]{:S(2)}) collective-permute-start(f32[8,1024]{1,0:T(8,128)S(1)} %project.1), channel_id=1, source_target_pairs={{0,8},{4,12},{8,0},{12,4},{16,24},{20,28},{24,16},{28,20},{32,40},... | collective-permute-start | bytes 98312 | tf_op jit(solution)/shard_map/ppermute | solution.py:696
  38.9 3.9 %collective-permute-start = (f32[8,1024]{1,0:T(8,128)S(1)}, f32[8,1024]{1,0:T(8,128)S(1)}, u32[]{:S(2)}, u32[]{:S(2)}) collective-permute-start(f32[8,1024]{1,0:T(8,128)S(1)} %project.1), channel_id=1, source_target_pairs={{0,4},{4,0},{8,12},{12,8},{16,20},{20,16},{24,28},{28,24},{32,36},... | collective-permute-start | bytes 98312 | tf_op jit(solution)/shard_map/ppermute | solution.py:696
  42.8 5.2 %collective-permute-start.5 = (f32[8,1024]{1,0:T(8,128)S(1)}, f32[8,1024]{1,0:T(8,128)S(1)}, u32[]{:S(2)}, u32[]{:S(2)}) collective-permute-start(f32[8,1024]{1,0:T(8,128)S(1)} %add_add_fusion.1), channel_id=1, source_target_pairs={{0,96},{4,100},{8,104},{12,108},{16,112},{20,116},{24,120},{28,124... | collective-permute-start | bytes 98312 | tf_op jit(solution)/shard_map/ppermute | solution.py:696
  45.0 5.4 %collective-permute-start.4 = (f32[8,1024]{1,0:T(8,128)S(1)}, f32[8,1024]{1,0:T(8,128)S(1)}, u32[]{:S(2)}, u32[]{:S(2)}) collective-permute-start(f32[8,1024]{1,0:T(8,128)S(1)} %add_add_fusion.1), channel_id=1, source_target_pairs={{0,64},{4,68},{8,72},{12,76},{16,80},{20,84},{24,88},{28,92},{32,9... | collective-permute-start | bytes 98312 | tf_op jit(solution)/shard_map/ppermute | solution.py:696
  46.2 4.3 %collective-permute-start.3 = (f32[8,1024]{1,0:T(8,128)S(1)}, f32[8,1024]{1,0:T(8,128)S(1)}, u32[]{:S(2)}, u32[]{:S(2)}) collective-permute-start(f32[8,1024]{1,0:T(8,128)S(1)} %add_add_fusion.1), channel_id=1, source_target_pairs={{0,32},{4,36},{8,40},{12,44},{16,48},{20,52},{24,56},{28,60},{32,0... | collective-permute-start | bytes 98312 | tf_op jit(solution)/shard_map/ppermute | solution.py:696
  53.1 36.9 %collective-permute-start.7 = (f32[2,1024,128]{2,1,0:T(8,128)}, f32[2,1024,128]{2,1,0:T(8,128)}, u32[]{:S(2)}, u32[]{:S(2)}) collective-permute-start(f32[2,1024,128]{2,1,0:T(8,128)} %get-tuple-element.29), channel_id=1, source_target_pairs={{0,1},{1,0},{2,3},{3,2},{4,5},{5,4},{6,7},{7,6},{8,9},{9,8},{10,11... | collective-permute-start | bytes 3145736 | tf_op jit(solution)/shard_map/ppermute | solution.py:713
  53.2 44.7 %all-to-all-start.1 = ((f32[128,32,128]{2,1,0:T(8,128)}), f32[128,32,128]{2,1,0:T(8,128)S(1)}, u32[]{:S(2)}, u32[]{:S(2)}) async-start(f32[128,32,128]{2,1,0:T(8,128)} %bitcast.48), calls=%async_computation.1 | async-start | bytes 4194304 | tf_op jit(solution)/shard_map/all_to_all | solution.py:731
  92.1 5.8 %collective-permute-start.9 = (f32[2,1024,128]{2,1,0:T(8,128)}, f32[2,1024,128]{2,1,0:T(8,128)}, u32[]{:S(2)}, u32[]{:S(2)}) collective-permute-start(f32[2,1024,128]{2,1,0:T(8,128)} %second.1), channel_id=1, source_target_pairs={{0,1},{1,0},{2,3},{3,2},{4,5},{5,4},{6,7},{7,6},{8,9},{9,8},{10,11... | collective-permute-start | bytes 3145736 | tf_op jit(solution)/shard_map/ppermute | solution.py:713
  92.1 2.3 %collective-permute-start.8 = (f32[8,1024]{1,0:T(8,128)S(1)}, f32[8,1024]{1,0:T(8,128)S(1)}, u32[]{:S(2)}, u32[]{:S(2)}) collective-permute-start(f32[8,1024]{1,0:T(8,128)S(1)} %add_add_fusion), channel_id=1, source_target_pairs={{0,1},{1,0},{2,3},{3,2},{4,5},{5,4},{6,7},{7,6},{8,9},{9,8},{10,11... | collective-permute-start | bytes 98312 | tf_op jit(solution)/shard_map/ppermute | solution.py:696
  108.6 31.5 %copy-start.6 = (f32[1,2,1024]{2,1,0:T(2,128)S(1)}, f32[1,2,1024]{2,1,0:T(2,128)}, u32[]{:S(2)}) copy-start(f32[1,2,1024]{2,1,0:T(2,128)} %param.22) | copy-start | bytes 24580
  108.6 35.3 %all-to-all-start.2 = ((f32[128,32,128]{2,1,0:T(8,128)}), f32[128,32,128]{2,1,0:T(8,128)S(1)}, u32[]{:S(2)}, u32[]{:S(2)}) async-start(f32[128,32,128]{2,1,0:T(8,128)} %middle.1), calls=%async_computation.2 | async-start | bytes 4194304 | tf_op jit(solution)/shard_map/all_to_all | solution.py:743
  114.2 25.9 %collective-permute-start.12 = (f32[8,1024]{1,0:T(8,128)S(1)}, f32[8,1024]{1,0:T(8,128)S(1)}, u32[]{:S(2)}, u32[]{:S(2)}) collective-permute-start(f32[8,1024]{1,0:T(8,128)S(1)} %add.106), channel_id=1, source_target_pairs={{0,18},{1,19},{2,16},{3,17},{4,22},{5,23},{6,20},{7,21},{8,26},{9,... | collective-permute-start | bytes 98312 | tf_op jit(solution)/shard_map/ppermute | solution.py:696
  116.5 23.6 %collective-permute-start.11 = (f32[8,1024]{1,0:T(8,128)S(1)}, f32[8,1024]{1,0:T(8,128)S(1)}, u32[]{:S(2)}, u32[]{:S(2)}) collective-permute-start(f32[8,1024]{1,0:T(8,128)S(1)} %add.106), channel_id=1, source_target_pairs={{0,16},{1,17},{2,18},{3,19},{4,20},{5,21},{6,22},{7,23},{8,24},{9,... | collective-permute-start | bytes 98312 | tf_op jit(solution)/shard_map/ppermute | solution.py:696
  116.7 23.4 %collective-permute-start.10 = (f32[8,1024]{1,0:T(8,128)S(1)}, f32[8,1024]{1,0:T(8,128)S(1)}, u32[]{:S(2)}, u32[]{:S(2)}) collective-permute-start(f32[8,1024]{1,0:T(8,128)S(1)} %add.106), channel_id=1, source_target_pairs={{0,2},{1,3},{2,0},{3,1},{4,6},{5,7},{6,4},{7,5},{8,10},{9,11},{10,... | collective-permute-start | bytes 98312 | tf_op jit(solution)/shard_map/ppermute | solution.py:696
  140.2 8.2 %copy-start.5 = (f32[1,2,1024]{2,1,0:T(2,128)}, f32[1,2,1024]{2,1,0:T(2,128)S(1)}, u32[]{:S(2)}) copy-start(f32[1,2,1024]{2,1,0:T(2,128)S(1)} %fusion.8) | copy-start | bytes 24580
  148.4 21.2 %all-to-all-start.3 = ((f32[32,64,128]{2,1,0:T(8,128)}), f32[32,64,128]{2,1,0:T(8,128)S(1)}, u32[]{:S(2)}, u32[]{:S(2)}) async-start(f32[32,64,128]{2,1,0:T(8,128)} %x_inverse.1), calls=%async_computation.3 | async-start | bytes 2097152 | tf_op jit(solution)/shard_map/all_to_all | solution.py:755
  153.3 2.2 %copy-start.3 = (f32[2,32,1024]{2,1,0:T(8,128)S(1)}, f32[2,32,1024]{2,1,0:T(8,128)}, u32[]{:S(2)}) copy-start(f32[2,32,1024]{2,1,0:T(8,128)} %copy-done.2) | copy-start | bytes 786436
  155.5 5.7 %copy-start.1 = (f32[2,128,1024]{2,1,0:T(8,128)S(1)}, f32[2,128,1024]{2,1,0:T(8,128)}, u32[]{:S(2)}) copy-start(f32[2,128,1024]{2,1,0:T(8,128)} %contrast_ref) | copy-start | bytes 3145732
  155.5 5.7 %copy-start.4 = (f32[1,2,128,1024]{3,2,1,0:T(8,128)S(1)}, f32[1,2,128,1024]{3,2,1,0:T(8,128)}, u32[]{:S(2)}) copy-start(f32[1,2,128,1024]{3,2,1,0:T(8,128)} %param.18) | copy-start | bytes 3145732
  (1 other events, 1.2 us)

commit v8 on v7

--- a/solution.py
+++ b/solution.py
@@ -569,17 +569,35 @@
     return out[0] if across else out
 
 
-def second_kernel(in_ref, out_ref):
-    out_ref[...] = in_ref[0]
+def second_kernel(pair_hbm, out_hbm, held_ref, arrived, sent):
+    pieces = [(part, pl.ds(first, 512)) for part in range(2) for first in (0, 512)]
+    copies = fetch(
+        [pair_hbm.at[1, part, rows] for part, rows in pieces],
+        [held_ref.at[part, rows] for part, rows in pieces],
+        arrived,
+    )
+    leaving = []
+    for k, (part, rows) in enumerate(pieces):
+        copies[k].wait()
+        leaving.append(
+            pltpu.make_async_copy(held_ref.at[part, rows], out_hbm.at[part, rows], sent.at[k])
+        )
+        leaving[-1].start()
+    for copy in leaving:
+        copy.wait()
 
 
 def second_of(values):
     return pl.pallas_call(
         second_kernel,
-        grid=(2,),
-        in_specs=[pl.BlockSpec((1, 1, 1024, 128), lambda t: (1, t, 0, 0))],
-        out_specs=pl.BlockSpec((1, 1024, 128), lambda t: (t, 0, 0)),
+        in_specs=[spec_hbm()],
+        out_specs=spec_hbm(),
         out_shape=pltpu.HBM(values.shape[1:], f32),
+        scratch_shapes=[
+            pltpu.VMEM((2, 1024, 128), f32),
+            pltpu.SemaphoreType.DMA((4,)),
+            pltpu.SemaphoreType.DMA((4,)),
+        ],
         compiler_params=params(8),
         cost_estimate=cost(0, 2 << 20),
         name="second",

time: 172 us -> 172 us (level)
  no operation moved by 1% of the time
where the time goes in v8:
time: 172 us; the launch traced here: 171 us
  waiting for transfers between devices  75.8 us (44%)
  starting transfers between devices  44.6 us (26%)
  Pallas kernels  43.9 us (26%)
  other arithmetic  5.65 us (3%)
    ppermute x10, waiting for transfers between devices, exchange(): lax.ppermute(value, axis, [(j, j ^ stride) for j in range(size)])  29.6 us
    ppermute x3, waiting for transfers between devices, partner(): return lax.ppermute(value, 'narrow', [(j, j ^ k) for j in range(NARROW)])  28.7 us
    all_to_all x2, starting transfers between devices, local(): lax.all_to_all(lines.reshape(WIDE, 64, 128), 'wide', 0, 0, tiled=True)  14.2 us
    all_to_all x2, starting transfers between devices, local(): lax.all_to_all(lines.reshape(128, 32, 128), ('wide', 'narrow'), 0, 0, til...  13.6 us
    ppermute x10, starting transfers between devices, exchange(): lax.ppermute(value, axis, [(j, j ^ stride) for j in range(size)])  13.6 us
    pallas_call x1, Pallas kernels, middle(): pl.pallas_call(middle_kernel, in_specs=[spec_vmem()] + [spec_hbm()] * 9,...  10.8 us
    all_to_all x2, waiting for transfers between devices, local(): lax.all_to_all(lines.reshape(WIDE, 64, 128), 'wide', 0, 0, tiled=True)  10.6 us
    pallas_call x1, Pallas kernels, x_forward(): pl.pallas_call(x_forward_kernel, in_specs=[spec_vmem()] + [spec_hbm()] *...  7.09 us
  transfers between devices with their start and end apart: 17, of which 12 were waited for; matrix products, arithmetic and copies ran while one was open for 3% of the time, Pallas kernels for 15%

profile of v8, /device:TPU:0, one launch (start us, length us, event | category | flops | bytes accessed | tf_op | source)
XLA Modules:
  0.0 171.0 jit_solution(4995956900616752383)
XLA Ops:
  0.6 2.3 %columns_major.1 = f32[2048,128]{1,0:T(8,128)} custom-call(f32[2,128,1024]{2,1,0:T(8,128)} %bitcast.39), custom_call_target="tpu_custom_call" | custom-call | bytes 2097152 | tf_op jit(solution)/shard_map/columns_major/pallas_call | solution.py:199
  2.9 9.3 %all-to-all-start = ((f32[32,64,128]{2,1,0:T(8,128)}), f32[32,64,128]{2,1,0:T(8,128)S(1)}, u32[]{:S(2)}, u32[]{:S(2)}) async-start(f32[32,64,128]{2,1,0:T(8,128)} %bitcast.47), calls=%async_computation | async-start | bytes 2097152 | tf_op jit(solution)/shard_map/all_to_all | solution.py:736
  12.2 2.7 %pack_far.1 = f32[2,2,1024,128]{3,2,1,0:T(8,128)} custom-call(f32[2,2,1024,256]{3,2,1,0:T(8,128)} %bitcast.45), custom_call_target="tpu_custom_call" | custom-call | bytes 4194304 | tf_op jit(solution)/shard_map/pack_far/pallas_call | solution.py:554
  14.8 3.0 %collective-permute-start.6 = (f32[2,2,1024,128]{3,2,1,0:T(8,128)}, f32[2,2,1024,128]{3,2,1,0:T(8,128)}, u32[]{:S(2)}, u32[]{:S(2)}) collective-permute-start(f32[2,2,1024,128]{3,2,1,0:T(8,128)} %pack_far.1), channel_id=1, source_target_pairs={{0,2},{1,3},{2,0},{3,1},{4,6},{5,7},{6,4},{7,5},{8,10},{9,11},{10,... | collective-permute-start | bytes 6291464 | tf_op jit(solution)/shard_map/ppermute | solution.py:731
  21.0 5.0 %project.1 = f32[8,1024]{1,0:T(8,128)S(1)} custom-call(f32[2,128,1024]{2,1,0:T(8,128)S(1)} %bitcast.40, f32[2,32,1024]{2,1,0:T(8,128)S(1)} %get-tuple-element.57.ea_ref, f32[2,32,1024]{2,1,0:T(8,128)S(1)} %get-tuple-element.58.eb_ref, f32[2,128,1024]{2,1,0:T(8,128)S(1)} %pad_maximum_fusion.row_ref), custom_call_target="tpu_custom_call" | custom-call | flops 3221225472 | bytes 4194304 | tf_op jit(solution)/shard_map/project/pallas_call | solution.py:641
  26.1 2.6 %all-to-all-done = f32[32,64,128]{2,1,0:T(8,128)S(1)} async-done(((f32[32,64,128]{2,1,0:T(8,128)}), f32[32,64,128]{2,1,0:T(8,128)S(1)}, u32[]{:S(2)}, u32[]{:S(2)}) %all-to-all-start) | async-done | bytes 1048608 | tf_op jit(solution)/shard_map/all_to_all | solution.py:736
  28.7 7.1 %x_forward.1 = f32[4096,128]{1,0:T(8,128)} custom-call(f32[2048,128]{1,0:T(8,128)S(1)} %bitcast.44, bf16[128,192]{1,0:T(8,128)(2,1)} %constant.53.clone.t1_hbm, f32[2,64,128]{2,1,0:T(8,128)} %constant.54.clone.tw_hbm, bf16[256,768]{1,0:T(8,128)(2,1)} %constant.55.clone.t2_hbm), custom_call_target="tpu_custom_call" | custom-call | flops 1073741824 | bytes 4194304 | tf_op jit(solution)/shard_map/x_forward/pallas_call | solution.py:245
  42.8 2.2 %collective-permute-start.5 = (f32[8,1024]{1,0:T(8,128)S(1)}, f32[8,1024]{1,0:T(8,128)S(1)}, u32[]{:S(2)}, u32[]{:S(2)}) collective-permute-start(f32[8,1024]{1,0:T(8,128)S(1)} %add_add_fusion.1), channel_id=1, source_target_pairs={{0,96},{4,100},{8,104},{12,108},{16,112},{20,116},{24,120},{28,124... | collective-permute-start | bytes 98312 | tf_op jit(solution)/shard_map/ppermute | solution.py:714
  48.0 2.4 %collective-permute-done.4 = f32[8,1024]{1,0:T(8,128)S(1)} collective-permute-done((f32[8,1024]{1,0:T(8,128)S(1)}, f32[8,1024]{1,0:T(8,128)S(1)}, u32[]{:S(2)}, u32[]{:S(2)}) %collective-permute-start.4) | collective-permute-done | bytes 32800 | tf_op jit(solution)/shard_map/ppermute | solution.py:714
  50.4 2.6 %pack_near.1 = (f32[2,1024,128]{2,1,0:T(8,128)}, f32[2,1024,128]{2,1,0:T(8,128)}) custom-call(f32[2,2,1024,256]{3,2,1,0:T(8,128)} %bitcast.46), custom_call_target="tpu_custom_call" | custom-call | bytes 4194304 | tf_op jit(solution)/shard_map/pack_near/pallas_call | solution.py:554
  53.2 8.1 %all-to-all-start.1 = ((f32[128,32,128]{2,1,0:T(8,128)}), f32[128,32,128]{2,1,0:T(8,128)S(1)}, u32[]{:S(2)}, u32[]{:S(2)}) async-start(f32[128,32,128]{2,1,0:T(8,128)} %bitcast.48), calls=%async_computation.1 | async-start | bytes 4194304 | tf_op jit(solution)/shard_map/all_to_all | solution.py:749
  61.3 28.7 %collective-permute-done.6.pair_hbm.r2_hbm = f32[2,2,1024,128]{3,2,1,0:T(8,128)} collective-permute-done((f32[2,2,1024,128]{3,2,1,0:T(8,128)}, f32[2,2,1024,128]{3,2,1,0:T(8,128)}, u32[]{:S(2)}, u32[]{:S(2)}) %collective-permute-start.6) | collective-permute-done | bytes 2097184 | tf_op jit(solution)/shard_map/ppermute | solution.py:731
  92.6 2.2 %collective-permute-done.8 = f32[8,1024]{1,0:T(8,128)S(1)} collective-permute-done((f32[8,1024]{1,0:T(8,128)S(1)}, f32[8,1024]{1,0:T(8,128)S(1)}, u32[]{:S(2)}, u32[]{:S(2)}) %collective-permute-start.8) | collective-permute-done | bytes 32800 | tf_op jit(solution)/shard_map/ppermute | solution.py:714
  94.8 3.1 %all-to-all-done.1 = f32[128,32,128]{2,1,0:T(8,128)S(1)} async-done(((f32[128,32,128]{2,1,0:T(8,128)}), f32[128,32,128]{2,1,0:T(8,128)S(1)}, u32[]{:S(2)}, u32[]{:S(2)}) %all-to-all-start.1) | async-done | bytes 2097184 | tf_op jit(solution)/shard_map/all_to_all | solution.py:749
  97.9 10.8 %middle.1 = f32[128,32,128]{2,1,0:T(8,128)} custom-call(f32[4096,128]{1,0:T(8,128)S(1)} %bitcast.42, bf16[512,768]{1,0:T(8,128)(2,1)} %constant.56.clone.t3_hbm, f32[2,256,128]{2,1,0:T(8,128)} %constant.57.clone.tw_hbm, f32[2,256,128]{2,1,0:T(8,128)} %constant.58.clone.step_hbm, f32[2,1024,128]{2,1,0:T(8,128)} %get-tuple-element.34.r0_hbm, ...), custom_call_target="tpu_custom_call" | custom-call | flops 3221225472 | bytes 10485760 | tf_op jit(solution)/shard_map/middle/pallas_call | solution.py:383
  108.6 5.6 %all-to-all-start.2 = ((f32[128,32,128]{2,1,0:T(8,128)}), f32[128,32,128]{2,1,0:T(8,128)S(1)}, u32[]{:S(2)}, u32[]{:S(2)}) async-start(f32[128,32,128]{2,1,0:T(8,128)} %middle.1), calls=%async_computation.2 | async-start | bytes 4194304 | tf_op jit(solution)/shard_map/all_to_all | solution.py:761
  114.2 2.3 %collective-permute-start.12 = (f32[8,1024]{1,0:T(8,128)S(1)}, f32[8,1024]{1,0:T(8,128)S(1)}, u32[]{:S(2)}, u32[]{:S(2)}) collective-permute-start(f32[8,1024]{1,0:T(8,128)S(1)} %add.106), channel_id=1, source_target_pairs={{0,18},{1,19},{2,16},{3,17},{4,22},{5,23},{6,20},{7,21},{8,26},{9,... | collective-permute-start | bytes 98312 | tf_op jit(solution)/shard_map/ppermute | solution.py:714
  116.7 2.3 %collective-permute-start.10 = (f32[8,1024]{1,0:T(8,128)S(1)}, f32[8,1024]{1,0:T(8,128)S(1)}, u32[]{:S(2)}, u32[]{:S(2)}) collective-permute-start(f32[8,1024]{1,0:T(8,128)S(1)} %add.106), channel_id=1, source_target_pairs={{0,2},{1,3},{2,0},{3,1},{4,6},{5,7},{6,4},{7,5},{8,10},{9,11},{10,... | collective-permute-start | bytes 98312 | tf_op jit(solution)/shard_map/ppermute | solution.py:714
  119.0 21.1 %collective-permute-done.12 = f32[8,1024]{1,0:T(8,128)S(1)} collective-permute-done((f32[8,1024]{1,0:T(8,128)S(1)}, f32[8,1024]{1,0:T(8,128)S(1)}, u32[]{:S(2)}, u32[]{:S(2)}) %collective-permute-start.12) | collective-permute-done | bytes 32800 | tf_op jit(solution)/shard_map/ppermute | solution.py:714
  140.2 3.7 %all-to-all-done.2 = f32[128,32,128]{2,1,0:T(8,128)S(1)} async-done(((f32[128,32,128]{2,1,0:T(8,128)}), f32[128,32,128]{2,1,0:T(8,128)S(1)}, u32[]{:S(2)}, u32[]{:S(2)}) %all-to-all-start.2) | async-done | bytes 2097184 | tf_op jit(solution)/shard_map/all_to_all | solution.py:761
  143.9 4.4 %x_inverse.1 = f32[32,64,128]{2,1,0:T(8,128)} custom-call(f32[4096,128]{1,0:T(8,128)S(1)} %bitcast.43, bf16[256,768]{1,0:T(8,128)(2,1)} %constant.61.clone.t5_hbm, f32[2,128,128]{2,1,0:T(8,128)} %constant.62.clone.tw_hbm, bf16[128,768]{1,0:T(8,128)(2,1)} %constant.63.clone.t6_hbm), custom_call_target="tpu_custom_call" | custom-call | flops 1073741824 | bytes 4194304 | tf_op jit(solution)/shard_map/x_inverse/pallas_call | solution.py:462
  148.4 4.9 %all-to-all-start.3 = ((f32[32,64,128]{2,1,0:T(8,128)}), f32[32,64,128]{2,1,0:T(8,128)S(1)}, u32[]{:S(2)}, u32[]{:S(2)}) async-start(f32[32,64,128]{2,1,0:T(8,128)} %x_inverse.1), calls=%async_computation.3 | async-start | bytes 2097152 | tf_op jit(solution)/shard_map/all_to_all | solution.py:773
  155.5 5.6 %backproject.1 = f32[2,128,1024]{2,1,0:T(8,128)} custom-call(f32[2,128,1024]{2,1,0:T(8,128)S(1)} %pad_maximum_fusion.2.weight_ref, f32[2,32,1024]{2,1,0:T(8,128)S(1)} %get-tuple-element.57.ea_ref, f32[2,32,1024]{2,1,0:T(8,128)S(1)} %copy-done.3), custom_call_target="tpu_custom_call" | custom-call | flops 3221225472 | bytes 4194304 | tf_op jit(solution)/shard_map/backproject/pallas_call | solution.py:689
  161.6 8.0 %all-to-all-done.3 = f32[32,64,128]{2,1,0:T(8,128)S(1)} async-done(((f32[32,64,128]{2,1,0:T(8,128)}), f32[32,64,128]{2,1,0:T(8,128)S(1)}, u32[]{:S(2)}, u32[]{:S(2)}) %all-to-all-start.3) | async-done | bytes 1048608 | tf_op jit(solution)/shard_map/all_to_all | solution.py:773
  (53 shorter events, 20.0 us)
Async XLA Ops:
  2.9 25.8 %all-to-all-start = ((f32[32,64,128]{2,1,0:T(8,128)}), f32[32,64,128]{2,1,0:T(8,128)S(1)}, u32[]{:S(2)}, u32[]{:S(2)}) async-start(f32[32,64,128]{2,1,0:T(8,128)} %bitcast.47), calls=%async_computation | async-start | bytes 2097152 | tf_op jit(solution)/shard_map/all_to_all | solution.py:736
  12.2 5.7 %copy-start.7 = (f32[1024]{0:T(1024)S(1)}, f32[1024]{0:T(1024)}, u32[]{:S(2)}) copy-start(f32[1024]{0:T(1024)} %param.21) | copy-start | bytes 12292
  14.8 75.2 %collective-permute-start.6 = (f32[2,2,1024,128]{3,2,1,0:T(8,128)}, f32[2,2,1024,128]{3,2,1,0:T(8,128)}, u32[]{:S(2)}, u32[]{:S(2)}) collective-permute-start(f32[2,2,1024,128]{3,2,1,0:T(8,128)} %pack_far.1), channel_id=1, source_target_pairs={{0,2},{1,3},{2,0},{3,1},{4,6},{5,7},{6,4},{7,5},{8,10},{9,11},{10,... | collective-permute-start | bytes 6291464 | tf_op jit(solution)/shard_map/ppermute | solution.py:731
  21.0 5.1 %copy-start.2 = (f32[2,32,1024]{2,1,0:T(8,128)}, f32[2,32,1024]{2,1,0:T(8,128)S(1)}, u32[]{:S(2)}) copy-start(f32[2,32,1024]{2,1,0:T(8,128)S(1)} %get-tuple-element.58.eb_ref) | copy-start | bytes 786436
  35.8 5.2 %collective-permute-start.2 = (f32[8,1024]{1,0:T(8,128)S(1)}, f32[8,1024]{1,0:T(8,128)S(1)}, u32[]{:S(2)}, u32[]{:S(2)}) collective-permute-start(f32[8,1024]{1,0:T(8,128)S(1)} %project.1), channel_id=1, source_target_pairs={{0,12},{4,8},{8,4},{12,0},{16,28},{20,24},{24,20},{28,16},{32,44},... | collective-permute-start | bytes 98312 | tf_op jit(solution)/shard_map/ppermute | solution.py:714
  37.0 5.4 %collective-permute-start.1 = (f32[8,1024]{1,0:T(8,128)S(1)}, f32[8,1024]{1,0:T(8,128)S(1)}, u32[]{:S(2)}, u32[]{:S(2)}) collective-permute-start(f32[8,1024]{1,0:T(8,128)S(1)} %project.1), channel_id=1, source_target_pairs={{0,8},{4,12},{8,0},{12,4},{16,24},{20,28},{24,16},{28,20},{32,40},... | collective-permute-start | bytes 98312 | tf_op jit(solution)/shard_map/ppermute | solution.py:714
  38.9 3.9 %collective-permute-start = (f32[8,1024]{1,0:T(8,128)S(1)}, f32[8,1024]{1,0:T(8,128)S(1)}, u32[]{:S(2)}, u32[]{:S(2)}) collective-permute-start(f32[8,1024]{1,0:T(8,128)S(1)} %project.1), channel_id=1, source_target_pairs={{0,4},{4,0},{8,12},{12,8},{16,20},{20,16},{24,28},{28,24},{32,36},... | collective-permute-start | bytes 98312 | tf_op jit(solution)/shard_map/ppermute | solution.py:714
  42.8 5.2 %collective-permute-start.5 = (f32[8,1024]{1,0:T(8,128)S(1)}, f32[8,1024]{1,0:T(8,128)S(1)}, u32[]{:S(2)}, u32[]{:S(2)}) collective-permute-start(f32[8,1024]{1,0:T(8,128)S(1)} %add_add_fusion.1), channel_id=1, source_target_pairs={{0,96},{4,100},{8,104},{12,108},{16,112},{20,116},{24,120},{28,124... | collective-permute-start | bytes 98312 | tf_op jit(solution)/shard_map/ppermute | solution.py:714
  45.0 5.4 %collective-permute-start.4 = (f32[8,1024]{1,0:T(8,128)S(1)}, f32[8,1024]{1,0:T(8,128)S(1)}, u32[]{:S(2)}, u32[]{:S(2)}) collective-permute-start(f32[8,1024]{1,0:T(8,128)S(1)} %add_add_fusion.1), channel_id=1, source_target_pairs={{0,64},{4,68},{8,72},{12,76},{16,80},{20,84},{24,88},{28,92},{32,9... | collective-permute-start | bytes 98312 | tf_op jit(solution)/shard_map/ppermute | solution.py:714
  46.2 4.3 %collective-permute-start.3 = (f32[8,1024]{1,0:T(8,128)S(1)}, f32[8,1024]{1,0:T(8,128)S(1)}, u32[]{:S(2)}, u32[]{:S(2)}) collective-permute-start(f32[8,1024]{1,0:T(8,128)S(1)} %add_add_fusion.1), channel_id=1, source_target_pairs={{0,32},{4,36},{8,40},{12,44},{16,48},{20,52},{24,56},{28,60},{32,0... | collective-permute-start | bytes 98312 | tf_op jit(solution)/shard_map/ppermute | solution.py:714
  53.1 36.9 %collective-permute-start.7 = (f32[2,1024,128]{2,1,0:T(8,128)}, f32[2,1024,128]{2,1,0:T(8,128)}, u32[]{:S(2)}, u32[]{:S(2)}) collective-permute-start(f32[2,1024,128]{2,1,0:T(8,128)} %get-tuple-element.29), channel_id=1, source_target_pairs={{0,1},{1,0},{2,3},{3,2},{4,5},{5,4},{6,7},{7,6},{8,9},{9,8},{10,11... | collective-permute-start | bytes 3145736 | tf_op jit(solution)/shard_map/ppermute | solution.py:731
  53.2 44.7 %all-to-all-start.1 = ((f32[128,32,128]{2,1,0:T(8,128)}), f32[128,32,128]{2,1,0:T(8,128)S(1)}, u32[]{:S(2)}, u32[]{:S(2)}) async-start(f32[128,32,128]{2,1,0:T(8,128)} %bitcast.48), calls=%async_computation.1 | async-start | bytes 4194304 | tf_op jit(solution)/shard_map/all_to_all | solution.py:749
  92.0 5.9 %collective-permute-start.9 = (f32[2,1024,128]{2,1,0:T(8,128)}, f32[2,1024,128]{2,1,0:T(8,128)}, u32[]{:S(2)}, u32[]{:S(2)}) collective-permute-start(f32[2,1024,128]{2,1,0:T(8,128)} %second.1), channel_id=1, source_target_pairs={{0,1},{1,0},{2,3},{3,2},{4,5},{5,4},{6,7},{7,6},{8,9},{9,8},{10,11... | collective-permute-start | bytes 3145736 | tf_op jit(solution)/shard_map/ppermute | solution.py:731
  92.1 2.7 %collective-permute-start.8 = (f32[8,1024]{1,0:T(8,128)S(1)}, f32[8,1024]{1,0:T(8,128)S(1)}, u32[]{:S(2)}, u32[]{:S(2)}) collective-permute-start(f32[8,1024]{1,0:T(8,128)S(1)} %add_add_fusion), channel_id=1, source_target_pairs={{0,1},{1,0},{2,3},{3,2},{4,5},{5,4},{6,7},{7,6},{8,9},{9,8},{10,11... | collective-permute-start | bytes 98312 | tf_op jit(solution)/shard_map/ppermute | solution.py:714
  108.6 31.5 %copy-start.6 = (f32[1,2,1024]{2,1,0:T(2,128)S(1)}, f32[1,2,1024]{2,1,0:T(2,128)}, u32[]{:S(2)}) copy-start(f32[1,2,1024]{2,1,0:T(2,128)} %param.22) | copy-start | bytes 24580
  108.6 35.3 %all-to-all-start.2 = ((f32[128,32,128]{2,1,0:T(8,128)}), f32[128,32,128]{2,1,0:T(8,128)S(1)}, u32[]{:S(2)}, u32[]{:S(2)}) async-start(f32[128,32,128]{2,1,0:T(8,128)} %middle.1), calls=%async_computation.2 | async-start | bytes 4194304 | tf_op jit(solution)/shard_map/all_to_all | solution.py:761
  114.2 25.9 %collective-permute-start.12 = (f32[8,1024]{1,0:T(8,128)S(1)}, f32[8,1024]{1,0:T(8,128)S(1)}, u32[]{:S(2)}, u32[]{:S(2)}) collective-permute-start(f32[8,1024]{1,0:T(8,128)S(1)} %add.106), channel_id=1, source_target_pairs={{0,18},{1,19},{2,16},{3,17},{4,22},{5,23},{6,20},{7,21},{8,26},{9,... | collective-permute-start | bytes 98312 | tf_op jit(solution)/shard_map/ppermute | solution.py:714
  116.5 23.6 %collective-permute-start.11 = (f32[8,1024]{1,0:T(8,128)S(1)}, f32[8,1024]{1,0:T(8,128)S(1)}, u32[]{:S(2)}, u32[]{:S(2)}) collective-permute-start(f32[8,1024]{1,0:T(8,128)S(1)} %add.106), channel_id=1, source_target_pairs={{0,16},{1,17},{2,18},{3,19},{4,20},{5,21},{6,22},{7,23},{8,24},{9,... | collective-permute-start | bytes 98312 | tf_op jit(solution)/shard_map/ppermute | solution.py:714
  116.7 23.4 %collective-permute-start.10 = (f32[8,1024]{1,0:T(8,128)S(1)}, f32[8,1024]{1,0:T(8,128)S(1)}, u32[]{:S(2)}, u32[]{:S(2)}) collective-permute-start(f32[8,1024]{1,0:T(8,128)S(1)} %add.106), channel_id=1, source_target_pairs={{0,2},{1,3},{2,0},{3,1},{4,6},{5,7},{6,4},{7,5},{8,10},{9,11},{10,... | collective-permute-start | bytes 98312 | tf_op jit(solution)/shard_map/ppermute | solution.py:714
  140.2 8.2 %copy-start.5 = (f32[1,2,1024]{2,1,0:T(2,128)}, f32[1,2,1024]{2,1,0:T(2,128)S(1)}, u32[]{:S(2)}) copy-start(f32[1,2,1024]{2,1,0:T(2,128)S(1)} %fusion.8) | copy-start | bytes 24580
  148.4 21.2 %all-to-all-start.3 = ((f32[32,64,128]{2,1,0:T(8,128)}), f32[32,64,128]{2,1,0:T(8,128)S(1)}, u32[]{:S(2)}, u32[]{:S(2)}) async-start(f32[32,64,128]{2,1,0:T(8,128)} %x_inverse.1), calls=%async_computation.3 | async-start | bytes 2097152 | tf_op jit(solution)/shard_map/all_to_all | solution.py:773
  153.3 2.2 %copy-start.3 = (f32[2,32,1024]{2,1,0:T(8,128)S(1)}, f32[2,32,1024]{2,1,0:T(8,128)}, u32[]{:S(2)}) copy-start(f32[2,32,1024]{2,1,0:T(8,128)} %copy-done.2) | copy-start | bytes 786436
  155.5 5.7 %copy-start.1 = (f32[2,128,1024]{2,1,0:T(8,128)S(1)}, f32[2,128,1024]{2,1,0:T(8,128)}, u32[]{:S(2)}) copy-start(f32[2,128,1024]{2,1,0:T(8,128)} %contrast_ref) | copy-start | bytes 3145732
  155.5 5.7 %copy-start.4 = (f32[1,2,128,1024]{3,2,1,0:T(8,128)S(1)}, f32[1,2,128,1024]{3,2,1,0:T(8,128)}, u32[]{:S(2)}) copy-start(f32[1,2,128,1024]{3,2,1,0:T(8,128)} %param.18) | copy-start | bytes 3145732
  (1 other events, 1.2 us)
